TPU v7x, 32 devices: a whole 2x2x4 slice. The times are simulated.
32 devices in a mesh: kv: 2 (over core), seq: 16 (over z, y, x).
Axes of the slice: x: 2, y: 2, z: 4, core: 2. Of those that a mesh axis runs over, the one named last changes fastest.
Arguments:
- tokens: bfloat16 [4096, 4096], P(('seq', 'kv')), may hold values from -6 to 6
- gain: float32 [4096], replicated, may hold values from 0.25 to 1.75
- w_query: bfloat16 [4096, 4096], P(None, 'kv'), may hold values from -1 to 1
- w_key: bfloat16 [4096, 1024], P(None, 'kv'), may hold values from -4 to 4
- w_value: bfloat16 [4096, 1024], P(None, 'kv'), may hold values from -0.09375 to 0.09375
- w_out: bfloat16 [4096, 4096], P('kv'), may hold values from -0.09375 to 0.09375
- segment_ids: int32 [4096], replicated, may hold values from 0 to 4095, as said below
- page_table: int32 [32], P('seq'), may hold values from 0 to 1, as said below
Outputs:
- mixed: bfloat16 [4096, 4096], P(('seq', 'kv'))
- attn_out: bfloat16 [4096, 4096], P(('seq', 'kv'))
- page_pool: bfloat16 [32, 2, 8, 128, 128], P('seq', None, 'kv')
Inputs may be any that keep to these rules, and one draw needn't show every extreme that they name: `segment_ids`: never falls along the stream; tokens of one prompt share the position of its first token as id; every prompt has 1 to 1792 tokens; exactly two prompts have 1792 tokens, one in each half of the stream, each beginning inside a block of 256 tokens and not at its first token; every other prompt has fewer than 128 tokens; the last token of the stream is a prompt of its own. `page_table`: in each aligned block of 2 entries every value appears once.
All inputs are finite; a program needn't handle non-finite values.
Results may differ from a plain program's by a relative error of at most 0.0065.
The roundings to bfloat16 on the way count: a program that leaves them out, or rounds other values in their place, can miss the bound.
Values may be sent and summed in bfloat16 or wider, within the bound.
No kernel may reach another device: no remote copies, remote signals or barrier semaphores. Data moves between devices by JAX's collectives and lax.ppermute only.
A program may use at most 192 MiB of HBM per device.

v0:
```python
from functools import partial

import jax
import jax.numpy as jnp
from jax import lax
from jax.sharding import PartitionSpec as P

HD = 128


norm_eps = 1e-05


def shifted(value, axis, steps):
    count = lax.axis_size(axis)
    leading, last = (max(0, -steps), min(count, count - steps))
    return lax.ppermute(value, axis, [(source, source + steps) for source in range(leading, last)])


def head_attention(inputs, masks, live, sparse):
    query_head, key_blocks, value_blocks = inputs
    block_count = key_blocks.shape[0]
    key_width = key_blocks.shape[1]
    score_scale = query_head.shape[-1] ** (-0.5)

    def block_scores(distance):
        scores = (
            jnp.einsum(
                "qgd,kd->gqk", query_head, key_blocks[distance], preferred_element_type=jnp.float32
            )
            * score_scale
        )
        return jnp.where(masks[distance][None], scores, -jnp.inf)

    pieces = [block_scores(0)]
    for distance in range(1, block_count):
        pieces.append(block_scores(distance))
    scores = jnp.concatenate(pieces, axis=2)
    row_peak = jnp.max(scores, axis=2, keepdims=True)
    weights = jnp.exp(scores - row_peak).astype(jnp.bfloat16)
    row_total = jnp.sum(weights, axis=2, dtype=jnp.float32)
    all_values = value_blocks.reshape(block_count * key_width, value_blocks.shape[-1])
    weighted = jnp.einsum("gqk,kd->qgd", weights, all_values, preferred_element_type=jnp.float32)
    return (weighted / row_total.T[:, :, None]).astype(jnp.bfloat16)


def shards(tokens, gain, w_query, w_key, w_value, w_out, segment_ids, page_table):
    tok_rows = tokens.shape[0]
    block_rows = tok_rows * lax.axis_size("kv")
    reach = min(8, lax.axis_size("seq") // 2 - 1)
    kv_local = w_key.shape[1] // HD
    q_local = w_query.shape[1] // HD
    group_size = q_local // kv_local
    wide_rows = tokens.astype(jnp.float32)
    normed = (
        wide_rows
        * lax.rsqrt(jnp.mean(wide_rows * wide_rows, axis=1, keepdims=True) + norm_eps)
        * gain
    ).astype(jnp.bfloat16)
    piece = lax.all_gather(normed, "kv", axis=0, tiled=True)
    projected = jnp.concatenate(
        [
            jnp.dot(piece, w_query, preferred_element_type=jnp.float32),
            jnp.dot(piece, w_key, preferred_element_type=jnp.float32),
            jnp.dot(piece, w_value, preferred_element_type=jnp.float32),
        ],
        axis=1,
    ).astype(jnp.bfloat16)
    query_cols = q_local * HD
    key_cols = kv_local * HD
    query = projected[:, :query_cols].reshape(block_rows, kv_local, group_size, HD)
    key_rows = projected[:, query_cols : query_cols + key_cols].reshape(block_rows, kv_local, HD)
    value_rows = projected[:, query_cols + key_cols :].reshape(block_rows, kv_local, HD)
    pair_rows = jnp.stack([key_rows, value_rows], axis=0)
    page_rows = page_table.shape[0]
    page_len = block_rows // page_rows
    pages = pair_rows.reshape(2, page_rows, page_len, kv_local, HD).transpose(1, 0, 3, 2, 4)
    page_pool = jnp.zeros_like(pages).at[page_table].set(pages)
    received = [pair_rows]
    carried = pair_rows
    for distance in range(1, reach + 1):
        carried = shifted(carried, "seq", 1)
        received.append(carried)
    stacked_pairs = jnp.stack(received, axis=1)
    seq_index = lax.axis_index("seq")
    query_segs = lax.dynamic_slice_in_dim(segment_ids, seq_index * block_rows, block_rows)
    lower = jnp.arange(block_rows)[None, :] <= jnp.arange(block_rows)[:, None]
    mask_list = []
    live_list = []
    for distance in range(reach + 1):
        source = jnp.maximum(seq_index - distance, 0)
        valid = seq_index - distance >= 0
        key_segs = lax.dynamic_slice_in_dim(segment_ids, source * block_rows, block_rows)
        same = (key_segs[None, :] == query_segs[:, None]) & valid
        if distance == 0:
            same = same & lower
            live_list.append(jnp.array(True))
        else:
            live_list.append(valid & (key_segs[block_rows - 1] == query_segs[0]))
        mask_list.append(same)
    masks = jnp.stack(mask_list)
    live = jnp.stack(live_list)
    heads_out = lax.map(
        partial(head_attention, masks=masks, live=live, sparse=False),
        (
            query.transpose(1, 0, 2, 3),
            stacked_pairs[0].transpose(2, 0, 1, 3),
            stacked_pairs[1].transpose(2, 0, 1, 3),
        ),
    )
    attention = heads_out.transpose(1, 0, 2, 3).reshape(block_rows, q_local * HD)
    summed = lax.psum(jnp.dot(attention, w_out, preferred_element_type=jnp.float32), "kv")
    branch = lax.dynamic_slice_in_dim(summed, lax.axis_index("kv") * tok_rows, tok_rows, 0)
    attn_out = branch.astype(jnp.bfloat16)
    mixed = (wide_rows + branch).astype(jnp.bfloat16)
    return (mixed, attn_out, page_pool)


def solution(mesh):
    in_specs = (
        P(("seq", "kv"), None),
        P(),
        P(None, "kv"),
        P(None, "kv"),
        P(None, "kv"),
        P("kv", None),
        P(),
        P("seq"),
    )
    out_specs = (P(("seq", "kv"), None), P(("seq", "kv"), None), P("seq", None, "kv", None, None))
    return jax.shard_map(shards, mesh=mesh, in_specs=in_specs, out_specs=out_specs, check_vma=False)
```

profile of v0, /device:TPU:0, one launch (start us, length us, event | category | flops | bytes accessed | tf_op | source)
XLA Modules:
  0.0 304.2 jit_solution(18229778342534872131)
XLA Ops:
  8.7 2.5 fusion.64
  11.3 13.4 %all-gather.2.cloned.1.call-done = bf16[256,4096]{1,0:T(8,128)(2,1)} async-done(((bf16[128,4096]{1,0:T(8,128)(2,1)}), bf16[256,4096]{1,0:T(8,128)(2,1)}) %all-gather.2.cloned.1.call-update) | async-done | bytes 2097168 | tf_op jit(solution)/shard_map/all_gather | solution.py:60
  24.7 4.1 %convolution_convert_fusion.2 = bf16[256,512]{1,0:T(8,128)(2,1)S(1)} fusion(bf16[256,4096]{1,0:T(8,128)(2,1)} %all-gather.2.cloned.1.call-done, bf16[4096,512]{1,0:T(8,128)(2,1)} %param.13), kind=kOutput, calls=%fused_computation.104 | convolution fusion | flops 1073872896 | bytes 6553600 | tf_op jit(solution)/shard_map/dot_general | solution.py:64
  28.9 4.1 %convolution_convert_fusion.1 = bf16[256,512]{1,0:T(8,128)(2,1)S(1)} fusion(bf16[256,4096]{1,0:T(8,128)(2,1)} %all-gather.2.cloned.1.call-done, bf16[4096,512]{1,0:T(8,128)(2,1)} %param.14), kind=kOutput, calls=%fused_computation.103 | convolution fusion | flops 1073872896 | bytes 6553600 | tf_op jit(solution)/shard_map/dot_general | solution.py:65
  33.1 3.7 %collective-permute-start = (bf16[2,256,4,128]{3,1,2,0:T(8,128)(2,1)S(1)}, bf16[2,256,4,128]{3,1,2,0:T(8,128)(2,1)S(1)}, u32[]{:S(2)}, u32[]{:S(2)}) collective-permute-start(bf16[2,256,4,128]{3,1,2,0:T(8,128)(2,1)S(1)} %copy_dynamic-update-slice_fusion), channel_id=1, source_target_pairs={{0,1},{1,2},{2,3},{3,4},{4,5},{5,6},{6,7},{7,8},{8,9},{9,10},{10,1... | collective-permute-start | bytes 1572872 | tf_op jit(solution)/shard_map/ppermute | solution.py:17
  36.8 11.6 %collective-permute-done = bf16[2,256,4,128]{3,1,2,0:T(8,128)(2,1)S(1)} collective-permute-done((bf16[2,256,4,128]{3,1,2,0:T(8,128)(2,1)S(1)}, bf16[2,256,4,128]{3,1,2,0:T(8,128)(2,1)S(1)}, u32[]{:S(2)}, u32[]{:S(2)}) %collective-permute-start) | collective-permute-done | bytes 524320 | tf_op jit(solution)/shard_map/ppermute | solution.py:17
  48.4 4.4 %collective-permute-start.1 = (bf16[2,256,4,128]{3,1,2,0:T(8,128)(2,1)S(1)}, bf16[2,256,4,128]{3,1,2,0:T(8,128)(2,1)S(1)}, u32[]{:S(2)}, u32[]{:S(2)}) collective-permute-start(bf16[2,256,4,128]{3,1,2,0:T(8,128)(2,1)S(1)} %collective-permute-done), channel_id=1, source_target_pairs={{0,1},{1,2},{2,3},{3,4},{4,5},{5,6},{6,7},{7,8},{8,9},{9,10},{10,1... | collective-permute-start | bytes 1572872 | tf_op jit(solution)/shard_map/ppermute | solution.py:17
  52.8 10.8 %collective-permute-done.1 = bf16[2,256,4,128]{3,1,2,0:T(8,128)(2,1)S(1)} collective-permute-done((bf16[2,256,4,128]{3,1,2,0:T(8,128)(2,1)S(1)}, bf16[2,256,4,128]{3,1,2,0:T(8,128)(2,1)S(1)}, u32[]{:S(2)}, u32[]{:S(2)}) %collective-permute-start.1) | collective-permute-done | bytes 524320 | tf_op jit(solution)/shard_map/ppermute | solution.py:17
  63.6 4.4 %collective-permute-start.2 = (bf16[2,256,4,128]{3,1,2,0:T(8,128)(2,1)S(1)}, bf16[2,256,4,128]{3,1,2,0:T(8,128)(2,1)S(1)}, u32[]{:S(2)}, u32[]{:S(2)}) collective-permute-start(bf16[2,256,4,128]{3,1,2,0:T(8,128)(2,1)S(1)} %collective-permute-done.1), channel_id=1, source_target_pairs={{0,1},{1,2},{2,3},{3,4},{4,5},{5,6},{6,7},{7,8},{8,9},{9,10},{10,1... | collective-permute-start | bytes 1572872 | tf_op jit(solution)/shard_map/ppermute | solution.py:17
  68.0 9.9 %collective-permute-done.2 = bf16[2,256,4,128]{3,1,2,0:T(8,128)(2,1)S(1)} collective-permute-done((bf16[2,256,4,128]{3,1,2,0:T(8,128)(2,1)S(1)}, bf16[2,256,4,128]{3,1,2,0:T(8,128)(2,1)S(1)}, u32[]{:S(2)}, u32[]{:S(2)}) %collective-permute-start.2) | collective-permute-done | bytes 524320 | tf_op jit(solution)/shard_map/ppermute | solution.py:17
  77.9 6.0 %collective-permute-start.3 = (bf16[2,256,4,128]{3,1,2,0:T(8,128)(2,1)S(1)}, bf16[2,256,4,128]{3,1,2,0:T(8,128)(2,1)}, u32[]{:S(2)}, u32[]{:S(2)}) collective-permute-start(bf16[2,256,4,128]{3,1,2,0:T(8,128)(2,1)S(1)} %collective-permute-done.2), channel_id=1, source_target_pairs={{0,1},{1,2},{2,3},{3,4},{4,5},{5,6},{6,7},{7,8},{8,9},{9,10},{10,1... | collective-permute-start | bytes 1572872 | tf_op jit(solution)/shard_map/ppermute | solution.py:17
  84.0 8.1 %collective-permute-done.3 = bf16[2,256,4,128]{3,1,2,0:T(8,128)(2,1)} collective-permute-done((bf16[2,256,4,128]{3,1,2,0:T(8,128)(2,1)S(1)}, bf16[2,256,4,128]{3,1,2,0:T(8,128)(2,1)}, u32[]{:S(2)}, u32[]{:S(2)}) %collective-permute-start.3) | collective-permute-done | bytes 524320 | tf_op jit(solution)/shard_map/ppermute | solution.py:17
  92.0 6.1 %collective-permute-start.4 = (bf16[2,256,4,128]{3,1,2,0:T(8,128)(2,1)}, bf16[2,256,4,128]{3,1,2,0:T(8,128)(2,1)}, u32[]{:S(2)}, u32[]{:S(2)}) collective-permute-start(bf16[2,256,4,128]{3,1,2,0:T(8,128)(2,1)} %collective-permute-done.3), channel_id=1, source_target_pairs={{0,1},{1,2},{2,3},{3,4},{4,5},{5,6},{6,7},{7,8},{8,9},{9,10},{10,1... | collective-permute-start | bytes 1572872 | tf_op jit(solution)/shard_map/ppermute | solution.py:17
  98.1 10.9 %convolution_convert_fusion = bf16[256,2048]{1,0:T(8,128)(2,1)S(1)} fusion(bf16[256,4096]{1,0:T(8,128)(2,1)} %all-gather.2.cloned.1.call-done, bf16[4096,2048]{1,0:T(8,128)(2,1)} %param.12), kind=kOutput, calls=%fused_computation.95 | convolution fusion | flops 4295491584 | bytes 19922944 | tf_op jit(solution)/shard_map/dot_general | solution.py:63
  111.1 4.6 %collective-permute-start.5 = (bf16[2,256,4,128]{3,1,2,0:T(8,128)(2,1)}, bf16[2,256,4,128]{3,1,2,0:T(8,128)(2,1)S(1)}, u32[]{:S(2)}, u32[]{:S(2)}) collective-permute-start(bf16[2,256,4,128]{3,1,2,0:T(8,128)(2,1)} %collective-permute-done.4), channel_id=1, source_target_pairs={{0,1},{1,2},{2,3},{3,4},{4,5},{5,6},{6,7},{7,8},{8,9},{9,10},{10,1... | collective-permute-start | bytes 1572872 | tf_op jit(solution)/shard_map/ppermute | solution.py:17
  117.1 6.8 %collective-permute-done.5 = bf16[2,256,4,128]{3,1,2,0:T(8,128)(2,1)S(1)} collective-permute-done((bf16[2,256,4,128]{3,1,2,0:T(8,128)(2,1)}, bf16[2,256,4,128]{3,1,2,0:T(8,128)(2,1)S(1)}, u32[]{:S(2)}, u32[]{:S(2)}) %collective-permute-start.5) | collective-permute-done | bytes 524320 | tf_op jit(solution)/shard_map/ppermute | solution.py:17
  123.8 4.5 %collective-permute-start.6 = (bf16[2,256,4,128]{3,1,2,0:T(8,128)(2,1)S(1)}, bf16[2,256,4,128]{3,1,2,0:T(8,128)(2,1)S(1)}, u32[]{:S(2)}, u32[]{:S(2)}) collective-permute-start(bf16[2,256,4,128]{3,1,2,0:T(8,128)(2,1)S(1)} %collective-permute-done.5), channel_id=1, source_target_pairs={{0,1},{1,2},{2,3},{3,4},{4,5},{5,6},{6,7},{7,8},{8,9},{9,10},{10,1... | collective-permute-start | bytes 1572872 | tf_op jit(solution)/shard_map/ppermute | solution.py:17
  130.6 4.3 %collective-permute-done.6 = bf16[2,256,4,128]{3,1,2,0:T(8,128)(2,1)S(1)} collective-permute-done((bf16[2,256,4,128]{3,1,2,0:T(8,128)(2,1)S(1)}, bf16[2,256,4,128]{3,1,2,0:T(8,128)(2,1)S(1)}, u32[]{:S(2)}, u32[]{:S(2)}) %collective-permute-start.6) | collective-permute-done | bytes 524320 | tf_op jit(solution)/shard_map/ppermute | solution.py:17
  136.8 107.5 %while.12 = (s32[]{:T(128)}, bf16[4,256,4,128]{1,3,2,0:T(8,128)(2,1)}, bf16[4,8,256,128]{3,2,1,0:T(8,128)(2,1)S(1)}, bf16[4,8,256,128]{3,2,1,0:T(8,128)(2,1)}, b...) while((s32[]{:T(128)}, ...), condition=%wide.region_11.12_spmd.clone.clone, body=%wide.region_1.11_spmd.clone.clone.sunk | while | flops 1094055936 | bytes 64329636 | solution.py:103
  137.4 2.3 fusion.96
  139.6 2.3 fusion.97
  141.9 2.3 fusion.98
  146.5 2.3 fusion.100
  153.3 2.3 fusion.103
  155.6 4.6 %convert_reduce_fusion.2 = f32[4,256]{1,0:T(4,128)S(1)} fusion(f32[4,256,2048]{1,2,0:T(8,128)} %get-tuple-element.484, f32[4,256]{1,0:T(4,128)S(1)} %maximum_maximum_fusion.2), kind=kLoop, calls=%fused_computation.9.clone.1 | loop fusion | flops 8387584 | bytes 8396800 | tf_op jit(solution)/shard_map/while/body/eval_jaxpr/reduce_sum | solution.py:41
  161.4 2.3 fusion.104
  164.2 2.3 fusion.96
  168.8 2.3 fusion.98
  173.3 2.3 fusion.100
  180.2 2.3 fusion.103
  182.5 4.6 %convert_reduce_fusion.2 = f32[4,256]{1,0:T(4,128)S(1)} fusion(f32[4,256,2048]{1,2,0:T(8,128)} %get-tuple-element.484, f32[4,256]{1,0:T(4,128)S(1)} %maximum_maximum_fusion.2), kind=kLoop, calls=%fused_computation.9.clone.1 | loop fusion | flops 8387584 | bytes 8396800 | tf_op jit(solution)/shard_map/while/body/eval_jaxpr/reduce_sum | solution.py:41
  188.2 2.3 fusion.104
  191.1 2.3 fusion.96
  195.6 2.3 fusion.98
  200.2 2.3 fusion.100
  207.0 2.3 fusion.103
  209.3 4.6 %convert_reduce_fusion.2 = f32[4,256]{1,0:T(4,128)S(1)} fusion(f32[4,256,2048]{1,2,0:T(8,128)} %get-tuple-element.484, f32[4,256]{1,0:T(4,128)S(1)} %maximum_maximum_fusion.2), kind=kLoop, calls=%fused_computation.9.clone.1 | loop fusion | flops 8387584 | bytes 8396800 | tf_op jit(solution)/shard_map/while/body/eval_jaxpr/reduce_sum | solution.py:41
  215.1 2.3 fusion.104
  217.9 2.3 fusion.96
  222.5 2.3 fusion.98
  227.1 2.3 fusion.100
  233.9 2.3 fusion.103
  236.2 4.6 %convert_reduce_fusion.2 = f32[4,256]{1,0:T(4,128)S(1)} fusion(f32[4,256,2048]{1,2,0:T(8,128)} %get-tuple-element.484, f32[4,256]{1,0:T(4,128)S(1)} %maximum_maximum_fusion.2), kind=kLoop, calls=%fused_computation.9.clone.1 | loop fusion | flops 8387584 | bytes 8396800 | tf_op jit(solution)/shard_map/while/body/eval_jaxpr/reduce_sum | solution.py:41
  242.0 2.3 fusion.104
  244.3 12.7 %fusion.75 = f32[256,4096]{1,0:T(8,128)} fusion(bf16[256,2048]{0,1:T(8,128)(2,1)} %bitcast.253, bf16[2048,4096]{1,0:T(8,128)(2,1)} %param.15), kind=kOutput, calls=%fused_computation.128 | convolution fusion | flops 4294967296 | bytes 22020096 | tf_op jit(solution)/shard_map/dot_general | solution.py:112
  258.7 33.2 %all-reduce.2.cloned.1.call-done = f32[256,4096]{1,0:T(8,128)} async-done(((f32[256,4096]{1,0:T(8,128)}), f32[256,4096]{1,0:T(8,128)}) %all-reduce.2.cloned.1.call-update) | async-done | bytes 4194320 | tf_op jit(solution)/shard_map/psum | solution.py:112
  291.9 2.7 dynamic-slice_convert_fusion
  294.6 2.8 fusion.65
  (85 shorter events, 51.9 us)
Async XLA Ops:
  7.2 17.6 %all-gather.2.cloned.1.call-start = ((), (), s32[]{:S(2)}) async-start(), calls=%async_computation | async-start | bytes 3145728 | tf_op jit(solution)/shard_map/all_gather | solution.py:60
  11.3 280.6 %all-reduce.2.cloned.1.call-start = ((), (), s32[]{:S(2)}) async-start(), calls=%async_computation.1 | async-start | bytes 8388608 | tf_op jit(solution)/shard_map/psum | solution.py:112
  28.9 54.9 %copy-start.8 = (s32[4096]{0:T(1024)S(1)}, s32[4096]{0:T(1024)}, u32[]{:S(2)}) copy-start(s32[4096]{0:T(1024)} %param.16) | copy-start | bytes 49156
  33.1 15.3 %collective-permute-start = (bf16[2,256,4,128]{3,1,2,0:T(8,128)(2,1)S(1)}, bf16[2,256,4,128]{3,1,2,0:T(8,128)(2,1)S(1)}, u32[]{:S(2)}, u32[]{:S(2)}) collective-permute-start(bf16[2,256,4,128]{3,1,2,0:T(8,128)(2,1)S(1)} %copy_dynamic-update-slice_fusion), channel_id=1, source_target_pairs={{0,1},{1,2},{2,3},{3,4},{4,5},{5,6},{6,7},{7,8},{8,9},{9,10},{10,1... | collective-permute-start | bytes 1572872 | tf_op jit(solution)/shard_map/ppermute | solution.py:17
  48.4 43.6 %copy-start.3 = (bf16[2,256,4,128]{3,1,2,0:T(8,128)(2,1)}, bf16[2,256,4,128]{3,1,2,0:T(8,128)(2,1)S(1)}, u32[]{:S(2)}) copy-start(bf16[2,256,4,128]{3,1,2,0:T(8,128)(2,1)S(1)} %collective-permute-done) | copy-start | bytes 1572868
  48.4 15.2 %collective-permute-start.1 = (bf16[2,256,4,128]{3,1,2,0:T(8,128)(2,1)S(1)}, bf16[2,256,4,128]{3,1,2,0:T(8,128)(2,1)S(1)}, u32[]{:S(2)}, u32[]{:S(2)}) collective-permute-start(bf16[2,256,4,128]{3,1,2,0:T(8,128)(2,1)S(1)} %collective-permute-done), channel_id=1, source_target_pairs={{0,1},{1,2},{2,3},{3,4},{4,5},{5,6},{6,7},{7,8},{8,9},{9,10},{10,1... | collective-permute-start | bytes 1572872 | tf_op jit(solution)/shard_map/ppermute | solution.py:17
  63.6 28.4 %copy-start.4 = (bf16[2,256,4,128]{3,1,2,0:T(8,128)(2,1)}, bf16[2,256,4,128]{3,1,2,0:T(8,128)(2,1)S(1)}, u32[]{:S(2)}) copy-start(bf16[2,256,4,128]{3,1,2,0:T(8,128)(2,1)S(1)} %collective-permute-done.1) | copy-start | bytes 1572868
  63.6 14.3 %collective-permute-start.2 = (bf16[2,256,4,128]{3,1,2,0:T(8,128)(2,1)S(1)}, bf16[2,256,4,128]{3,1,2,0:T(8,128)(2,1)S(1)}, u32[]{:S(2)}, u32[]{:S(2)}) collective-permute-start(bf16[2,256,4,128]{3,1,2,0:T(8,128)(2,1)S(1)} %collective-permute-done.1), channel_id=1, source_target_pairs={{0,1},{1,2},{2,3},{3,4},{4,5},{5,6},{6,7},{7,8},{8,9},{9,10},{10,1... | collective-permute-start | bytes 1572872 | tf_op jit(solution)/shard_map/ppermute | solution.py:17
  77.9 20.2 %copy-start.6 = (bf16[2,256,4,128]{3,1,2,0:T(8,128)(2,1)}, bf16[2,256,4,128]{3,1,2,0:T(8,128)(2,1)S(1)}, u32[]{:S(2)}) copy-start(bf16[2,256,4,128]{3,1,2,0:T(8,128)(2,1)S(1)} %collective-permute-done.2) | copy-start | bytes 1572868
  77.9 14.1 %collective-permute-start.3 = (bf16[2,256,4,128]{3,1,2,0:T(8,128)(2,1)S(1)}, bf16[2,256,4,128]{3,1,2,0:T(8,128)(2,1)}, u32[]{:S(2)}, u32[]{:S(2)}) collective-permute-start(bf16[2,256,4,128]{3,1,2,0:T(8,128)(2,1)S(1)} %collective-permute-done.2), channel_id=1, source_target_pairs={{0,1},{1,2},{2,3},{3,4},{4,5},{5,6},{6,7},{7,8},{8,9},{9,10},{10,1... | collective-permute-start | bytes 1572872 | tf_op jit(solution)/shard_map/ppermute | solution.py:17
  92.0 19.1 %collective-permute-start.4 = (bf16[2,256,4,128]{3,1,2,0:T(8,128)(2,1)}, bf16[2,256,4,128]{3,1,2,0:T(8,128)(2,1)}, u32[]{:S(2)}, u32[]{:S(2)}) collective-permute-start(bf16[2,256,4,128]{3,1,2,0:T(8,128)(2,1)} %collective-permute-done.3), channel_id=1, source_target_pairs={{0,1},{1,2},{2,3},{3,4},{4,5},{5,6},{6,7},{7,8},{8,9},{9,10},{10,1... | collective-permute-start | bytes 1572872 | tf_op jit(solution)/shard_map/ppermute | solution.py:17
  109.8 7.1 %copy-start.5 = (bf16[2,256,4,128]{3,1,2,0:T(8,128)(2,1)S(1)}, bf16[2,256,4,128]{3,1,2,0:T(8,128)(2,1)}, u32[]{:S(2)}) copy-start(bf16[2,256,4,128]{3,1,2,0:T(8,128)(2,1)} %copy-done.4) | copy-start | bytes 1572868
  109.8 7.1 %copy-start.7 = (bf16[2,256,4,128]{3,1,2,0:T(8,128)(2,1)S(1)}, bf16[2,256,4,128]{3,1,2,0:T(8,128)(2,1)}, u32[]{:S(2)}) copy-start(bf16[2,256,4,128]{3,1,2,0:T(8,128)(2,1)} %copy-done.6) | copy-start | bytes 1572868
  111.1 12.7 %collective-permute-start.5 = (bf16[2,256,4,128]{3,1,2,0:T(8,128)(2,1)}, bf16[2,256,4,128]{3,1,2,0:T(8,128)(2,1)S(1)}, u32[]{:S(2)}, u32[]{:S(2)}) collective-permute-start(bf16[2,256,4,128]{3,1,2,0:T(8,128)(2,1)} %collective-permute-done.4), channel_id=1, source_target_pairs={{0,1},{1,2},{2,3},{3,4},{4,5},{5,6},{6,7},{7,8},{8,9},{9,10},{10,1... | collective-permute-start | bytes 1572872 | tf_op jit(solution)/shard_map/ppermute | solution.py:17
  123.8 11.1 %collective-permute-start.6 = (bf16[2,256,4,128]{3,1,2,0:T(8,128)(2,1)S(1)}, bf16[2,256,4,128]{3,1,2,0:T(8,128)(2,1)S(1)}, u32[]{:S(2)}, u32[]{:S(2)}) collective-permute-start(bf16[2,256,4,128]{3,1,2,0:T(8,128)(2,1)S(1)} %collective-permute-done.5), channel_id=1, source_target_pairs={{0,1},{1,2},{2,3},{3,4},{4,5},{5,6},{6,7},{7,8},{8,9},{9,10},{10,1... | collective-permute-start | bytes 1572872 | tf_op jit(solution)/shard_map/ppermute | solution.py:17
  155.6 5.8 %copy-start = (f32[4,256,2048]{1,2,0:T(8,128)S(1)}, f32[4,256,2048]{1,2,0:T(8,128)}, u32[]{:S(2)}) copy-start(f32[4,256,2048]{1,2,0:T(8,128)} %get-tuple-element.484) | copy-start | bytes 25165828 | tf_op jit(solution)/shard_map/while
  182.5 5.8 %copy-start = (f32[4,256,2048]{1,2,0:T(8,128)S(1)}, f32[4,256,2048]{1,2,0:T(8,128)}, u32[]{:S(2)}) copy-start(f32[4,256,2048]{1,2,0:T(8,128)} %get-tuple-element.484) | copy-start | bytes 25165828 | tf_op jit(solution)/shard_map/while
  209.3 5.8 %copy-start = (f32[4,256,2048]{1,2,0:T(8,128)S(1)}, f32[4,256,2048]{1,2,0:T(8,128)}, u32[]{:S(2)}) copy-start(f32[4,256,2048]{1,2,0:T(8,128)} %get-tuple-element.484) | copy-start | bytes 25165828 | tf_op jit(solution)/shard_map/while
  236.2 5.8 %copy-start = (f32[4,256,2048]{1,2,0:T(8,128)S(1)}, f32[4,256,2048]{1,2,0:T(8,128)}, u32[]{:S(2)}) copy-start(f32[4,256,2048]{1,2,0:T(8,128)} %get-tuple-element.484) | copy-start | bytes 25165828 | tf_op jit(solution)/shard_map/while
  256.9 0.7 copy-start.9
  256.9 37.7 %copy-start.1 = (bf16[128,4096]{1,0:T(8,128)(2,1)S(1)}, bf16[128,4096]{1,0:T(8,128)(2,1)}, u32[]{:S(2)}) copy-start(bf16[128,4096]{1,0:T(8,128)(2,1)} %param.10) | copy-start | bytes 3145732
  258.7 38.7 %copy-start.2 = (bf16[2,2,4,128,128]{4,3,2,1,0:T(8,128)(2,1)}, bf16[2,2,4,128,128]{4,3,2,1,0:T(8,128)(2,1)S(1)}, u32[]{:S(2)}) copy-start(bf16[2,2,4,128,128]{4,3,2,1,0:T(8,128)(2,1)S(1)} %scatter_fusion) | copy-start | bytes 1572868
Sparse Core Ops, SparseCore 0:
  11.4 13.2 all-gather.1
  257.1 34.8 all-reduce.1
where the time goes:
time: 305 us; the launch traced here: 304 us
  matrix products  114 us (37%)
  waiting for transfers between devices  98 us (32%)
  starting transfers between devices  33.7 us (11%)
  other arithmetic  27.7 us (9%)
  local copies, waits for them, and re-layouts  16.6 us (5%)
  between operations  14.3 us (5%)
    dot_general x32, matrix products, block_scores(): jnp.einsum('qgd,kd->gqk', query_head, key_blocks[distance], preferred_ele...  73 us
    ppermute x7, waiting for transfers between devices, shifted(): lax.ppermute(value, axis, [(source, source + steps) for source in range(l...  51.4 us
    ppermute x7, starting transfers between devices, shifted(): lax.ppermute(value, axis, [(source, source + steps) for source in range(l...  33.6 us
    psum x1, waiting for transfers between devices, shards(): lax.psum(jnp.dot(attention, w_out, preferred_element_type=jnp.float32), '...  33.2 us
    reduce_sum x4, other arithmetic, head_attention(): row_total = jnp.sum(weights, axis=2, dtype=jnp.float32)  18.5 us
    all_gather x1, waiting for transfers between devices, shards(): piece = lax.all_gather(normed, 'kv', axis=0, tiled=True)  13.4 us
    dot_general x1, matrix products, shards(): jnp.dot(attention, w_out, preferred_element_type=jnp.float32)  12.7 us
    dot_general x1, matrix products, shards(): jnp.dot(piece, w_query, preferred_element_type=jnp.float32)  10.9 us
  transfers between devices with their start and end apart: 9, of which 8 were waited for; matrix products, arithmetic and copies ran while one was open for 6% of the time, Pallas kernels for 0%

commit v1 on v0

v1 whole, which is shorter than its diff:
```python
import functools
import math

import jax
import jax.numpy as jnp
from jax import lax
from jax.experimental import pallas as pl
from jax.experimental.pallas import tpu as pltpu
from jax.sharding import PartitionSpec as P

HD = 128
NORM_EPS = 1e-05
MASKED = -1e30
MIB = 1024 * 1024


def project_kv_kernel(own_ref, other_ref, gain_ref, wk_ref, wv_ref, normed_ref, kv_ref):
    half = own_ref.shape[0]

    @pl.when(pl.program_id(0) == 0)
    def _():
        for index, ref in enumerate((own_ref, other_ref)):
            for start in range(0, half, 32):
                wide = ref[start : start + 32, :].astype(jnp.float32)
                mean = jnp.mean(wide * wide, axis=1, keepdims=True)
                normed = wide * lax.rsqrt(mean + NORM_EPS) * gain_ref[...]
                first = index * half + start
                normed_ref[first : first + 32, :] = normed.astype(jnp.bfloat16)

    weights = jnp.concatenate([wk_ref[...], wv_ref[...]], axis=1)
    pair = jnp.dot(normed_ref[...], weights, preferred_element_type=jnp.float32)
    pair = pair.astype(jnp.bfloat16)
    kv_ref[0, 0] = pair[:, :HD]
    kv_ref[0, 1] = pair[:, HD:]


def project_kv(own, other, gain, w_key, w_value):
    half, width = own.shape
    heads = w_key.shape[1] // HD
    rows = 2 * half
    whole = lambda h: (0, 0)
    return pl.pallas_call(
        project_kv_kernel,
        grid=(heads,),
        in_specs=[
            pl.BlockSpec((half, width), whole),
            pl.BlockSpec((half, width), whole),
            pl.BlockSpec((1, width), whole),
            pl.BlockSpec((width, HD), lambda h: (0, h)),
            pl.BlockSpec((width, HD), lambda h: (0, h)),
        ],
        out_specs=[
            pl.BlockSpec((rows, width), whole),
            pl.BlockSpec((1, 2, rows, HD), lambda h: (h, 0, 0, 0)),
        ],
        out_shape=[
            jax.ShapeDtypeStruct((rows, width), jnp.bfloat16),
            jax.ShapeDtypeStruct((heads, 2, rows, HD), jnp.bfloat16),
        ],
        compiler_params=pltpu.CompilerParams(vmem_limit_bytes=32 * MIB),
        cost_estimate=pl.CostEstimate(
            flops=4 * rows * width * heads * HD,
            bytes_accessed=4 * width * heads * HD + 4 * rows * width,
            transcendentals=0,
        ),
        name="project_kv",
    )(own, other, gain.reshape(1, width), w_key, w_value)


def matmul_kernel(x_ref, w_ref, out_ref):
    out_ref[...] = jnp.dot(x_ref[...], w_ref[...], preferred_element_type=jnp.float32).astype(
        out_ref.dtype
    )


def project_query(normed, w_query, tile=256):
    rows, width = normed.shape
    cols = w_query.shape[1]
    return pl.pallas_call(
        matmul_kernel,
        grid=(cols // tile,),
        in_specs=[
            pl.BlockSpec((rows, width), lambda n: (0, 0)),
            pl.BlockSpec((width, tile), lambda n: (0, n)),
        ],
        out_specs=pl.BlockSpec((rows, tile), lambda n: (0, n)),
        out_shape=jax.ShapeDtypeStruct((rows, cols), jnp.bfloat16),
        compiler_params=pltpu.CompilerParams(vmem_limit_bytes=32 * MIB),
        cost_estimate=pl.CostEstimate(
            flops=2 * rows * width * cols,
            bytes_accessed=2 * (width * cols + rows * (width + cols)),
            transcendentals=0,
        ),
        name="project_query",
    )(normed, w_query)


def attention_kernel(block_count, first, last, group, *refs):
    seg_q, pos_q, seg_k, pos_k, q_ref = refs[:5]
    blocks = refs[5 : 5 + block_count]
    refs = refs[5 + block_count :]
    if not first:
        acc_in, stat_in = refs[:2]
        refs = refs[2:]
    if last:
        out_ref, bias_ref = refs
    else:
        acc_out, stat_out, bias_ref = refs

    @pl.when(pl.program_id(0) == 0)
    def _():
        seen = (seg_q[...] == seg_k[...]) & (pos_k[...] <= pos_q[...])
        bias_ref[...] = jnp.where(seen, 0.0, MASKED)

    rows = q_ref.shape[0]
    factor = math.log2(math.e) / math.sqrt(HD)
    keys = jnp.concatenate([block[0, 0] for block in blocks], axis=0)
    values = jnp.concatenate([block[0, 1] for block in blocks], axis=0)
    values = jnp.concatenate([values, jnp.ones_like(values)], axis=1)
    for head in range(group):
        cols = slice(head * HD, (head + 1) * HD)
        scores = lax.dot_general(
            q_ref[:, cols], keys, (((1,), (1,)), ((), ())), preferred_element_type=jnp.float32
        )
        scores = scores + bias_ref[...]
        peak = jnp.max(scores, axis=1, keepdims=True)
        if not first:
            old = stat_in[0, :, head : head + 1]
            peak = jnp.maximum(peak, old)
        weights = jnp.exp2(scores * factor - peak * factor).astype(jnp.bfloat16)
        total = jnp.dot(weights, values, preferred_element_type=jnp.float32)
        acc = total[:, :HD]
        mass = total[:, HD:]
        if not first:
            keep = jnp.exp2((old - peak) * factor)
            acc = acc + acc_in[:, cols] * keep
            mass = mass + stat_in[0, :, group + head : group + head + 1] * keep
        if last:
            out_ref[:, cols] = (acc / mass).astype(jnp.bfloat16)
        else:
            acc_out[:, cols] = acc
            stat_out[0, :, head : head + 1] = peak
            stat_out[0, :, group + head : group + head + 1] = mass[:, :1]


def attend(query, blocks, sources, segs, positions, state, last):
    rows, q_cols = query.shape
    heads = blocks[0].shape[0]
    width = q_cols // heads
    group = width // HD
    seg_of, pos_of = segs, positions
    seg_k = jnp.concatenate([seg_of(s) for s in sources])[None, :]
    pos_k = jnp.concatenate([pos_of(s) for s in sources])[None, :]
    seg_q = seg_of(None)[:, None]
    pos_q = pos_of(None)[:, None]
    keys = len(blocks) * rows
    first = state is None
    whole = lambda h: (0, 0)
    acc_spec = pl.BlockSpec((rows, width), lambda h: (0, h))
    stat_spec = pl.BlockSpec((1, rows, HD), lambda h: (h, 0, 0))
    in_specs = [
        pl.BlockSpec((rows, 1), whole),
        pl.BlockSpec((rows, 1), whole),
        pl.BlockSpec((1, keys), whole),
        pl.BlockSpec((1, keys), whole),
        pl.BlockSpec((rows, width), lambda h: (0, h)),
    ]
    in_specs += [pl.BlockSpec((1, 2, rows, HD), lambda h: (h, 0, 0, 0))] * len(blocks)
    if not first:
        in_specs += [acc_spec, stat_spec]
    if last:
        out_specs = acc_spec
        out_shape = jax.ShapeDtypeStruct((rows, q_cols), jnp.bfloat16)
    else:
        out_specs = [acc_spec, stat_spec]
        out_shape = [
            jax.ShapeDtypeStruct((rows, q_cols), jnp.float32),
            jax.ShapeDtypeStruct((heads, rows, HD), jnp.float32),
        ]
    return pl.pallas_call(
        functools.partial(attention_kernel, len(blocks), first, last, group),
        grid=(heads,),
        in_specs=in_specs,
        out_specs=out_specs,
        out_shape=out_shape,
        scratch_shapes=[pltpu.VMEM((rows, keys), jnp.float32)],
        compiler_params=pltpu.CompilerParams(vmem_limit_bytes=48 * MIB),
        cost_estimate=pl.CostEstimate(
            flops=6 * rows * keys * q_cols,
            bytes_accessed=8 * rows * q_cols,
            transcendentals=rows * keys * heads * group,
        ),
        name="attend",
    )(seg_q, pos_q, seg_k, pos_k, query, *blocks, *(state or ()))


def project_out_kernel(x_ref, w_ref, own_ref, other_ref):
    half = own_ref.shape[0]
    part = jnp.dot(x_ref[...], w_ref[...], preferred_element_type=jnp.float32)
    own_ref[...] = part[:half]
    other_ref[...] = part[half:].astype(other_ref.dtype)


def project_out(attention, w_out, piece, pieces, tile=256):
    rows, depth = attention.shape
    cols = w_out.shape[1] // pieces
    tiles = cols // tile
    half = rows // 2
    return pl.pallas_call(
        project_out_kernel,
        grid=(tiles,),
        in_specs=[
            pl.BlockSpec((rows, depth), lambda n: (0, 0)),
            pl.BlockSpec((depth, tile), lambda n: (0, piece * tiles + n)),
        ],
        out_specs=[
            pl.BlockSpec((half, tile), lambda n: (0, n)),
            pl.BlockSpec((half, tile), lambda n: (0, n)),
        ],
        out_shape=[
            jax.ShapeDtypeStruct((half, cols), jnp.float32),
            jax.ShapeDtypeStruct((half, cols), jnp.bfloat16),
        ],
        compiler_params=pltpu.CompilerParams(vmem_limit_bytes=32 * MIB),
        cost_estimate=pl.CostEstimate(
            flops=2 * rows * depth * cols,
            bytes_accessed=2 * depth * cols + 6 * half * cols,
            transcendentals=0,
        ),
        name="project_out",
    )(attention, w_out)


def swap_cores(value):
    return lax.ppermute(value, "kv", [(0, 1), (1, 0)])


def gather_in_half(block, index, count):
    half = count // 2

    def exchange(value, bit):
        return lax.ppermute(value, "seq", [(i, i ^ bit) for i in range(count)])

    pairs = [(i, i ^ 4) for i in range(count)]
    for start in range(half, count, half):
        before = start - 1
        pairs = [p for p in pairs if p[0] != before and p[1] != start] + [(before, start)]
    from_x = exchange(block, 1)
    from_y = exchange(block, 2)
    from_z = lax.ppermute(block, "seq", pairs)
    seam = (index % half == 0) & (index > 0)
    z_source = jnp.where(seam, index - 1, index ^ 4)
    near = [(from_x, index ^ 1), (from_y, index ^ 2), (from_z, z_source)]
    from_xy = exchange(from_y, 1)
    from_yz = exchange(from_z, 2)
    from_xz = exchange(from_x, 4)
    far = [(from_xy, index ^ 3), (from_yz, index ^ 6), (from_xz, index ^ 5)]
    flat = lambda value: value.reshape((-1,) + value.shape[2:])
    last = jnp.concatenate(
        [
            exchange(flat(from_yz)[:3], 1),
            exchange(flat(from_xz)[3:6], 2),
            exchange(flat(from_xy)[6:], 4),
        ]
    ).reshape(block.shape)
    return [near, far, [(last, index ^ 7)]]


def gather_by_distance(block, index, count, reach):
    received = []
    for distance in range(1, reach + 1):
        moved = lax.ppermute(block, "seq", [(i, i + distance) for i in range(count - distance)])
        received.append((moved, index - distance))
    return [received[start : start + 3] for start in range(0, reach, 3)]


def shards(tokens, gain, w_query, w_key, w_value, w_out, segment_ids, page_table):
    half_rows = tokens.shape[0]
    block_rows = 2 * half_rows
    count = lax.axis_size("seq")
    index = lax.axis_index("seq")
    core = lax.axis_index("kv")
    reach = min(8, count // 2 - 1)

    other_tokens = swap_cores(tokens)
    normed, own_block = project_kv(tokens, other_tokens, gain, w_key, w_value)

    if count == 2 * (reach + 1) and count // 2 == 8:
        groups = gather_in_half(own_block, index, count)
    else:
        groups = gather_by_distance(own_block, index, count, reach)

    query = project_query(normed, w_query)

    offsets = jnp.arange(half_rows, dtype=jnp.int32)
    local = jnp.concatenate([core * half_rows + offsets, (1 - core) * half_rows + offsets])

    def positions(source):
        return (index if source is None else source) * block_rows + local

    def segs(source):
        start = jnp.maximum(index if source is None else source, 0) * block_rows
        first = lax.dynamic_slice_in_dim(segment_ids, start + core * half_rows, half_rows)
        second = lax.dynamic_slice_in_dim(segment_ids, start + (1 - core) * half_rows, half_rows)
        found = jnp.concatenate([first, second])
        return found if source is None else jnp.where(source >= 0, found, -1)

    groups[0] = [(own_block, index)] + groups[0]
    state = None
    for number, group in enumerate(groups):
        blocks = [block for block, _ in group]
        sources = [source for _, source in group]
        state = attend(
            query, blocks, sources, segs, positions, state, number == len(groups) - 1
        )
    attention = state

    heads = own_block.shape[0]
    pages = own_block.reshape(heads, 2, 2, half_rows, HD).transpose(2, 1, 0, 3, 4)
    own_slot = lax.dynamic_index_in_dim(page_table, core, keepdims=False)
    page_pool = jnp.where(own_slot == 0, pages, pages[::-1])

    pieces = 2
    wide = tokens.astype(jnp.float32)
    cols = w_out.shape[1] // pieces
    attn_out, mixed = [], []
    parts = [project_out(attention, w_out, piece, pieces) for piece in range(pieces)]
    for piece, (mine, theirs) in enumerate(parts):
        branch = mine + swap_cores(theirs).astype(jnp.float32)
        attn_out.append(branch.astype(jnp.bfloat16))
        mixed.append(
            (wide[:, piece * cols : (piece + 1) * cols] + branch).astype(jnp.bfloat16)
        )
    return (jnp.concatenate(mixed, axis=1), jnp.concatenate(attn_out, axis=1), page_pool)


def solution(mesh):
    in_specs = (
        P(("seq", "kv"), None),
        P(),
        P(None, "kv"),
        P(None, "kv"),
        P(None, "kv"),
        P("kv", None),
        P(),
        P("seq"),
    )
    out_specs = (P(("seq", "kv"), None), P(("seq", "kv"), None), P("seq", None, "kv", None, None))
    return jax.shard_map(shards, mesh=mesh, in_specs=in_specs, out_specs=out_specs, check_vma=False)
```

time: 305 us -> 117 us (0.38)
  the two profiles are of different devices: /device:TPU:0 before, /device:TPU:17 now
where the time goes in v1:
time: 117 us
  Pallas kernels  51.5 us (44%)
  waiting for transfers between devices  23 us (20%)
  local copies, waits for them, and re-layouts  21.2 us (18%)
  starting transfers between devices  12.8 us (11%)
  other arithmetic  6.62 us (6%)
  between operations  1.65 us (1%)
    pallas_call x3, Pallas kernels, attend(): pl.pallas_call(functools.partial(attention_kernel, len(blocks), first, la...  26.7 us
    unnamed x20, local copies, waits for them, and re-layouts  19.2 us
    ppermute x8, waiting for transfers between devices, exchange(): return lax.ppermute(value, 'seq', [(i, i ^ bit) for i in range(count)])  11.2 us
    pallas_call x2, Pallas kernels, project_out(): pl.pallas_call(project_out_kernel, grid=(tiles,), in_specs=[pl.BlockSpec(...  11.1 us
    ppermute x1, waiting for transfers between devices, gather_in_half(): from_z = lax.ppermute(block, 'seq', pairs)  10.9 us
    pallas_call x1, Pallas kernels, project_query(): pl.pallas_call(matmul_kernel, grid=(cols // tile,), in_specs=[pl.BlockSpe...  8.27 us
    ppermute x8, starting transfers between devices, exchange(): return lax.ppermute(value, 'seq', [(i, i ^ bit) for i in range(count)])  6.64 us
    pallas_call x1, Pallas kernels, project_kv(): pl.pallas_call(project_kv_kernel, grid=(heads,), in_specs=[pl.BlockSpec((...  5.46 us
  transfers between devices with their start and end apart: 12, of which 3 were waited for; matrix products, arithmetic and copies ran while one was open for 4% of the time, Pallas kernels for 24%

profile of v1, /device:TPU:17, one launch (start us, length us, event | category | flops | bytes accessed | tf_op | source)
XLA Modules:
  0.0 116.8 jit_solution(3829626802241304782)
XLA Ops:
  0.6 0.7 collective-permute-start
  1.4 1.1 fusion.8
  2.5 0.1 copy.23.refs_0_
  2.7 0.1 copy.20
  3.0 0.9 collective-permute-done.other_ref
  3.9 2.2 %copy-done.2 = bf16[4096,512]{1,0:T(8,128)(2,1)S(1)} copy-done((bf16[4096,512]{1,0:T(8,128)(2,1)S(1)}, bf16[4096,512]{1,0:T(8,128)(2,1)}, u32[]{:S(2)}) %copy-start.2) | copy-done | bytes 4194328
  6.1 2.2 %copy-done.3 = bf16[4096,512]{1,0:T(8,128)(2,1)S(1)} copy-done((bf16[4096,512]{1,0:T(8,128)(2,1)S(1)}, bf16[4096,512]{1,0:T(8,128)(2,1)}, u32[]{:S(2)}) %copy-start.3) | copy-done | bytes 4194328
  8.2 1.2 %copy-done.4 = bf16[128,4096]{1,0:T(8,128)(2,1)S(1)} copy-done((bf16[128,4096]{1,0:T(8,128)(2,1)S(1)}, bf16[128,4096]{1,0:T(8,128)(2,1)}, u32[]{:S(2)}) %copy-start.4) | copy-done | bytes 1048600
  9.5 0.7 copy-done.6
  10.2 5.5 %project_kv.1 = (bf16[256,4096]{1,0:T(8,128)(2,1)S(1)}, bf16[4,2,256,128]{3,2,1,0:T(8,128)(2,1)S(1)}) custom-call(bf16[128,4096]{1,0:T(8,128)(2,1)S(1)} %copy-done.4, bf16[128,4096]{1,0:T(8,128)(2,1)S(1)} %collective-permute-done.other_ref, f32[1,4096]{1,0:T(1,128)S(1)} %bitcast.30, bf16[4096,512]{1,0:T(8,128)(2,1)S(1)} %copy-done.2, ...), custom_call_target="tpu_custom_call" | custom-call | flops 2147483648 | bytes 12582912 | tf_op jit(solution)/shard_map/project_kv/pallas_call | solution.py:42
  15.7 3.4 %collective-permute-start.1 = (bf16[4,2,256,128]{3,2,1,0:T(8,128)(2,1)S(1)}, bf16[4,2,256,128]{3,2,1,0:T(8,128)(2,1)S(1)}, u32[]{:S(2)}, u32[]{:S(2)}) collective-permute-start(bf16[4,2,256,128]{3,2,1,0:T(8,128)(2,1)S(1)} %get-tuple-element.14.refs_5_), channel_id=1, source_target_pairs={{0,4},{1,5},{2,6},{3,7},{4,0},{5,1},{6,2},{8,12},{9,13},{10,14},{1... | collective-permute-start | bytes 1572872 | tf_op jit(solution)/shard_map/ppermute | solution.py:250
  19.1 1.3 %collective-permute-start.4 = (bf16[4,2,256,128]{3,2,1,0:T(8,128)(2,1)S(1)}, bf16[4,2,256,128]{3,2,1,0:T(8,128)(2,1)S(1)}, u32[]{:S(2)}, u32[]{:S(2)}) collective-permute-start(bf16[4,2,256,128]{3,2,1,0:T(8,128)(2,1)S(1)} %get-tuple-element.14.refs_5_), channel_id=1, source_target_pairs={{0,1},{1,0},{2,3},{3,2},{4,5},{5,4},{6,7},{7,6},{8,9},{9,8},{10,11... | collective-permute-start | bytes 1572872 | tf_op jit(solution)/shard_map/ppermute | solution.py:242
  20.3 1.2 %collective-permute-start.7 = (bf16[4,2,256,128]{3,2,1,0:T(8,128)(2,1)S(1)}, bf16[4,2,256,128]{3,2,1,0:T(8,128)(2,1)S(1)}, u32[]{:S(2)}, u32[]{:S(2)}) collective-permute-start(bf16[4,2,256,128]{3,2,1,0:T(8,128)(2,1)S(1)} %get-tuple-element.14.refs_5_), channel_id=1, source_target_pairs={{0,2},{1,3},{2,0},{3,1},{4,6},{5,7},{6,4},{7,5},{8,10},{9,11},{10,... | collective-permute-start | bytes 1572872 | tf_op jit(solution)/shard_map/ppermute | solution.py:242
  21.6 10.9 %collective-permute-done.1.refs_8_ = bf16[4,2,256,128]{3,2,1,0:T(8,128)(2,1)S(1)} collective-permute-done((bf16[4,2,256,128]{3,2,1,0:T(8,128)(2,1)S(1)}, bf16[4,2,256,128]{3,2,1,0:T(8,128)(2,1)S(1)}, u32[]{:S(2)}, u32[]{:S(2)}) %collective-permute-start.1) | collective-permute-done | bytes 524320 | tf_op jit(solution)/shard_map/ppermute | solution.py:250
  32.5 0.0 collective-permute-start.2
  32.5 0.0 collective-permute-done.4.refs_6_
  32.5 0.7 collective-permute-start.5
  33.2 11.2 %collective-permute-done.7.refs_7_ = bf16[4,2,256,128]{3,2,1,0:T(8,128)(2,1)S(1)} collective-permute-done((bf16[4,2,256,128]{3,2,1,0:T(8,128)(2,1)S(1)}, bf16[4,2,256,128]{3,2,1,0:T(8,128)(2,1)S(1)}, u32[]{:S(2)}, u32[]{:S(2)}) %collective-permute-start.7) | collective-permute-done | bytes 524320 | tf_op jit(solution)/shard_map/ppermute | solution.py:242
  44.4 0.0 collective-permute-start.8
  44.4 5.8 %copy-done.1 = bf16[4096,2048]{1,0:T(8,128)(2,1)S(1)} copy-done((bf16[4096,2048]{1,0:T(8,128)(2,1)S(1)}, bf16[4096,2048]{1,0:T(8,128)(2,1)}, u32[]{:S(2)}) %copy-start.1) | copy-done | bytes 16777240
  50.2 8.3 %project_query.1.refs_4_ = bf16[256,2048]{1,0:T(8,128)(2,1)S(1)} custom-call(bf16[256,4096]{1,0:T(8,128)(2,1)S(1)} %get-tuple-element.13.x_ref, bf16[4096,2048]{1,0:T(8,128)(2,1)S(1)} %copy-done.1), custom_call_target="tpu_custom_call" | custom-call | flops 4294967296 | bytes 19922944 | tf_op jit(solution)/shard_map/project_query/pallas_call | solution.py:79
  58.5 8.3 %attend.3 = (f32[256,2048]{1,0:T(8,128)S(1)}, f32[4,256,128]{2,1,0:T(8,128)S(1)}) custom-call(s32[256,1]{1,0:T(8,128)S(1)} %copy.23.refs_0_, s32[256,1]{1,0:T(8,128)S(1)} %broadcast_add_fusion.refs_1_, s32[1,1024]{1,0:T(1,128)S(1)} %bitcast.31, s32[1,1024]{1,0:T(1,128)S(1)} %bitcast.32, bf16[256,2048]{1,0:T(8,128)(2,1)S(1)} %project_query.1.refs_4_, ...), custom_call_target="tpu_custom_call" | custom-call | flops 3221225472 | bytes 4194304 | tf_op jit(solution)/shard_map/attend/pallas_call | solution.py:180
  66.8 1.3 %copy-done.7 = f32[256,2048]{1,0:T(8,128)} copy-done((f32[256,2048]{1,0:T(8,128)}, f32[256,2048]{1,0:T(8,128)S(1)}, u32[]{:S(2)}) %copy-start.7) | copy-done | bytes 2097176
  68.1 0.0 collective-permute-done.2.refs_6_
  68.2 1.5 %collective-permute-start.3 = (bf16[3,256,128]{2,1,0:T(8,128)(2,1)S(1)}, bf16[3,256,128]{2,1,0:T(8,128)(2,1)S(1)}, u32[]{:S(2)}, u32[]{:S(2)}) collective-permute-start(bf16[3,256,128]{2,1,0:T(8,128)(2,1)S(1)} %slice.25), channel_id=1, source_target_pairs={{0,1},{1,0},{2,3},{3,2},{4,5},{5,4},{6,7},{7,6},{8,9},{9,8},{10,11... | collective-permute-start | bytes 589832 | tf_op jit(solution)/shard_map/ppermute | solution.py:242
  69.7 0.0 collective-permute-done.5.refs_7_
  69.7 0.4 collective-permute-start.6
  70.1 0.0 collective-permute-done.8.refs_5_
  70.1 1.5 %collective-permute-start.9 = (bf16[2,256,128]{2,1,0:T(8,128)(2,1)S(1)}, bf16[2,256,128]{2,1,0:T(8,128)(2,1)S(1)}, u32[]{:S(2)}, u32[]{:S(2)}) collective-permute-start(bf16[2,256,128]{2,1,0:T(8,128)(2,1)S(1)} %slice_bitcast_fusion), channel_id=1, source_target_pairs={{0,4},{1,5},{2,6},{3,7},{4,0},{5,1},{6,2},{7,3},{8,12},{9,13},{10,... | collective-permute-start | bytes 393224 | tf_op jit(solution)/shard_map/ppermute | solution.py:242
  71.6 11.5 %attend.4 = (f32[256,2048]{1,0:T(8,128)S(1)}, f32[4,256,128]{2,1,0:T(8,128)S(1)}) custom-call(s32[256,1]{1,0:T(8,128)S(1)} %copy.23.refs_0_, s32[256,1]{1,0:T(8,128)S(1)} %broadcast_add_fusion.refs_1_, s32[1,768]{1,0:T(1,128)S(1)} %broadcast_in_dim.38.refs_2_, s32[1,768]{1,0:T(1,128)S(1)} %broadcast_in_dim.39.refs_3_, ...), custom_call_target="tpu_custom_call" | custom-call | flops 2415919104 | bytes 4194304 | tf_op jit(solution)/shard_map/attend/pallas_call | solution.py:180
  83.1 0.0 collective-permute-done.9
  83.1 0.1 pad_maximum_fusion.2
  83.2 6.9 %attend.5.x_ref = bf16[256,2048]{1,0:T(8,128)(2,1)S(1)} custom-call(s32[256,1]{1,0:T(8,128)S(1)} %copy.23.refs_0_, s32[256,1]{1,0:T(8,128)S(1)} %broadcast_add_fusion.refs_1_, s32[1,256]{1,0:T(1,128)S(1)} %broadcast_select_fusion.refs_2_, s32[1,256]{1,0:T(1,128)S(1)} %add_add_fusion.refs_3_, bf16[256,2048]{1,0:T(8,128)(2,1)S(1)} %project_query.1.refs_4_, ...), custom_call_target="tpu_custom_call" | custom-call | flops 805306368 | bytes 4194304 | tf_op jit(solution)/shard_map/attend/pallas_call | solution.py:180
  90.1 0.0 copy-start
  90.1 5.8 %copy-done = bf16[2048,4096]{1,0:T(8,128)(2,1)S(1)} copy-done((bf16[2048,4096]{1,0:T(8,128)(2,1)S(1)}, bf16[2048,4096]{1,0:T(8,128)(2,1)}, u32[]{:S(2)}) %copy-start) | copy-done | bytes 16777240
  95.9 5.9 %project_out.2 = (f32[128,2048]{1,0:T(8,128)S(1)}, bf16[128,2048]{1,0:T(8,128)(2,1)}) custom-call(bf16[256,2048]{1,0:T(8,128)(2,1)S(1)} %attend.5.x_ref, bf16[2048,4096]{1,0:T(8,128)(2,1)S(1)} %copy-done), custom_call_target="tpu_custom_call" | custom-call | flops 2147483648 | bytes 9961472 | tf_op jit(solution)/shard_map/project_out/pallas_call | solution.py:209
  101.8 5.2 %project_out.3 = (f32[128,2048]{1,0:T(8,128)S(1)}, bf16[128,2048]{1,0:T(8,128)(2,1)S(1)}) custom-call(bf16[256,2048]{1,0:T(8,128)(2,1)S(1)} %attend.5.x_ref, bf16[2048,4096]{1,0:T(8,128)(2,1)S(1)} %copy-done), custom_call_target="tpu_custom_call" | custom-call | flops 2147483648 | bytes 9961472 | tf_op jit(solution)/shard_map/project_out/pallas_call | solution.py:209
  107.0 0.0 copy-start.9
  107.0 1.9 %collective-permute-start.10 = (bf16[128,2048]{1,0:T(8,128)(2,1)}, bf16[128,2048]{1,0:T(8,128)(2,1)}, u32[]{:S(2)}, u32[]{:S(2)}) collective-permute-start(bf16[128,2048]{1,0:T(8,128)(2,1)} %get-tuple-element.20), channel_id=1, source_target_pairs={{0,16},{16,0},{1,17},{17,1},{2,18},{18,2},{3,19},{19,3},{4,20},{20... | collective-permute-start | bytes 1572872 | tf_op jit(solution)/shard_map/ppermute | solution.py:235
  108.9 0.1 collective-permute-start.11
  109.0 1.6 %convert_element_type.21 = f32[128,4096]{1,0:T(8,128)} convert(bf16[128,4096]{1,0:T(8,128)(2,1)S(1)} %copy-done.5) | non-fusion elementwise | flops 524288 | bytes 3145728 | tf_op jit(solution)/shard_map/convert_element_type | solution.py:324
  110.6 0.6 dynamic_slice.74
  111.9 0.9 reverse_select_fusion
  112.8 0.0 collective-permute-done.10
  112.8 0.0 collective-permute-done.11
  112.8 1.8 %fusion.1 = (bf16[128,2048]{1,0:T(8,128)(2,1)S(1)}, bf16[128,2048]{1,0:T(8,128)(2,1)S(1)}, bf16[128,2048]{1,0:T(8,128)(2,1)S(1)}, bf16[128,2048]{1,0:T(8,128)(2,1)S(1)}) fusion(f32[128,4096]{1,0:T(8,128)S(1)} %copy-done.8, f32[128,2048]{1,0:T(8,128)S(1)} %get-tuple-element.19, bf16[128,2048]{1,0:T(8,128)(2,1)} %collective-permute-done.10, ...), kind=kLoop, calls=%fused_computation.3 | loop fusion | flops 2621440 | bytes 7340032 | tf_op jit(solution)/shard_map/convert_element_type | solution.py:332
  114.7 1.1 pad_maximum_fusion.1
  115.7 1.1 pad_maximum_fusion
  (36 shorter events, 0.3 us)
Async XLA Ops:
  0.6 3.2 %collective-permute-start = (bf16[128,4096]{1,0:T(8,128)(2,1)}, bf16[128,4096]{1,0:T(8,128)(2,1)S(1)}, u32[]{:S(2)}, u32[]{:S(2)}) collective-permute-start(bf16[128,4096]{1,0:T(8,128)(2,1)} %own_ref.1), channel_id=1, source_target_pairs={{0,16},{16,0},{1,17},{17,1},{2,18},{18,2},{3,19},{19,3},{4,20},{20... | collective-permute-start | bytes 3145736 | tf_op jit(solution)/shard_map/ppermute | solution.py:235
  3.9 2.2 %copy-start.2 = (bf16[4096,512]{1,0:T(8,128)(2,1)S(1)}, bf16[4096,512]{1,0:T(8,128)(2,1)}, u32[]{:S(2)}) copy-start(bf16[4096,512]{1,0:T(8,128)(2,1)} %wk_ref.1) | copy-start | bytes 12582916
  6.1 2.2 %copy-start.3 = (bf16[4096,512]{1,0:T(8,128)(2,1)S(1)}, bf16[4096,512]{1,0:T(8,128)(2,1)}, u32[]{:S(2)}) copy-start(bf16[4096,512]{1,0:T(8,128)(2,1)} %wv_ref.1) | copy-start | bytes 12582916
  8.2 1.2 %copy-start.4 = (bf16[128,4096]{1,0:T(8,128)(2,1)S(1)}, bf16[128,4096]{1,0:T(8,128)(2,1)}, u32[]{:S(2)}) copy-start(bf16[128,4096]{1,0:T(8,128)(2,1)} %own_ref.1) | copy-start | bytes 3145732
  9.5 0.7 copy-start.6
  15.7 16.9 %collective-permute-start.1 = (bf16[4,2,256,128]{3,2,1,0:T(8,128)(2,1)S(1)}, bf16[4,2,256,128]{3,2,1,0:T(8,128)(2,1)S(1)}, u32[]{:S(2)}, u32[]{:S(2)}) collective-permute-start(bf16[4,2,256,128]{3,2,1,0:T(8,128)(2,1)S(1)} %get-tuple-element.14.refs_5_), channel_id=1, source_target_pairs={{0,4},{1,5},{2,6},{3,7},{4,0},{5,1},{6,2},{8,12},{9,13},{10,14},{1... | collective-permute-start | bytes 1572872 | tf_op jit(solution)/shard_map/ppermute | solution.py:250
  19.1 13.5 %collective-permute-start.4 = (bf16[4,2,256,128]{3,2,1,0:T(8,128)(2,1)S(1)}, bf16[4,2,256,128]{3,2,1,0:T(8,128)(2,1)S(1)}, u32[]{:S(2)}, u32[]{:S(2)}) collective-permute-start(bf16[4,2,256,128]{3,2,1,0:T(8,128)(2,1)S(1)} %get-tuple-element.14.refs_5_), channel_id=1, source_target_pairs={{0,1},{1,0},{2,3},{3,2},{4,5},{5,4},{6,7},{7,6},{8,9},{9,8},{10,11... | collective-permute-start | bytes 1572872 | tf_op jit(solution)/shard_map/ppermute | solution.py:242
  20.3 24.1 %collective-permute-start.7 = (bf16[4,2,256,128]{3,2,1,0:T(8,128)(2,1)S(1)}, bf16[4,2,256,128]{3,2,1,0:T(8,128)(2,1)S(1)}, u32[]{:S(2)}, u32[]{:S(2)}) collective-permute-start(bf16[4,2,256,128]{3,2,1,0:T(8,128)(2,1)S(1)} %get-tuple-element.14.refs_5_), channel_id=1, source_target_pairs={{0,2},{1,3},{2,0},{3,1},{4,6},{5,7},{6,4},{7,5},{8,10},{9,11},{10,... | collective-permute-start | bytes 1572872 | tf_op jit(solution)/shard_map/ppermute | solution.py:242
  32.5 35.6 %collective-permute-start.2 = (bf16[4,2,256,128]{3,2,1,0:T(8,128)(2,1)S(1)}, bf16[4,2,256,128]{3,2,1,0:T(8,128)(2,1)S(1)}, u32[]{:S(2)}, u32[]{:S(2)}) collective-permute-start(bf16[4,2,256,128]{3,2,1,0:T(8,128)(2,1)S(1)} %collective-permute-done.1.refs_8_), channel_id=1, source_target_pairs={{0,2},{1,3},{2,0},{3,1},{4,6},{5,7},{6,4},{7,5},{8,10},{9,11},{10,... | collective-permute-start | bytes 1572872 | tf_op jit(solution)/shard_map/ppermute | solution.py:242
  32.5 37.2 %collective-permute-start.5 = (bf16[4,2,256,128]{3,2,1,0:T(8,128)(2,1)S(1)}, bf16[4,2,256,128]{3,2,1,0:T(8,128)(2,1)S(1)}, u32[]{:S(2)}, u32[]{:S(2)}) collective-permute-start(bf16[4,2,256,128]{3,2,1,0:T(8,128)(2,1)S(1)} %collective-permute-done.4.refs_6_), channel_id=1, source_target_pairs={{0,4},{1,5},{2,6},{3,7},{4,0},{5,1},{6,2},{7,3},{8,12},{9,13},{10,... | collective-permute-start | bytes 1572872 | tf_op jit(solution)/shard_map/ppermute | solution.py:242
  44.4 25.7 %collective-permute-start.8 = (bf16[4,2,256,128]{3,2,1,0:T(8,128)(2,1)S(1)}, bf16[4,2,256,128]{3,2,1,0:T(8,128)(2,1)S(1)}, u32[]{:S(2)}, u32[]{:S(2)}) collective-permute-start(bf16[4,2,256,128]{3,2,1,0:T(8,128)(2,1)S(1)} %collective-permute-done.7.refs_7_), channel_id=1, source_target_pairs={{0,1},{1,0},{2,3},{3,2},{4,5},{5,4},{6,7},{7,6},{8,9},{9,8},{10,11... | collective-permute-start | bytes 1572872 | tf_op jit(solution)/shard_map/ppermute | solution.py:242
  44.4 5.8 %copy-start.1 = (bf16[4096,2048]{1,0:T(8,128)(2,1)S(1)}, bf16[4096,2048]{1,0:T(8,128)(2,1)}, u32[]{:S(2)}) copy-start(bf16[4096,2048]{1,0:T(8,128)(2,1)} %w_ref.3) | copy-start | bytes 50331652
  66.8 1.3 %copy-start.7 = (f32[256,2048]{1,0:T(8,128)}, f32[256,2048]{1,0:T(8,128)S(1)}, u32[]{:S(2)}) copy-start(f32[256,2048]{1,0:T(8,128)S(1)} %get-tuple-element.15.refs_8_) | copy-start | bytes 6291460
  68.2 15.0 %collective-permute-start.3 = (bf16[3,256,128]{2,1,0:T(8,128)(2,1)S(1)}, bf16[3,256,128]{2,1,0:T(8,128)(2,1)S(1)}, u32[]{:S(2)}, u32[]{:S(2)}) collective-permute-start(bf16[3,256,128]{2,1,0:T(8,128)(2,1)S(1)} %slice.25), channel_id=1, source_target_pairs={{0,1},{1,0},{2,3},{3,2},{4,5},{5,4},{6,7},{7,6},{8,9},{9,8},{10,11... | collective-permute-start | bytes 589832 | tf_op jit(solution)/shard_map/ppermute | solution.py:242
  69.7 13.4 %collective-permute-start.6 = (bf16[3,256,128]{2,1,0:T(8,128)(2,1)S(1)}, bf16[3,256,128]{2,1,0:T(8,128)(2,1)S(1)}, u32[]{:S(2)}, u32[]{:S(2)}) collective-permute-start(bf16[3,256,128]{2,1,0:T(8,128)(2,1)S(1)} %slice.26), channel_id=1, source_target_pairs={{0,2},{1,3},{2,0},{3,1},{4,6},{5,7},{6,4},{7,5},{8,10},{9,11},{10,... | collective-permute-start | bytes 589832 | tf_op jit(solution)/shard_map/ppermute | solution.py:242
  70.1 13.0 %collective-permute-start.9 = (bf16[2,256,128]{2,1,0:T(8,128)(2,1)S(1)}, bf16[2,256,128]{2,1,0:T(8,128)(2,1)S(1)}, u32[]{:S(2)}, u32[]{:S(2)}) collective-permute-start(bf16[2,256,128]{2,1,0:T(8,128)(2,1)S(1)} %slice_bitcast_fusion), channel_id=1, source_target_pairs={{0,4},{1,5},{2,6},{3,7},{4,0},{5,1},{6,2},{7,3},{8,12},{9,13},{10,... | collective-permute-start | bytes 393224 | tf_op jit(solution)/shard_map/ppermute | solution.py:242
  90.1 5.8 %copy-start = (bf16[2048,4096]{1,0:T(8,128)(2,1)S(1)}, bf16[2048,4096]{1,0:T(8,128)(2,1)}, u32[]{:S(2)}) copy-start(bf16[2048,4096]{1,0:T(8,128)(2,1)} %w_ref.5) | copy-start | bytes 50331652
  101.8 7.2 %copy-start.5 = (bf16[128,4096]{1,0:T(8,128)(2,1)S(1)}, bf16[128,4096]{1,0:T(8,128)(2,1)}, u32[]{:S(2)}) copy-start(bf16[128,4096]{1,0:T(8,128)(2,1)} %own_ref.1) | copy-start | bytes 3145732
  107.0 3.6 %copy-start.9 = (s32[2]{0:T(128)S(1)}, s32[2]{0:T(128)}, u32[]{:S(2)}) copy-start(s32[2]{0:T(128)} %param.15) | copy-start | bytes 28
  107.0 5.8 %collective-permute-start.10 = (bf16[128,2048]{1,0:T(8,128)(2,1)}, bf16[128,2048]{1,0:T(8,128)(2,1)}, u32[]{:S(2)}, u32[]{:S(2)}) collective-permute-start(bf16[128,2048]{1,0:T(8,128)(2,1)} %get-tuple-element.20), channel_id=1, source_target_pairs={{0,16},{16,0},{1,17},{17,1},{2,18},{18,2},{3,19},{19,3},{4,20},{20... | collective-permute-start | bytes 1572872 | tf_op jit(solution)/shard_map/ppermute | solution.py:235
  108.9 3.9 %collective-permute-start.11 = (bf16[128,2048]{1,0:T(8,128)(2,1)S(1)}, bf16[128,2048]{1,0:T(8,128)(2,1)}, u32[]{:S(2)}, u32[]{:S(2)}) collective-permute-start(bf16[128,2048]{1,0:T(8,128)(2,1)S(1)} %get-tuple-element.22), channel_id=1, source_target_pairs={{0,16},{16,0},{1,17},{17,1},{2,18},{18,2},{3,19},{19,3},{4,20},{20... | collective-permute-start | bytes 1572872 | tf_op jit(solution)/shard_map/ppermute | solution.py:235
  110.6 2.3 %copy-start.8 = (f32[128,4096]{1,0:T(8,128)S(1)}, f32[128,4096]{1,0:T(8,128)}, u32[]{:S(2)}) copy-start(f32[128,4096]{1,0:T(8,128)} %convert_element_type.21) | copy-start | bytes 6291460

commit v2 on v1

v2 whole, which is shorter than its diff:
```python
import functools
import math

import jax
import jax.numpy as jnp
from jax import lax
from jax.experimental import pallas as pl
from jax.experimental.pallas import tpu as pltpu
from jax.sharding import PartitionSpec as P

HD = 128
NORM_EPS = 1e-05
MASKED = -1e30
MIB = 1024 * 1024


IN_VMEM = pl.BlockSpec(memory_space=pltpu.VMEM)
IN_PLACE = pl.BlockSpec(memory_space=pl.ANY)


def call(kernel, name, args, outs, flops, limit=8, scratch=(), out_specs=IN_VMEM, exps=0):
    outs_list = outs if isinstance(outs, list) else [outs]
    moved = sum(math.prod(a.shape) * a.dtype.itemsize for a in list(args) + outs_list)
    return pl.pallas_call(
        kernel,
        in_specs=[IN_VMEM] * len(args),
        out_specs=jax.tree.map(lambda _: out_specs, outs),
        out_shape=outs,
        scratch_shapes=scratch,
        compiler_params=pltpu.CompilerParams(vmem_limit_bytes=limit * MIB),
        cost_estimate=pl.CostEstimate(flops=flops, bytes_accessed=moved, transcendentals=exps),
        name=name,
    )(*args)


def norm_kernel(x_ref, gain_ref, out_ref):
    step = 16
    for start in range(0, x_ref.shape[0], step):
        wide = x_ref[start : start + step, :].astype(jnp.float32)
        mean = jnp.mean(wide * wide, axis=1, keepdims=True)
        normed = wide * lax.rsqrt(mean + NORM_EPS) * gain_ref[...]
        out_ref[start : start + step, :] = normed.astype(jnp.bfloat16)


def norm(tokens, gain):
    out = jax.ShapeDtypeStruct(tokens.shape, jnp.bfloat16)
    return call(norm_kernel, "norm", (tokens, gain[None, :]), out, 4 * tokens.size)


def project_kv_kernel(own_ref, other_ref, wk_ref, wv_ref, kv_ref):
    rows = jnp.concatenate([own_ref[...], other_ref[...]], axis=0)
    for head in range(kv_ref.shape[0]):
        cols = slice(head * HD, (head + 1) * HD)
        weights = jnp.concatenate([wk_ref[:, cols], wv_ref[:, cols]], axis=1)
        pair = jnp.dot(rows, weights, preferred_element_type=jnp.float32).astype(jnp.bfloat16)
        kv_ref[head, 0] = pair[:, :HD]
        kv_ref[head, 1] = pair[:, HD:]


def project_kv(own, other, w_key, w_value):
    half, width = own.shape
    heads = w_key.shape[1] // HD
    out = jax.ShapeDtypeStruct((heads, 2, 2 * half, HD), jnp.bfloat16)
    flops = 8 * half * width * heads * HD
    return call(project_kv_kernel, "project_kv", (own, other, w_key, w_value), out, flops)


def project_query_kernel(own_ref, other_ref, w_ref, out_ref):
    rows = jnp.concatenate([own_ref[...], other_ref[...]], axis=0)
    tile = 512
    for start in range(0, w_ref.shape[1], tile):
        part = jnp.dot(
            rows, w_ref[:, start : start + tile], preferred_element_type=jnp.float32
        )
        out_ref[:, start : start + tile] = part.astype(out_ref.dtype)


def project_query(own, other, w_query):
    half, width = own.shape
    out = jax.ShapeDtypeStruct((2 * half, w_query.shape[1]), jnp.bfloat16)
    flops = 4 * half * w_query.size
    return call(project_query_kernel, "project_query", (own, other, w_query), out, flops)


def attention_kernel(block_count, first, last, group, *refs):
    seg_q, pos_q, seg_k, pos_k, q_ref = refs[:5]
    blocks = refs[5 : 5 + block_count]
    refs = refs[5 + block_count :]
    if not first:
        acc_in, peak_in, mass_in = refs[:3]
        refs = refs[3:]
    if last:
        out_ref, bias_ref = refs
    else:
        acc_out, peak_out, mass_out, bias_ref = refs
    seen = (seg_q[...] == seg_k[...]) & (pos_k[...] <= pos_q[...])
    bias_ref[...] = jnp.where(seen, 0.0, MASKED)
    rows = q_ref.shape[0]
    width = seg_k.shape[1]
    factor = math.log2(math.e) / math.sqrt(HD)
    for head in range(q_ref.shape[1] // HD):
        if head % group == 0:
            keys = jnp.concatenate([block[head // group, 0] for block in blocks], axis=0)
            values = jnp.concatenate([block[head // group, 1] for block in blocks], axis=0)
            values = jnp.concatenate([values, jnp.ones_like(values)], axis=1)
        cols = slice(head * HD, (head + 1) * HD)
        scores = lax.dot_general(
            q_ref[:, cols], keys, (((1,), (1,)), ((), ())), preferred_element_type=jnp.float32
        )
        scores = scores + bias_ref[...]
        peak = jnp.broadcast_to(jnp.max(scores, axis=1, keepdims=True), (rows, HD))
        if not first:
            old = peak_in[:, cols]
            peak = jnp.maximum(peak, old)
        shift = peak * factor
        weights = jnp.concatenate(
            [
                jnp.exp2(scores[:, at : at + HD] * factor - shift).astype(jnp.bfloat16)
                for at in range(0, width, HD)
            ],
            axis=1,
        )
        total = jnp.dot(weights, values, preferred_element_type=jnp.float32)
        acc = total[:, :HD]
        mass = total[:, HD:]
        if not first:
            keep = jnp.exp2((old - peak) * factor)
            acc = acc + acc_in[:, cols] * keep
            mass = mass + mass_in[:, cols] * keep
        if last:
            out_ref[:, cols] = (acc / mass).astype(jnp.bfloat16)
        else:
            acc_out[:, cols] = acc
            peak_out[:, cols] = peak
            mass_out[:, cols] = mass


def attend(query, blocks, sources, segs, positions, state, last):
    rows, q_cols = query.shape
    group = q_cols // HD // blocks[0].shape[0]
    seg_k = jnp.concatenate([segs(s) for s in sources])[None, :]
    pos_k = jnp.concatenate([positions(s) for s in sources])[None, :]
    keys = len(blocks) * rows
    args = [segs(None)[:, None], positions(None)[:, None], seg_k, pos_k, query, *blocks]
    first = state is None
    args += [] if first else state
    if last:
        outs = jax.ShapeDtypeStruct((rows, q_cols), jnp.bfloat16)
    else:
        outs = [jax.ShapeDtypeStruct((rows, q_cols), jnp.float32)] * 3
    return call(
        functools.partial(attention_kernel, len(blocks), first, last, group),
        "attend",
        args,
        outs,
        6 * rows * keys * q_cols,
        limit=14,
        scratch=[pltpu.VMEM((rows, keys), jnp.float32)],
        exps=rows * keys * q_cols // HD,
    )


def project_out_kernel(pieces, x_ref, w_ref, own_ref, other_ref, *, piece):
    half = own_ref.shape[0]
    cols = own_ref.shape[1]
    tile = 512
    for start in range(0, cols, tile):
        at = piece * cols + start
        part = jnp.dot(
            x_ref[...], w_ref[:, at : at + tile], preferred_element_type=jnp.float32
        )
        own_ref[:, start : start + tile] = part[:half]
        other_ref[:, start : start + tile] = part[half:].astype(other_ref.dtype)


def project_out(attention, w_out, piece, pieces):
    rows, depth = attention.shape
    cols = w_out.shape[1] // pieces
    outs = [
        jax.ShapeDtypeStruct((rows // 2, cols), jnp.float32),
        jax.ShapeDtypeStruct((rows // 2, cols), jnp.bfloat16),
    ]
    return call(
        functools.partial(project_out_kernel, pieces, piece=piece),
        "project_out",
        (attention, w_out),
        outs,
        2 * rows * depth * cols,
    )


def finish_kernel(pieces, tokens_ref, *refs):
    mine, theirs = refs[:pieces], refs[pieces : 2 * pieces]
    mixed_hbm, out_hbm, mixed, out, sems = refs[2 * pieces :]
    cols = mine[0].shape[1]
    copies = []
    for piece in range(pieces):
        at = slice(piece * cols, (piece + 1) * cols)
        branch = mine[piece][...] + theirs[piece][...].astype(jnp.float32)
        out[:, at] = branch.astype(out.dtype)
        mixed[:, at] = (tokens_ref[:, at].astype(jnp.float32) + branch).astype(mixed.dtype)
        for number, (here, there) in enumerate(((out, out_hbm), (mixed, mixed_hbm))):
            copies.append(
                pltpu.make_async_copy(here.at[:, at], there.at[:, at], sems.at[piece, number])
            )
            copies[-1].start()
    for copy in copies:
        copy.wait()


def finish(tokens, mine, theirs):
    pieces = len(mine)
    outs = [jax.ShapeDtypeStruct(tokens.shape, jnp.bfloat16)] * 2
    return call(
        functools.partial(finish_kernel, pieces),
        "finish",
        (tokens, *mine, *theirs),
        outs,
        2 * tokens.size,
        scratch=[
            pltpu.VMEM(tokens.shape, jnp.bfloat16),
            pltpu.VMEM(tokens.shape, jnp.bfloat16),
            pltpu.SemaphoreType.DMA((pieces, 2)),
        ],
        out_specs=IN_PLACE,
    )


def after(values, *others):
    return lax.optimization_barrier((values, others))[0]


def swap_cores(value):
    return lax.ppermute(value, "kv", [(0, 1), (1, 0)])


def cube_exchanges(block, index, count):
    half = count // 2

    def exchange(value, bit):
        return lax.ppermute(value, "seq", [(i, i ^ bit) for i in range(count)])

    pairs = [(i, i ^ 4) for i in range(count)]
    for start in range(half, count, half):
        before = start - 1
        pairs = [p for p in pairs if p[0] != before and p[1] != start] + [(before, start)]
    from_x = exchange(block, 1)
    from_y = exchange(block, 2)
    from_z = lax.ppermute(block, "seq", pairs)
    seam = (index % half == 0) & (index > 0)
    z_source = jnp.where(seam, index - 1, index ^ 4)
    near = [(from_x, index ^ 1), (from_y, index ^ 2), (from_z, z_source)]
    work = yield near
    from_x, from_y, from_z = after((from_x, from_y, from_z), work)
    from_xy = exchange(from_y, 1)
    from_yz = exchange(from_z, 2)
    from_xz = exchange(from_x, 4)
    far = [(from_xy, index ^ 3), (from_yz, index ^ 6), (from_xz, index ^ 5)]
    work = yield far
    from_xy, from_yz, from_xz = after((from_xy, from_yz, from_xz), work)
    flat = lambda value: value.reshape((-1,) + value.shape[2:])
    last = jnp.concatenate(
        [
            exchange(flat(from_yz)[:3], 1),
            exchange(flat(from_xz)[3:6], 2),
            exchange(flat(from_xy)[6:], 4),
        ]
    ).reshape(block.shape)
    yield [(last, index ^ 7)]


def distance_exchanges(block, index, count, reach):
    step = 3
    for start in range(1, reach + 1, step):
        received = []
        for distance in range(start, min(start + step, reach + 1)):
            moved = lax.ppermute(block, "seq", [(i, i + distance) for i in range(count - distance)])
            received.append((moved, index - distance))
        work = yield received
        block = after(block, work)


def shards(tokens, gain, w_query, w_key, w_value, w_out, segment_ids, page_table):
    half_rows = tokens.shape[0]
    block_rows = 2 * half_rows
    count = lax.axis_size("seq")
    index = lax.axis_index("seq")
    core = lax.axis_index("kv")
    reach = min(8, count // 2 - 1)

    normed = norm(tokens, gain)
    other_normed = swap_cores(normed)
    own_block = project_kv(normed, other_normed, w_key, w_value)

    if count == 2 * (reach + 1) and count // 2 == 8:
        exchanges = cube_exchanges(own_block, index, count)
    else:
        exchanges = distance_exchanges(own_block, index, count, reach)
    group = [(own_block, index)] + next(exchanges)

    query = project_query(normed, other_normed, w_query)

    offsets = jnp.arange(half_rows, dtype=jnp.int32)
    local = jnp.concatenate([core * half_rows + offsets, (1 - core) * half_rows + offsets])

    def positions(source):
        return (index if source is None else source) * block_rows + local

    def segs(source):
        start = jnp.maximum(index if source is None else source, 0) * block_rows
        first = lax.dynamic_slice_in_dim(segment_ids, start + core * half_rows, half_rows)
        second = lax.dynamic_slice_in_dim(segment_ids, start + (1 - core) * half_rows, half_rows)
        found = jnp.concatenate([first, second])
        return found if source is None else jnp.where(source >= 0, found, -1)

    heads = own_block.shape[0]
    pages = own_block.reshape(heads, 2, 2, half_rows, HD).transpose(2, 1, 0, 3, 4)
    own_slot = lax.dynamic_index_in_dim(page_table, core, keepdims=False)
    page_pool = jnp.where(own_slot == 0, pages, pages[::-1])

    state, done = None, query
    while group:
        blocks = [block for block, _ in group]
        sources = [source for _, source in group]
        try:
            following = exchanges.send(done)
        except StopIteration:
            following = None
        state = attend(query, blocks, sources, segs, positions, state, following is None)
        group, done = following, (state, page_pool)
    attention = state

    pieces = 2
    parts = [project_out(attention, w_out, piece, pieces) for piece in range(pieces)]
    mine = [part for part, _ in parts]
    theirs = [swap_cores(part) for _, part in parts]
    mixed, attn_out = finish(tokens, mine, theirs)
    return (mixed, attn_out, page_pool)


def solution(mesh):
    in_specs = (
        P(("seq", "kv"), None),
        P(),
        P(None, "kv"),
        P(None, "kv"),
        P(None, "kv"),
        P("kv", None),
        P(),
        P("seq"),
    )
    out_specs = (P(("seq", "kv"), None), P(("seq", "kv"), None), P("seq", None, "kv", None, None))
    return jax.shard_map(shards, mesh=mesh, in_specs=in_specs, out_specs=out_specs, check_vma=False)
```

time: 117 us -> 74.2 us (0.63)
  the two profiles are of different devices: /device:TPU:17 before, /device:TPU:25 now
where the time goes in v2:
time: 74.2 us; the launch traced here: 73.9 us
  Pallas kernels  29 us (39%)
  starting transfers between devices  21 us (28%)
  local copies, waits for them, and re-layouts  13.2 us (18%)
  waiting for transfers between devices  7.51 us (10%)
  between operations  1.95 us (3%)
  other arithmetic  1.12 us (2%)
    pallas_call x9, Pallas kernels, call(): pl.pallas_call(kernel, in_specs=[IN_VMEM] * len(args), out_specs=jax.tree...  29 us
    ppermute x8, starting transfers between devices, exchange(): return lax.ppermute(value, 'seq', [(i, i ^ bit) for i in range(count)])  14.8 us
    unnamed x24, local copies, waits for them, and re-layouts  12.1 us
    ppermute x3, starting transfers between devices, swap_cores(): return lax.ppermute(value, 'kv', [(0, 1), (1, 0)])  4.72 us
    ppermute x3, waiting for transfers between devices, swap_cores(): return lax.ppermute(value, 'kv', [(0, 1), (1, 0)])  3.87 us
    ppermute x8, waiting for transfers between devices, exchange(): return lax.ppermute(value, 'seq', [(i, i ^ bit) for i in range(count)])  2.41 us
  transfers between devices with their start and end apart: 12, of which 5 were waited for; matrix products, arithmetic and copies ran while one was open for 3% of the time, Pallas kernels for 24%

profile of v2, /device:TPU:25, one launch (start us, length us, event | category | flops | bytes accessed | tf_op | source)
XLA Modules:
  0.0 73.9 jit_solution(14432815660637555975)
XLA Ops:
  0.6 0.0 copy-start.3
  0.6 1.2 %copy-done.3 = bf16[128,4096]{1,0:T(8,128)(2,1)S(1)} copy-done((bf16[128,4096]{1,0:T(8,128)(2,1)S(1)}, bf16[128,4096]{1,0:T(8,128)(2,1)}, u32[]{:S(2)}) %copy-start.3) | copy-done | bytes 1048600
  1.9 0.7 copy-done.5
  2.6 0.5 norm.1.own_ref
  3.1 0.7 %collective-permute-start = (bf16[128,4096]{1,0:T(8,128)(2,1)S(1)}, bf16[128,4096]{1,0:T(8,128)(2,1)S(1)}, u32[]{:S(2)}, u32[]{:S(2)}) collective-permute-start(bf16[128,4096]{1,0:T(8,128)(2,1)S(1)} %norm.1.own_ref), channel_id=1, source_target_pairs={{0,16},{16,0},{1,17},{17,1},{2,18},{18,2},{3,19},{19,3},{4,20},{20... | collective-permute-start | bytes 3145736 | tf_op jit(solution)/shard_map/ppermute | solution.py:234
  3.9 0.2 fusion.4
  4.2 0.1 copy.20
  4.4 1.7 %collective-permute-done.other_ref = bf16[128,4096]{1,0:T(8,128)(2,1)S(1)} collective-permute-done((bf16[128,4096]{1,0:T(8,128)(2,1)S(1)}, bf16[128,4096]{1,0:T(8,128)(2,1)S(1)}, u32[]{:S(2)}, u32[]{:S(2)}) %collective-permute-start) | collective-permute-done | bytes 1048608 | tf_op jit(solution)/shard_map/ppermute | solution.py:234
  6.1 2.2 %copy-done.1 = bf16[4096,512]{1,0:T(8,128)(2,1)S(1)} copy-done((bf16[4096,512]{1,0:T(8,128)(2,1)S(1)}, bf16[4096,512]{1,0:T(8,128)(2,1)}, u32[]{:S(2)}) %copy-start.1) | copy-done | bytes 4194328
  8.3 2.2 %copy-done.2 = bf16[4096,512]{1,0:T(8,128)(2,1)S(1)} copy-done((bf16[4096,512]{1,0:T(8,128)(2,1)S(1)}, bf16[4096,512]{1,0:T(8,128)(2,1)}, u32[]{:S(2)}) %copy-start.2) | copy-done | bytes 4194328
  10.5 2.3 %project_kv.1.refs_5_ = bf16[4,2,256,128]{3,2,1,0:T(8,128)(2,1)S(1)} custom-call(bf16[128,4096]{1,0:T(8,128)(2,1)S(1)} %norm.1.own_ref, bf16[128,4096]{1,0:T(8,128)(2,1)S(1)} %collective-permute-done.other_ref, bf16[4096,512]{1,0:T(8,128)(2,1)S(1)} %copy-done.1, bf16[4096,512]{1,0:T(8,128)(2,1)S(1)} %copy-done.2), custom_call_target="tpu_custom_call" | custom-call | flops 2147483648 | bytes 11010048 | tf_op jit(solution)/shard_map/project_kv/pallas_call | solution.py:24
  12.8 1.3 %collective-permute-start.1 = (bf16[4,2,256,128]{3,2,1,0:T(8,128)(2,1)S(1)}, bf16[4,2,256,128]{3,2,1,0:T(8,128)(2,1)S(1)}, u32[]{:S(2)}, u32[]{:S(2)}) collective-permute-start(bf16[4,2,256,128]{3,2,1,0:T(8,128)(2,1)S(1)} %project_kv.1.refs_5_), channel_id=1, source_target_pairs={{0,1},{1,0},{2,3},{3,2},{4,5},{5,4},{6,7},{7,6},{8,9},{9,8},{10,11... | collective-permute-start | bytes 1572872 | tf_op jit(solution)/shard_map/ppermute | solution.py:241
  14.1 1.2 %collective-permute-start.2 = (bf16[4,2,256,128]{3,2,1,0:T(8,128)(2,1)S(1)}, bf16[4,2,256,128]{3,2,1,0:T(8,128)(2,1)}, u32[]{:S(2)}, u32[]{:S(2)}) collective-permute-start(bf16[4,2,256,128]{3,2,1,0:T(8,128)(2,1)S(1)} %project_kv.1.refs_5_), channel_id=1, source_target_pairs={{0,2},{1,3},{2,0},{3,1},{4,6},{5,7},{6,4},{7,5},{8,10},{9,11},{10,... | collective-permute-start | bytes 1572872 | tf_op jit(solution)/shard_map/ppermute | solution.py:241
  15.3 1.5 %collective-permute-start.3 = (bf16[4,2,256,128]{3,2,1,0:T(8,128)(2,1)S(1)}, bf16[4,2,256,128]{3,2,1,0:T(8,128)(2,1)}, u32[]{:S(2)}, u32[]{:S(2)}) collective-permute-start(bf16[4,2,256,128]{3,2,1,0:T(8,128)(2,1)S(1)} %project_kv.1.refs_5_), channel_id=1, source_target_pairs={{0,4},{1,5},{2,6},{3,7},{4,0},{5,1},{6,2},{8,12},{9,13},{10,14},{1... | collective-permute-start | bytes 1572872 | tf_op jit(solution)/shard_map/ppermute | solution.py:249
  16.8 0.1 copy.24.refs_0_
  17.0 0.6 dynamic_slice.68
  18.3 0.0 copy-start
  18.3 5.8 %copy-done = bf16[4096,2048]{1,0:T(8,128)(2,1)S(1)} copy-done((bf16[4096,2048]{1,0:T(8,128)(2,1)S(1)}, bf16[4096,2048]{1,0:T(8,128)(2,1)}, u32[]{:S(2)}) %copy-start) | copy-done | bytes 16777240
  24.1 4.5 %project_query.1.refs_4_ = bf16[256,2048]{1,0:T(8,128)(2,1)S(1)} custom-call(bf16[128,4096]{1,0:T(8,128)(2,1)S(1)} %norm.1.own_ref, bf16[128,4096]{1,0:T(8,128)(2,1)S(1)} %collective-permute-done.other_ref, bf16[4096,2048]{1,0:T(8,128)(2,1)S(1)} %copy-done), custom_call_target="tpu_custom_call" | custom-call | flops 4294967296 | bytes 19922944 | tf_op jit(solution)/shard_map/project_query/pallas_call | solution.py:24
  28.6 0.0 collective-permute-done.1.refs_6_
  28.6 0.0 collective-permute-done.2.refs_7_
  28.6 1.2 %collective-permute-done.3.refs_8_ = bf16[4,2,256,128]{3,2,1,0:T(8,128)(2,1)} collective-permute-done((bf16[4,2,256,128]{3,2,1,0:T(8,128)(2,1)S(1)}, bf16[4,2,256,128]{3,2,1,0:T(8,128)(2,1)}, u32[]{:S(2)}, u32[]{:S(2)}) %collective-permute-start.3) | collective-permute-done | bytes 524320 | tf_op jit(solution)/shard_map/ppermute | solution.py:249
  29.8 0.2 collective-permute-start.4
  30.1 0.2 collective-permute-start.5
  30.3 8.5 %collective-permute-start.6 = (bf16[4,2,256,128]{3,2,1,0:T(8,128)(2,1)S(1)}, bf16[4,2,256,128]{3,2,1,0:T(8,128)(2,1)S(1)}, u32[]{:S(2)}, u32[]{:S(2)}) collective-permute-start(bf16[4,2,256,128]{3,2,1,0:T(8,128)(2,1)S(1)} %collective-permute-done.1.refs_6_), channel_id=1, source_target_pairs={{0,4},{1,5},{2,6},{3,7},{4,0},{5,1},{6,2},{7,3},{8,12},{9,13},{10,... | collective-permute-start | bytes 1572872 | tf_op jit(solution)/shard_map/ppermute | solution.py:241
  38.7 0.9 %reverse_select_fusion = bf16[2,2,4,128,128]{4,3,2,1,0:T(8,128)(2,1)} fusion(bf16[2,2,4,128,128]{4,3,2,1,0:T(8,128)(2,1)S(1)} %bitcast.35, pred[]{:T(512)} %bitcast.10), kind=kLoop, calls=%fused_computation | loop fusion | flops 262144 | bytes 1048577 | tf_op jit(solution)/shard_map/jit(_where)/select_n | solution.py:319
  39.7 7.4 %attend.3 = (f32[256,2048]{1,0:T(8,128)S(1)}, f32[256,2048]{1,0:T(8,128)S(1)}, f32[256,2048]{1,0:T(8,128)S(1)}) custom-call(s32[256,1]{1,0:T(8,128)S(1)} %copy.24.refs_0_, s32[256,1]{1,0:T(8,128)S(1)} %broadcast_add_fusion.refs_1_, s32[1,1024]{1,0:T(1,128)S(1)} %bitcast.33, s32[1,1024]{1,0:T(1,128)S(1)} %bitcast.34, ...), custom_call_target="tpu_custom_call" | custom-call | flops 3221225472 | bytes 9447424 | tf_op jit(solution)/shard_map/attend/pallas_call | solution.py:24
  47.1 0.0 collective-permute-done.4.refs_5_
  47.1 0.0 collective-permute-done.5.refs_6_
  47.1 2.4 %collective-permute-done.6.refs_7_ = bf16[4,2,256,128]{3,2,1,0:T(8,128)(2,1)S(1)} collective-permute-done((bf16[4,2,256,128]{3,2,1,0:T(8,128)(2,1)S(1)}, bf16[4,2,256,128]{3,2,1,0:T(8,128)(2,1)S(1)}, u32[]{:S(2)}, u32[]{:S(2)}) %collective-permute-start.6) | collective-permute-done | bytes 524320 | tf_op jit(solution)/shard_map/ppermute | solution.py:241
  49.5 1.2 %collective-permute-start.7 = (bf16[3,256,128]{2,1,0:T(8,128)(2,1)S(1)}, bf16[3,256,128]{2,1,0:T(8,128)(2,1)S(1)}, u32[]{:S(2)}, u32[]{:S(2)}) collective-permute-start(bf16[3,256,128]{2,1,0:T(8,128)(2,1)S(1)} %slice.16), channel_id=1, source_target_pairs={{0,1},{1,0},{2,3},{3,2},{4,5},{5,4},{6,7},{7,6},{8,9},{9,8},{10,11... | collective-permute-start | bytes 589832 | tf_op jit(solution)/shard_map/ppermute | solution.py:241
  50.7 1.0 %collective-permute-start.8 = (bf16[3,256,128]{2,1,0:T(8,128)(2,1)S(1)}, bf16[3,256,128]{2,1,0:T(8,128)(2,1)S(1)}, u32[]{:S(2)}, u32[]{:S(2)}) collective-permute-start(bf16[3,256,128]{2,1,0:T(8,128)(2,1)S(1)} %slice.17), channel_id=1, source_target_pairs={{0,2},{1,3},{2,0},{3,1},{4,6},{5,7},{6,4},{7,5},{8,10},{9,11},{10,... | collective-permute-start | bytes 589832 | tf_op jit(solution)/shard_map/ppermute | solution.py:241
  51.7 0.0 slice-start.2
  51.7 1.2 %collective-permute-start.9 = (bf16[2,256,128]{2,1,0:T(8,128)(2,1)S(1)}, bf16[2,256,128]{2,1,0:T(8,128)(2,1)S(1)}, u32[]{:S(2)}, u32[]{:S(2)}) collective-permute-start(bf16[2,256,128]{2,1,0:T(8,128)(2,1)S(1)} %slice_bitcast_fusion), channel_id=1, source_target_pairs={{0,4},{1,5},{2,6},{3,7},{4,0},{5,1},{6,2},{7,3},{8,12},{9,13},{10,... | collective-permute-start | bytes 393224 | tf_op jit(solution)/shard_map/ppermute | solution.py:241
  53.0 5.7 %attend.4 = (f32[256,2048]{1,0:T(8,128)S(1)}, f32[256,2048]{1,0:T(8,128)S(1)}, f32[256,2048]{1,0:T(8,128)S(1)}) custom-call(s32[256,1]{1,0:T(8,128)S(1)} %copy.24.refs_0_, s32[256,1]{1,0:T(8,128)S(1)} %broadcast_add_fusion.refs_1_, s32[1,768]{1,0:T(1,128)S(1)} %broadcast_in_dim.44.refs_2_, s32[1,768]{1,0:T(1,128)S(1)} %broadcast_in_dim.45.refs_3_, ...), custom_call_target="tpu_custom_call" | custom-call | flops 2415919104 | bytes 15212544 | tf_op jit(solution)/shard_map/attend/pallas_call | solution.py:24
  58.7 0.0 collective-permute-done.9
  58.7 0.0 collective-permute-done.8
  58.7 0.1 pad_maximum_fusion
  58.8 0.0 slice-start.3
  58.8 2.5 %attend.5.x_ref = bf16[256,2048]{1,0:T(8,128)(2,1)S(1)} custom-call(s32[256,1]{1,0:T(8,128)S(1)} %copy.24.refs_0_, s32[256,1]{1,0:T(8,128)S(1)} %broadcast_add_fusion.refs_1_, s32[1,256]{1,0:T(1,128)S(1)} %broadcast_select_fusion.refs_2_, s32[1,256]{1,0:T(1,128)S(1)} %add_add_fusion.refs_3_, bf16[256,2048]{1,0:T(8,128)(2,1)S(1)} %project_query.1.refs_4_, ...), custom_call_target="tpu_custom_call" | custom-call | flops 805306368 | bytes 8916992 | tf_op jit(solution)/shard_map/attend/pallas_call | solution.py:24
  61.4 2.3 %project_out.2 = (f32[128,2048]{1,0:T(8,128)S(1)}, bf16[128,2048]{1,0:T(8,128)(2,1)S(1)}) custom-call(bf16[256,2048]{1,0:T(8,128)(2,1)S(1)} %attend.5.x_ref, bf16[2048,4096]{1,0:T(8,128)(2,1)S(1)} %bitcast.27), custom_call_target="tpu_custom_call" | custom-call | flops 2147483648 | bytes 19398656 | tf_op jit(solution)/shard_map/project_out/pallas_call | solution.py:24
  63.7 0.0 copy-start.4
  63.7 2.3 %project_out.3 = (f32[128,2048]{1,0:T(8,128)S(1)}, bf16[128,2048]{1,0:T(8,128)(2,1)S(1)}) custom-call(bf16[256,2048]{1,0:T(8,128)(2,1)S(1)} %attend.5.x_ref, bf16[2048,4096]{1,0:T(8,128)(2,1)S(1)} %bitcast.27), custom_call_target="tpu_custom_call" | custom-call | flops 2147483648 | bytes 19398656 | tf_op jit(solution)/shard_map/project_out/pallas_call | solution.py:24
  66.0 3.9 %collective-permute-start.10 = (bf16[128,2048]{1,0:T(8,128)(2,1)S(1)}, bf16[128,2048]{1,0:T(8,128)(2,1)S(1)}, u32[]{:S(2)}, u32[]{:S(2)}) collective-permute-start(bf16[128,2048]{1,0:T(8,128)(2,1)S(1)} %get-tuple-element.35), channel_id=1, source_target_pairs={{0,16},{16,0},{1,17},{17,1},{2,18},{18,2},{3,19},{19,3},{4,20},{20... | collective-permute-start | bytes 1572872 | tf_op jit(solution)/shard_map/ppermute | solution.py:234
  69.9 0.1 collective-permute-start.11
  70.0 1.5 %collective-permute-done.10.refs_2_ = bf16[128,2048]{1,0:T(8,128)(2,1)S(1)} collective-permute-done((bf16[128,2048]{1,0:T(8,128)(2,1)S(1)}, bf16[128,2048]{1,0:T(8,128)(2,1)S(1)}, u32[]{:S(2)}, u32[]{:S(2)}) %collective-permute-start.10) | collective-permute-done | bytes 524320 | tf_op jit(solution)/shard_map/ppermute | solution.py:234
  71.5 0.7 %collective-permute-done.11.refs_3_ = bf16[128,2048]{1,0:T(8,128)(2,1)S(1)} collective-permute-done((bf16[128,2048]{1,0:T(8,128)(2,1)S(1)}, bf16[128,2048]{1,0:T(8,128)(2,1)S(1)}, u32[]{:S(2)}, u32[]{:S(2)}) %collective-permute-start.11) | collective-permute-done | bytes 524320 | tf_op jit(solution)/shard_map/ppermute | solution.py:234
  72.2 1.4 %finish.1 = (bf16[128,4096]{1,0:T(8,128)(2,1)}, bf16[128,4096]{1,0:T(8,128)(2,1)}) custom-call(bf16[128,4096]{1,0:T(8,128)(2,1)S(1)} %copy-done.4, f32[128,2048]{1,0:T(8,128)S(1)} %get-tuple-element.33.refs_0_, f32[128,2048]{1,0:T(8,128)S(1)} %get-tuple-element.34.refs_1_, bf16[128,2048]{1,0:T(8,128)(2,1)S(1)} %collective-permute-done.10.refs_2_, ...), custom_call_target="tpu_custom_call" | custom-call | flops 1048576 | bytes 6291456 | tf_op jit(solution)/shard_map/finish/pallas_call | solution.py:24
  (39 shorter events, 0.3 us)
Async XLA Ops:
  0.6 1.2 %copy-start.3 = (bf16[128,4096]{1,0:T(8,128)(2,1)S(1)}, bf16[128,4096]{1,0:T(8,128)(2,1)}, u32[]{:S(2)}) copy-start(bf16[128,4096]{1,0:T(8,128)(2,1)} %tokens_ref.1) | copy-start | bytes 3145732
  1.9 0.7 copy-start.5
  2.6 1.4 %copy-start.6 = (s32[4096]{0:T(1024)S(1)}, s32[4096]{0:T(1024)}, u32[]{:S(2)}) copy-start(s32[4096]{0:T(1024)} %param.14) | copy-start | bytes 49156
  3.1 3.0 %collective-permute-start = (bf16[128,4096]{1,0:T(8,128)(2,1)S(1)}, bf16[128,4096]{1,0:T(8,128)(2,1)S(1)}, u32[]{:S(2)}, u32[]{:S(2)}) collective-permute-start(bf16[128,4096]{1,0:T(8,128)(2,1)S(1)} %norm.1.own_ref), channel_id=1, source_target_pairs={{0,16},{16,0},{1,17},{17,1},{2,18},{18,2},{3,19},{19,3},{4,20},{20... | collective-permute-start | bytes 3145736 | tf_op jit(solution)/shard_map/ppermute | solution.py:234
  6.1 2.2 %copy-start.1 = (bf16[4096,512]{1,0:T(8,128)(2,1)S(1)}, bf16[4096,512]{1,0:T(8,128)(2,1)}, u32[]{:S(2)}) copy-start(bf16[4096,512]{1,0:T(8,128)(2,1)} %wk_ref.1) | copy-start | bytes 12582916
  8.3 2.2 %copy-start.2 = (bf16[4096,512]{1,0:T(8,128)(2,1)S(1)}, bf16[4096,512]{1,0:T(8,128)(2,1)}, u32[]{:S(2)}) copy-start(bf16[4096,512]{1,0:T(8,128)(2,1)} %wv_ref.1) | copy-start | bytes 12582916
  10.5 6.5 %copy-start.7 = (s32[2]{0:T(128)S(1)}, s32[2]{0:T(128)}, u32[]{:S(2)}) copy-start(s32[2]{0:T(128)} %param.15) | copy-start | bytes 28
  12.8 15.7 %collective-permute-start.1 = (bf16[4,2,256,128]{3,2,1,0:T(8,128)(2,1)S(1)}, bf16[4,2,256,128]{3,2,1,0:T(8,128)(2,1)S(1)}, u32[]{:S(2)}, u32[]{:S(2)}) collective-permute-start(bf16[4,2,256,128]{3,2,1,0:T(8,128)(2,1)S(1)} %project_kv.1.refs_5_), channel_id=1, source_target_pairs={{0,1},{1,0},{2,3},{3,2},{4,5},{5,4},{6,7},{7,6},{8,9},{9,8},{10,11... | collective-permute-start | bytes 1572872 | tf_op jit(solution)/shard_map/ppermute | solution.py:241
  14.1 14.5 %collective-permute-start.2 = (bf16[4,2,256,128]{3,2,1,0:T(8,128)(2,1)S(1)}, bf16[4,2,256,128]{3,2,1,0:T(8,128)(2,1)}, u32[]{:S(2)}, u32[]{:S(2)}) collective-permute-start(bf16[4,2,256,128]{3,2,1,0:T(8,128)(2,1)S(1)} %project_kv.1.refs_5_), channel_id=1, source_target_pairs={{0,2},{1,3},{2,0},{3,1},{4,6},{5,7},{6,4},{7,5},{8,10},{9,11},{10,... | collective-permute-start | bytes 1572872 | tf_op jit(solution)/shard_map/ppermute | solution.py:241
  15.3 14.5 %collective-permute-start.3 = (bf16[4,2,256,128]{3,2,1,0:T(8,128)(2,1)S(1)}, bf16[4,2,256,128]{3,2,1,0:T(8,128)(2,1)}, u32[]{:S(2)}, u32[]{:S(2)}) collective-permute-start(bf16[4,2,256,128]{3,2,1,0:T(8,128)(2,1)S(1)} %project_kv.1.refs_5_), channel_id=1, source_target_pairs={{0,4},{1,5},{2,6},{3,7},{4,0},{5,1},{6,2},{8,12},{9,13},{10,14},{1... | collective-permute-start | bytes 1572872 | tf_op jit(solution)/shard_map/ppermute | solution.py:249
  18.3 5.8 %copy-start = (bf16[4096,2048]{1,0:T(8,128)(2,1)S(1)}, bf16[4096,2048]{1,0:T(8,128)(2,1)}, u32[]{:S(2)}) copy-start(bf16[4096,2048]{1,0:T(8,128)(2,1)} %w_ref.3) | copy-start | bytes 50331652
  29.8 17.3 %collective-permute-start.4 = (bf16[4,2,256,128]{3,2,1,0:T(8,128)(2,1)}, bf16[4,2,256,128]{3,2,1,0:T(8,128)(2,1)S(1)}, u32[]{:S(2)}, u32[]{:S(2)}) collective-permute-start(bf16[4,2,256,128]{3,2,1,0:T(8,128)(2,1)} %collective-permute-done.2.refs_7_), channel_id=1, source_target_pairs={{0,1},{1,0},{2,3},{3,2},{4,5},{5,4},{6,7},{7,6},{8,9},{9,8},{10,11... | collective-permute-start | bytes 1572872 | tf_op jit(solution)/shard_map/ppermute | solution.py:241
  30.1 17.0 %collective-permute-start.5 = (bf16[4,2,256,128]{3,2,1,0:T(8,128)(2,1)}, bf16[4,2,256,128]{3,2,1,0:T(8,128)(2,1)S(1)}, u32[]{:S(2)}, u32[]{:S(2)}) collective-permute-start(bf16[4,2,256,128]{3,2,1,0:T(8,128)(2,1)} %collective-permute-done.3.refs_8_), channel_id=1, source_target_pairs={{0,2},{1,3},{2,0},{3,1},{4,6},{5,7},{6,4},{7,5},{8,10},{9,11},{10,... | collective-permute-start | bytes 1572872 | tf_op jit(solution)/shard_map/ppermute | solution.py:241
  30.3 19.2 %collective-permute-start.6 = (bf16[4,2,256,128]{3,2,1,0:T(8,128)(2,1)S(1)}, bf16[4,2,256,128]{3,2,1,0:T(8,128)(2,1)S(1)}, u32[]{:S(2)}, u32[]{:S(2)}) collective-permute-start(bf16[4,2,256,128]{3,2,1,0:T(8,128)(2,1)S(1)} %collective-permute-done.1.refs_6_), channel_id=1, source_target_pairs={{0,4},{1,5},{2,6},{3,7},{4,0},{5,1},{6,2},{7,3},{8,12},{9,13},{10,... | collective-permute-start | bytes 1572872 | tf_op jit(solution)/shard_map/ppermute | solution.py:241
  39.7 21.7 %slice-start = ((s8[16777216]{0:T(1024)(128)(4,1)}), s8[4194304]{0:T(1024)(128)(4,1)S(1)}, s32[]{:S(2)}) async-start(s8[16777216]{0:T(1024)(128)(4,1)} %bitcast.26), calls=%async_computation | async-start | bytes 8388608
  39.7 21.7 %slice-start.1 = ((s8[16777216]{0:T(1024)(128)(4,1)}), s8[4194304]{0:T(1024)(128)(4,1)S(1)}, s32[]{:S(2)}) async-start(s8[16777216]{0:T(1024)(128)(4,1)} %bitcast.26), calls=%async_computation.1 | async-start | bytes 8388608
  49.5 9.2 %collective-permute-start.7 = (bf16[3,256,128]{2,1,0:T(8,128)(2,1)S(1)}, bf16[3,256,128]{2,1,0:T(8,128)(2,1)S(1)}, u32[]{:S(2)}, u32[]{:S(2)}) collective-permute-start(bf16[3,256,128]{2,1,0:T(8,128)(2,1)S(1)} %slice.16), channel_id=1, source_target_pairs={{0,1},{1,0},{2,3},{3,2},{4,5},{5,4},{6,7},{7,6},{8,9},{9,8},{10,11... | collective-permute-start | bytes 589832 | tf_op jit(solution)/shard_map/ppermute | solution.py:241
  50.7 8.0 %collective-permute-start.8 = (bf16[3,256,128]{2,1,0:T(8,128)(2,1)S(1)}, bf16[3,256,128]{2,1,0:T(8,128)(2,1)S(1)}, u32[]{:S(2)}, u32[]{:S(2)}) collective-permute-start(bf16[3,256,128]{2,1,0:T(8,128)(2,1)S(1)} %slice.17), channel_id=1, source_target_pairs={{0,2},{1,3},{2,0},{3,1},{4,6},{5,7},{6,4},{7,5},{8,10},{9,11},{10,... | collective-permute-start | bytes 589832 | tf_op jit(solution)/shard_map/ppermute | solution.py:241
  51.7 9.6 %slice-start.2 = ((s8[16777216]{0:T(1024)(128)(4,1)}), s8[4194304]{0:T(1024)(128)(4,1)S(1)}, s32[]{:S(2)}) async-start(s8[16777216]{0:T(1024)(128)(4,1)} %bitcast.26), calls=%async_computation.2 | async-start | bytes 8388608
  51.7 7.0 %collective-permute-start.9 = (bf16[2,256,128]{2,1,0:T(8,128)(2,1)S(1)}, bf16[2,256,128]{2,1,0:T(8,128)(2,1)S(1)}, u32[]{:S(2)}, u32[]{:S(2)}) collective-permute-start(bf16[2,256,128]{2,1,0:T(8,128)(2,1)S(1)} %slice_bitcast_fusion), channel_id=1, source_target_pairs={{0,4},{1,5},{2,6},{3,7},{4,0},{5,1},{6,2},{7,3},{8,12},{9,13},{10,... | collective-permute-start | bytes 393224 | tf_op jit(solution)/shard_map/ppermute | solution.py:241
  58.8 2.6 %slice-start.3 = ((s8[16777216]{0:T(1024)(128)(4,1)}), s8[4194304]{0:T(1024)(128)(4,1)S(1)}, s32[]{:S(2)}) async-start(s8[16777216]{0:T(1024)(128)(4,1)} %bitcast.26), calls=%async_computation.3 | async-start | bytes 8388608
  63.7 8.5 %copy-start.4 = (bf16[128,4096]{1,0:T(8,128)(2,1)S(1)}, bf16[128,4096]{1,0:T(8,128)(2,1)}, u32[]{:S(2)}) copy-start(bf16[128,4096]{1,0:T(8,128)(2,1)} %tokens_ref.1) | copy-start | bytes 3145732
  66.0 5.4 %collective-permute-start.10 = (bf16[128,2048]{1,0:T(8,128)(2,1)S(1)}, bf16[128,2048]{1,0:T(8,128)(2,1)S(1)}, u32[]{:S(2)}, u32[]{:S(2)}) collective-permute-start(bf16[128,2048]{1,0:T(8,128)(2,1)S(1)} %get-tuple-element.35), channel_id=1, source_target_pairs={{0,16},{16,0},{1,17},{17,1},{2,18},{18,2},{3,19},{19,3},{4,20},{20... | collective-permute-start | bytes 1572872 | tf_op jit(solution)/shard_map/ppermute | solution.py:234
  69.9 2.3 %collective-permute-start.11 = (bf16[128,2048]{1,0:T(8,128)(2,1)S(1)}, bf16[128,2048]{1,0:T(8,128)(2,1)S(1)}, u32[]{:S(2)}, u32[]{:S(2)}) collective-permute-start(bf16[128,2048]{1,0:T(8,128)(2,1)S(1)} %get-tuple-element.36), channel_id=1, source_target_pairs={{0,16},{16,0},{1,17},{17,1},{2,18},{18,2},{3,19},{19,3},{4,20},{20... | collective-permute-start | bytes 1572872 | tf_op jit(solution)/shard_map/ppermute | solution.py:234

commit v3 on v2

v3 whole, which is shorter than its diff:
```python
import functools
import math
import typing

import jax
import jax.numpy as jnp
from jax import lax
from jax.experimental import pallas as pl
from jax.experimental.pallas import tpu as pltpu
from jax.sharding import PartitionSpec as P

HD = 128
NORM_EPS = 1e-05
MASKED = -1e30
MIB = 1024 * 1024


IN_VMEM = pl.BlockSpec(memory_space=pltpu.VMEM)
IN_PLACE = pl.BlockSpec(memory_space=pltpu.HBM)


def call(
    kernel,
    name,
    args,
    outs,
    flops,
    limit=8,
    scratch=(),
    in_specs=None,
    out_specs=IN_VMEM,
    exps=0,
    aliases=None,
):
    outs_list = outs if isinstance(outs, list) else [outs]
    moved = sum(math.prod(a.shape) * a.dtype.itemsize for a in list(args) + outs_list)
    return pl.pallas_call(
        kernel,
        in_specs=in_specs or [IN_VMEM] * len(args),
        out_specs=jax.tree.map(lambda _: out_specs, outs),
        out_shape=outs,
        scratch_shapes=scratch,
        input_output_aliases=aliases or {},
        compiler_params=pltpu.CompilerParams(vmem_limit_bytes=limit * MIB),
        cost_estimate=pl.CostEstimate(flops=flops, bytes_accessed=moved, transcendentals=exps),
        name=name,
    )(
        *(
            pltpu.with_memory_space_constraint(arg, pltpu.HBM) if spec is IN_PLACE else arg
            for arg, spec in zip(args, in_specs or [IN_VMEM] * len(args))
        )
    )


def norm_rows(x_ref, gain_ref, out_ref, first):
    step = 16
    for start in range(0, x_ref.shape[0], step):
        wide = x_ref[start : start + step, :].astype(jnp.float32)
        mean = jnp.mean(wide * wide, axis=1, keepdims=True)
        normed = wide * lax.rsqrt(mean + NORM_EPS) * gain_ref[...]
        out_ref[first + start : first + start + step, :] = normed.astype(jnp.bfloat16)


def stream(copies, ahead, use):
    for n in range(min(ahead, len(copies))):
        for copy in copies[n]:
            copy.start()
    for n in range(len(copies)):
        for copy in copies[n]:
            copy.wait()
        if n + ahead < len(copies):
            for copy in copies[n + ahead]:
                copy.start()
        use(n)


def project_kv_kernel(
    tokens_hbm, gain_hbm, wk_hbm, wv_hbm, other_ref, normed_ref, kv_ref,
    x_ref, gain_ref, wk_ref, wv_ref, sems,
):
    half = x_ref.shape[0]
    pairs = ((tokens_hbm, x_ref), (gain_hbm, gain_ref), (wk_hbm, wk_ref), (wv_hbm, wv_ref))
    copies = [pltpu.make_async_copy(*pair, sems.at[n]) for n, pair in enumerate(pairs)]
    for copy in copies:
        copy.start()
    copies[1].wait()
    norm_rows(other_ref, gain_ref, normed_ref, half)
    copies[0].wait()
    norm_rows(x_ref, gain_ref, normed_ref, 0)
    for n, ref in enumerate((wk_ref, wv_ref)):
        copies[2 + n].wait()
        part = jnp.dot(normed_ref[...], ref[...], preferred_element_type=jnp.float32)
        for head in range(kv_ref.shape[0]):
            kv_ref[head, n] = part[:, head * HD : (head + 1) * HD].astype(kv_ref.dtype)


def project_kv(tokens, other_tokens, gain, w_key, w_value):
    half, width = tokens.shape
    heads = w_key.shape[1] // HD
    outs = [
        jax.ShapeDtypeStruct((2 * half, width), jnp.bfloat16),
        jax.ShapeDtypeStruct((heads, 2, 2 * half, HD), jnp.bfloat16),
    ]
    return call(
        project_kv_kernel,
        "project_kv",
        (tokens, gain[None, :], w_key, w_value, other_tokens),
        outs,
        8 * half * width * heads * HD,
        limit=14,
        scratch=[
            pltpu.VMEM(tokens.shape, tokens.dtype),
            pltpu.VMEM((1, width), jnp.float32),
            pltpu.VMEM(w_key.shape, w_key.dtype),
            pltpu.VMEM(w_value.shape, w_value.dtype),
            pltpu.SemaphoreType.DMA((4,)),
        ],
        in_specs=[IN_PLACE] * 4 + [IN_VMEM],
    )


def project_query_kernel(depth, x_ref, w_hbm, out_ref, w_ref, acc_ref, sems):
    chunks = w_ref.shape[0] // depth
    copies = []
    for n in range(chunks):
        rows = slice(n * depth, (n + 1) * depth)
        copies.append([pltpu.make_async_copy(w_hbm.at[rows], w_ref.at[rows], sems.at[n])])

    def use(n):
        rows = slice(n * depth, (n + 1) * depth)
        tile = 512
        for start in range(0, out_ref.shape[1], tile):
            cols = slice(start, start + tile)
            part = jnp.dot(
                x_ref[:, rows], w_ref[rows, cols], preferred_element_type=jnp.float32
            )
            if n:
                part = part + acc_ref[:, cols]
            if n < chunks - 1:
                acc_ref[:, cols] = part
            else:
                out_ref[:, cols] = part.astype(out_ref.dtype)

    stream(copies, 3, use)


def project_query(normed, w_query, depth=512):
    out = (normed.shape[0], w_query.shape[1])
    return call(
        functools.partial(project_query_kernel, depth),
        "project_query",
        (normed, w_query),
        jax.ShapeDtypeStruct(out, jnp.bfloat16),
        2 * normed.shape[0] * w_query.size,
        limit=22,
        scratch=[
            pltpu.VMEM(w_query.shape, w_query.dtype),
            pltpu.VMEM(out, jnp.float32),
            pltpu.SemaphoreType.DMA((w_query.shape[0] // depth,)),
        ],
        in_specs=[IN_VMEM, IN_PLACE],
    )


def attention_kernel(block_count, first, last, group, *refs):
    seg_q, pos_q, seg_k, pos_k, q_ref = refs[:5]
    blocks = refs[5 : 5 + block_count]
    refs = refs[5 + block_count :]
    if not first:
        acc_in, peak_in, mass_in = refs[:3]
        refs = refs[3:]
    if last:
        out_ref, bias_ref = refs
    else:
        acc_out, peak_out, mass_out, bias_ref = refs
    seen = (seg_q[...] == seg_k[...]) & (pos_k[...] <= pos_q[...])
    bias_ref[...] = jnp.where(seen, 0.0, MASKED)
    rows = q_ref.shape[0]
    width = seg_k.shape[1]
    factor = math.log2(math.e) / math.sqrt(HD)
    for head in range(q_ref.shape[1] // HD):
        if head % group == 0:
            keys = jnp.concatenate([block[head // group, 0] for block in blocks], axis=0)
            values = jnp.concatenate([block[head // group, 1] for block in blocks], axis=0)
            values = jnp.concatenate([values, jnp.ones_like(values)], axis=1)
        cols = slice(head * HD, (head + 1) * HD)
        scores = lax.dot_general(
            q_ref[:, cols], keys, (((1,), (1,)), ((), ())), preferred_element_type=jnp.float32
        )
        scores = scores + bias_ref[...]
        peak = jnp.broadcast_to(jnp.max(scores, axis=1, keepdims=True), (rows, HD))
        if not first:
            old = peak_in[:, cols]
            peak = jnp.maximum(peak, old)
        shift = peak * factor
        weights = jnp.concatenate(
            [
                jnp.exp2(scores[:, at : at + HD] * factor - shift).astype(jnp.bfloat16)
                for at in range(0, width, HD)
            ],
            axis=1,
        )
        total = jnp.dot(weights, values, preferred_element_type=jnp.float32)
        acc = total[:, :HD]
        mass = total[:, HD:]
        if not first:
            keep = jnp.exp2((old - peak) * factor)
            acc = acc + acc_in[:, cols] * keep
            mass = mass + mass_in[:, cols] * keep
        if last:
            out_ref[:, cols] = (acc / mass).astype(jnp.bfloat16)
        else:
            acc_out[:, cols] = acc
            peak_out[:, cols] = peak
            mass_out[:, cols] = mass


def attend(query, query_labels, blocks, key_labels, group, state, last):
    rows, q_cols = query.shape
    seg_k, pos_k = (jnp.concatenate(parts)[None, :] for parts in zip(*key_labels))
    seg_q, pos_q = (part[:, None] for part in query_labels)
    keys = len(blocks) * rows
    args = [seg_q, pos_q, seg_k, pos_k, query]
    args += [block.block if isinstance(block, Farthest) else block for block in blocks]
    first = state is None
    args += [] if first else state
    if last:
        outs = jax.ShapeDtypeStruct((rows, q_cols), jnp.bfloat16)
    else:
        outs = [jax.ShapeDtypeStruct((rows, q_cols), jnp.float32)] * 3
    return call(
        functools.partial(attention_kernel, len(blocks), first, last, group),
        "attend",
        args,
        outs,
        6 * rows * keys * q_cols,
        limit=14,
        scratch=[pltpu.VMEM((rows, keys), jnp.float32)],
        exps=rows * keys * q_cols // HD,
    )


def project_out_kernel(pieces, x_ref, w_ref, own_ref, other_ref, *, piece):
    half = own_ref.shape[0]
    cols = own_ref.shape[1]
    tile = 512
    for start in range(0, cols, tile):
        at = piece * cols + start
        part = jnp.dot(
            x_ref[...], w_ref[:, at : at + tile], preferred_element_type=jnp.float32
        )
        own_ref[:, start : start + tile] = part[:half]
        other_ref[:, start : start + tile] = part[half:].astype(other_ref.dtype)


def project_out(attention, w_out, piece, pieces):
    rows, depth = attention.shape
    cols = w_out.shape[1] // pieces
    outs = [
        jax.ShapeDtypeStruct((rows // 2, cols), jnp.float32),
        jax.ShapeDtypeStruct((rows // 2, cols), jnp.bfloat16),
    ]
    return call(
        functools.partial(project_out_kernel, pieces, piece=piece),
        "project_out",
        (attention, w_out),
        outs,
        2 * rows * depth * cols,
    )


def finish_kernel(piece, tokens_ref, mine, theirs, *refs):
    mixed_hbm, out_hbm, mixed, out, sems = refs[-5:]
    at = slice(piece * mine.shape[1], (piece + 1) * mine.shape[1])
    branch = mine[...] + theirs[...].astype(jnp.float32)
    out[...] = branch.astype(out.dtype)
    out_copy = pltpu.make_async_copy(out, out_hbm.at[:, at], sems.at[0])
    out_copy.start()
    mixed[...] = (tokens_ref[:, at].astype(jnp.float32) + branch).astype(mixed.dtype)
    mixed_copy = pltpu.make_async_copy(mixed, mixed_hbm.at[:, at], sems.at[1])
    mixed_copy.start()
    out_copy.wait()
    mixed_copy.wait()


def finish(tokens, mine, theirs, piece, before):
    outs = [jax.ShapeDtypeStruct(tokens.shape, jnp.bfloat16)] * 2
    return call(
        functools.partial(finish_kernel, piece),
        "finish",
        (tokens, mine, theirs, *before),
        outs,
        2 * tokens.size,
        scratch=[
            pltpu.VMEM(mine.shape, jnp.bfloat16),
            pltpu.VMEM(mine.shape, jnp.bfloat16),
            pltpu.SemaphoreType.DMA((2,)),
        ],
        in_specs=[IN_VMEM] * 3 + [IN_PLACE] * len(before),
        out_specs=IN_PLACE,
        aliases={3 + n: n for n in range(len(before))},
    )


def after(values, *others):
    return lax.optimization_barrier((values, others))[0]


def swap_cores(value):
    return lax.ppermute(value, "kv", [(0, 1), (1, 0)])


class Farthest(typing.NamedTuple):
    block: jax.Array
    first: jax.Array


def cube_exchanges(block, index, core, count):
    half = count // 2
    rows = block.shape[2]
    page = rows // 2

    def exchange(value, bit):
        return lax.ppermute(value, "seq", [(i, i ^ bit) for i in range(count)])

    from_x, from_y, from_z = exchange(block, 1), exchange(block, 2), exchange(block, 4)
    work = yield [(from_x, index ^ 1), (from_y, index ^ 2), (from_z, index ^ 4)]
    from_x, from_y, from_z = after((from_x, from_y, from_z), work)
    from_xy, from_yz, from_xz = exchange(from_y, 1), exchange(from_z, 2), exchange(from_x, 4)
    work = yield [(from_xy, index ^ 3), (from_yz, index ^ 6), (from_xz, index ^ 5)]
    from_xy, from_yz, from_xz = after((from_xy, from_yz, from_xz), work)
    seam_page = lax.dynamic_slice_in_dim(from_xy, (1 - core) * page, page, 2)
    up = jnp.where(
        index % half == half // 2,
        seam_page.reshape(-1, HD),
        from_xy[2:].reshape(-1, HD),
    )
    swapped = {}
    for low in range(half // 2, count, half):
        swapped[low] = (low + half // 2) % count
    pairs = [(i, swapped.get(i, i ^ 4)) for i in range(count)]
    part_x, part_y = exchange(from_yz[:1], 1), exchange(from_xz[1:2], 2)
    part_z = lax.ppermute(up, "seq", pairs)
    first = index % half == 0
    usual = jnp.concatenate([part_x, part_y, part_z.reshape(2, 2, rows, HD)])
    before = part_z.reshape(4, 2, page, HD)
    before = jnp.concatenate([before, before], axis=2)
    yield [(Farthest(jnp.where(first, before, usual), first), index ^ 7)]


def distance_exchanges(block, index, count, reach):
    step = 3
    for start in range(1, reach + 1, step):
        received = []
        for distance in range(start, min(start + step, reach + 1)):
            moved = lax.ppermute(block, "seq", [(i, i + distance) for i in range(count - distance)])
            received.append((moved, index - distance))
        work = yield received
        block = after(block, work)


def shards(tokens, gain, w_query, w_key, w_value, w_out, segment_ids, page_table):
    half_rows = tokens.shape[0]
    block_rows = 2 * half_rows
    count = lax.axis_size("seq")
    index = lax.axis_index("seq")
    core = lax.axis_index("kv")
    reach = min(8, count // 2 - 1)

    other_tokens = swap_cores(tokens)
    normed, own_block = project_kv(tokens, other_tokens, gain, w_key, w_value)

    if count == 2 * (reach + 1) and count // 2 == 8:
        exchanges = cube_exchanges(own_block, index, core, count)
    else:
        exchanges = distance_exchanges(own_block, index, count, reach)
    group = [(own_block, index)] + next(exchanges)

    query = project_query(normed, w_query)

    offsets = jnp.arange(half_rows, dtype=jnp.int32)
    local = jnp.concatenate([core * half_rows + offsets, (1 - core) * half_rows + offsets])

    def labels(source):
        starts = (core * half_rows, (1 - core) * half_rows)
        begin = jnp.maximum(source, 0) * block_rows
        found = [lax.dynamic_slice_in_dim(segment_ids, begin + s, half_rows) for s in starts]
        return jnp.where(source >= 0, jnp.concatenate(found), -1), source * block_rows + local

    def labels_before():
        begin = index * block_rows - half_rows
        found = lax.dynamic_slice_in_dim(segment_ids, jnp.maximum(begin, 0), half_rows)
        nothing = jnp.full((half_rows,), -1, jnp.int32)
        segs = jnp.concatenate([jnp.where(index > 0, found, -1), nothing])
        return segs, jnp.concatenate([begin + offsets, begin + offsets])

    def key_labels(block, source):
        if not isinstance(block, Farthest):
            return labels(source)
        return jax.tree.map(
            lambda before, usual: jnp.where(block.first, before, usual),
            labels_before(),
            labels(source),
        )

    heads = own_block.shape[0]
    pages = own_block.reshape(heads, 2, 2, half_rows, HD).transpose(2, 1, 0, 3, 4)
    own_slot = lax.dynamic_index_in_dim(page_table, core, keepdims=False)
    page_pool = jnp.where(own_slot == 0, pages, pages[::-1])

    groups = query.shape[1] // HD // heads
    state, done = None, query
    while group:
        blocks = [block for block, _ in group]
        keys = [key_labels(block, source) for block, source in group]
        try:
            following = exchanges.send(done)
        except StopIteration:
            following = None
        state = attend(
            query, labels(index), blocks, keys, groups, state, following is None
        )
        group, done = following, (state, page_pool)
    attention = state

    pieces = 2
    parts = [project_out(attention, w_out, piece, pieces) for piece in range(pieces)]
    results = ()
    for piece, (mine, theirs) in enumerate(parts):
        results = finish(tokens, mine, swap_cores(theirs), piece, results)
    mixed, attn_out = results
    return (mixed, attn_out, page_pool)


def solution(mesh):
    in_specs = (
        P(("seq", "kv"), None),
        P(),
        P(None, "kv"),
        P(None, "kv"),
        P(None, "kv"),
        P("kv", None),
        P(),
        P("seq"),
    )
    out_specs = (P(("seq", "kv"), None), P(("seq", "kv"), None), P("seq", None, "kv", None, None))
    return jax.shard_map(shards, mesh=mesh, in_specs=in_specs, out_specs=out_specs, check_vma=False)
```

time: 74.2 us -> 62.2 us (0.84)
  the two profiles are of different devices: /device:TPU:25 before, /device:TPU:0 now
where the time goes in v3:
time: 62.2 us; the launch traced here: 61.9 us
  Pallas kernels  35.3 us (57%)
  starting transfers between devices  14.4 us (23%)
  waiting for transfers between devices  5.82 us (9%)
  other arithmetic  2.5 us (4%)
  local copies, waits for them, and re-layouts  2.04 us (3%)
  between operations  1.89 us (3%)
    pallas_call x9, Pallas kernels, call(): pl.pallas_call(kernel, in_specs=in_specs or [IN_VMEM] * len(args), out_sp...  35.3 us
    ppermute x8, starting transfers between devices, exchange(): return lax.ppermute(value, 'seq', [(i, i ^ bit) for i in range(count)])  11.6 us
    ppermute x8, waiting for transfers between devices, exchange(): return lax.ppermute(value, 'seq', [(i, i ^ bit) for i in range(count)])  4.72 us
    ppermute x1, starting transfers between devices, cube_exchanges(): part_z = lax.ppermute(up, 'seq', pairs)  1.61 us
  transfers between devices with their start and end apart: 12, of which 8 were waited for; matrix products, arithmetic and copies ran while one was open for 7% of the time, Pallas kernels for 38%

profile of v3, /device:TPU:0, one launch (start us, length us, event | category | flops | bytes accessed | tf_op | source)
XLA Modules:
  0.0 61.9 jit_solution(3408361089867774966)
XLA Ops:
  0.6 0.5 collective-permute-start
  1.2 1.2 %fusion.5 = (s32[128]{0:T(128)S(1)}, s32[128]{0:T(128)S(1)}, s32[128]{0:T(128)S(1)}, s32[128]{0:T(128)S(1)}, s32[128]{0:T(128)S(1)}, /*index=5*/s32[128]{0:T(128...) fusion(s32[4096]{0:T(1024)} %param.14, ...), kind=kLoop, calls=%fused_computation.40 | loop fusion | flops 128 | bytes 17477 | tf_op jit(solution)/shard_map/dynamic_slice | solution.py:387
  2.6 0.1 copy.18
  2.7 0.1 copy.19
  3.0 0.6 %collective-permute-done.other_ref = bf16[128,4096]{1,0:T(8,128)(2,1)S(1)} collective-permute-done((bf16[128,4096]{1,0:T(8,128)(2,1)}, bf16[128,4096]{1,0:T(8,128)(2,1)S(1)}, u32[]{:S(2)}, u32[]{:S(2)}) %collective-permute-start) | collective-permute-done | bytes 1048608 | tf_op jit(solution)/shard_map/ppermute | solution.py:310
  3.6 5.9 %project_kv.1 = (bf16[256,4096]{1,0:T(8,128)(2,1)S(1)}, bf16[4,2,256,128]{3,2,1,0:T(8,128)(2,1)}) custom-call(bf16[128,4096]{1,0:T(8,128)(2,1)} %tokens_ref.3, f32[1,4096]{1,0:T(1,128)} %bitcast.35, bf16[4096,512]{1,0:T(8,128)(2,1)} %wk_hbm.1, bf16[4096,512]{1,0:T(8,128)(2,1)} %wv_hbm.1, bf16[128,4096]{1,0:T(8,128)(2,1)S(1)} %collective-permute-done.other_ref), custom_call_target="tpu_custom_call" | custom-call | flops 2147483648 | bytes 13123584 | tf_op jit(solution)/shard_map/project_kv/pallas_call | solution.py:37
  9.5 2.9 %collective-permute-start.1 = (bf16[4,2,256,128]{3,2,1,0:T(8,128)(2,1)}, bf16[4,2,256,128]{3,2,1,0:T(8,128)(2,1)S(1)}, u32[]{:S(2)}, u32[]{:S(2)}) collective-permute-start(bf16[4,2,256,128]{3,2,1,0:T(8,128)(2,1)} %get-tuple-element.26.refs_5_), channel_id=1, source_target_pairs={{0,1},{1,0},{2,3},{3,2},{4,5},{5,4},{6,7},{7,6},{8,9},{9,8},{10,11... | collective-permute-start | bytes 1572872 | tf_op jit(solution)/shard_map/ppermute | solution.py:324
  12.4 1.5 %collective-permute-start.2 = (bf16[4,2,256,128]{3,2,1,0:T(8,128)(2,1)}, bf16[4,2,256,128]{3,2,1,0:T(8,128)(2,1)}, u32[]{:S(2)}, u32[]{:S(2)}) collective-permute-start(bf16[4,2,256,128]{3,2,1,0:T(8,128)(2,1)} %get-tuple-element.26.refs_5_), channel_id=1, source_target_pairs={{0,2},{1,3},{2,0},{3,1},{4,6},{5,7},{6,4},{7,5},{8,10},{9,11},{10,... | collective-permute-start | bytes 1572872 | tf_op jit(solution)/shard_map/ppermute | solution.py:324
  14.0 1.6 %collective-permute-start.3 = (bf16[4,2,256,128]{3,2,1,0:T(8,128)(2,1)}, bf16[4,2,256,128]{3,2,1,0:T(8,128)(2,1)}, u32[]{:S(2)}, u32[]{:S(2)}) collective-permute-start(bf16[4,2,256,128]{3,2,1,0:T(8,128)(2,1)} %get-tuple-element.26.refs_5_), channel_id=1, source_target_pairs={{0,4},{1,5},{2,6},{3,7},{4,0},{5,1},{6,2},{7,3},{8,12},{9,13},{10,... | collective-permute-start | bytes 1572872 | tf_op jit(solution)/shard_map/ppermute | solution.py:324
  15.5 0.0 copy-done.1
  15.5 0.6 dynamic_slice.75
  16.8 1.1 %copy.22 = bf16[4,2,2,128,128]{4,3,0,1,2:T(8,128)(2,1)S(1)} copy(bf16[4,2,2,128,128]{4,3,2,1,0:T(8,128)(2,1)} %bitcast.12) | data formatting | bytes 1048576 | tf_op jit(solution)/shard_map/reshape | solution.py:407
  17.9 6.9 %project_query.1.refs_4_ = bf16[256,2048]{1,0:T(8,128)(2,1)S(1)} custom-call(bf16[256,4096]{1,0:T(8,128)(2,1)S(1)} %get-tuple-element.25.x_ref, bf16[4096,2048]{1,0:T(8,128)(2,1)} %w_hbm.1), custom_call_target="tpu_custom_call" | custom-call | flops 4294967296 | bytes 19922944 | tf_op jit(solution)/shard_map/project_query/pallas_call | solution.py:37
  24.8 0.1 collective-permute-done.1.refs_6_
  24.9 1.6 %collective-permute-done.2.refs_7_ = bf16[4,2,256,128]{3,2,1,0:T(8,128)(2,1)} collective-permute-done((bf16[4,2,256,128]{3,2,1,0:T(8,128)(2,1)}, bf16[4,2,256,128]{3,2,1,0:T(8,128)(2,1)}, u32[]{:S(2)}, u32[]{:S(2)}) %collective-permute-start.2) | collective-permute-done | bytes 524320 | tf_op jit(solution)/shard_map/ppermute | solution.py:324
  26.4 1.2 %collective-permute-done.3.refs_8_ = bf16[4,2,256,128]{3,2,1,0:T(8,128)(2,1)} collective-permute-done((bf16[4,2,256,128]{3,2,1,0:T(8,128)(2,1)}, bf16[4,2,256,128]{3,2,1,0:T(8,128)(2,1)}, u32[]{:S(2)}, u32[]{:S(2)}) %collective-permute-start.3) | collective-permute-done | bytes 524320 | tf_op jit(solution)/shard_map/ppermute | solution.py:324
  27.7 0.5 collective-permute-start.4
  28.2 0.4 collective-permute-start.5
  28.6 1.7 %collective-permute-start.6 = (bf16[4,2,256,128]{3,2,1,0:T(8,128)(2,1)S(1)}, bf16[4,2,256,128]{3,2,1,0:T(8,128)(2,1)S(1)}, u32[]{:S(2)}, u32[]{:S(2)}) collective-permute-start(bf16[4,2,256,128]{3,2,1,0:T(8,128)(2,1)S(1)} %collective-permute-done.1.refs_6_), channel_id=1, source_target_pairs={{0,4},{1,5},{2,6},{3,7},{4,0},{5,1},{6,2},{7,3},{8,12},{9,13},{10,... | collective-permute-start | bytes 1572872 | tf_op jit(solution)/shard_map/ppermute | solution.py:324
  30.3 0.9 %reverse_select_fusion = bf16[2,2,4,128,128]{4,3,2,1,0:T(8,128)(2,1)} fusion(bf16[2,2,4,128,128]{4,3,2,1,0:T(8,128)(2,1)S(1)} %bitcast.32, pred[]{:T(512)} %bitcast.11), kind=kLoop, calls=%fused_computation | loop fusion | flops 262144 | bytes 1048577 | tf_op jit(solution)/shard_map/jit(_where)/select_n | solution.py:409
  31.2 7.8 %attend.3 = (f32[256,2048]{1,0:T(8,128)S(1)}, f32[256,2048]{1,0:T(8,128)S(1)}, f32[256,2048]{1,0:T(8,128)S(1)}) custom-call(s32[256,1]{1,0:T(8,128)S(1)} %broadcast_select_fusion.refs_0_, s32[256,1]{1,0:T(8,128)S(1)} %broadcast_add_fusion.refs_1_, s32[1,1024]{1,0:T(1,128)S(1)} %bitcast.30, s32[1,1024]{1,0:T(1,128)S(1)} %bitcast.31, ...), custom_call_target="tpu_custom_call" | custom-call | flops 3221225472 | bytes 9447424 | tf_op jit(solution)/shard_map/attend/pallas_call | solution.py:37
  39.0 1.4 %collective-permute-done.4.refs_5_ = bf16[4,2,256,128]{3,2,1,0:T(8,128)(2,1)S(1)} collective-permute-done((bf16[4,2,256,128]{3,2,1,0:T(8,128)(2,1)}, bf16[4,2,256,128]{3,2,1,0:T(8,128)(2,1)S(1)}, u32[]{:S(2)}, u32[]{:S(2)}) %collective-permute-start.4) | collective-permute-done | bytes 524320 | tf_op jit(solution)/shard_map/ppermute | solution.py:324
  40.4 0.3 collective-permute-done.5.refs_6_
  40.6 0.2 collective-permute-done.6.refs_7_
  40.9 0.1 bitcast_select_fusion
  41.0 1.6 %collective-permute-start.7 = (bf16[1024,128]{1,0:T(8,128)(2,1)S(1)}, bf16[1024,128]{1,0:T(8,128)(2,1)S(1)}, u32[]{:S(2)}, u32[]{:S(2)}) collective-permute-start(bf16[1024,128]{1,0:T(8,128)(2,1)S(1)} %bitcast_select_fusion), channel_id=1, source_target_pairs={{0,4},{1,5},{2,6},{3,7},{4,8},{5,1},{6,2},{7,3},{8,12},{9,13},{10,... | collective-permute-start | bytes 786440 | tf_op jit(solution)/shard_map/ppermute | solution.py:343
  42.6 1.5 %collective-permute-start.8 = (bf16[1,2,256,128]{3,2,1,0:T(8,128)(2,1)S(1)}, bf16[1,2,256,128]{3,2,1,0:T(8,128)(2,1)S(1)}, u32[]{:S(2)}, u32[]{:S(2)}) collective-permute-start(bf16[1,2,256,128]{3,2,1,0:T(8,128)(2,1)S(1)} %slice.10), channel_id=1, source_target_pairs={{0,1},{1,0},{2,3},{3,2},{4,5},{5,4},{6,7},{7,6},{8,9},{9,8},{10,11... | collective-permute-start | bytes 393224 | tf_op jit(solution)/shard_map/ppermute | solution.py:324
  44.1 0.0 slice-start.2
  44.1 1.5 %collective-permute-start.9 = (bf16[1,2,256,128]{3,2,1,0:T(8,128)(2,1)S(1)}, bf16[1,2,256,128]{3,2,1,0:T(8,128)(2,1)S(1)}, u32[]{:S(2)}, u32[]{:S(2)}) collective-permute-start(bf16[1,2,256,128]{3,2,1,0:T(8,128)(2,1)S(1)} %slice.11), channel_id=1, source_target_pairs={{0,2},{1,3},{2,0},{3,1},{4,6},{5,7},{6,4},{7,5},{8,10},{9,11},{10,... | collective-permute-start | bytes 393224 | tf_op jit(solution)/shard_map/ppermute | solution.py:324
  45.6 5.4 %attend.4 = (f32[256,2048]{1,0:T(8,128)S(1)}, f32[256,2048]{1,0:T(8,128)S(1)}, f32[256,2048]{1,0:T(8,128)S(1)}) custom-call(s32[256,1]{1,0:T(8,128)S(1)} %broadcast_select_fusion.refs_0_, s32[256,1]{1,0:T(8,128)S(1)} %broadcast_add_fusion.refs_1_, s32[1,768]{1,0:T(1,128)S(1)} %broadcast_in_dim.53.refs_2_, s32[1,768]{1,0:T(1,128)S(1)} %broadcast_in_dim.54.refs_3_, ...), custom_call_target="tpu_custom_call" | custom-call | flops 2415919104 | bytes 15212544 | tf_op jit(solution)/shard_map/attend/pallas_call | solution.py:37
  51.1 0.0 collective-permute-done.8
  51.1 0.0 collective-permute-done.9
  51.1 0.0 collective-permute-done.7
  51.1 0.1 maximum_select_fusion.refs_5_
  51.2 0.0 slice-start.3
  51.2 2.5 %attend.5.x_ref = bf16[256,2048]{1,0:T(8,128)(2,1)S(1)} custom-call(s32[256,1]{1,0:T(8,128)S(1)} %broadcast_select_fusion.refs_0_, s32[256,1]{1,0:T(8,128)S(1)} %broadcast_add_fusion.refs_1_, s32[1,256]{1,0:T(1,128)S(1)} %bitcast.29, s32[1,256]{1,0:T(1,128)S(1)} %broadcast_select_fusion.1.refs_3_, bf16[256,2048]{1,0:T(8,128)(2,1)S(1)} %project_query.1.refs_4_, ...), custom_call_target="tpu_custom_call" | custom-call | flops 805306368 | bytes 8916992 | tf_op jit(solution)/shard_map/attend/pallas_call | solution.py:37
  53.8 0.0 slice-done
  53.8 0.0 slice-done.1
  53.8 0.0 slice-done.2
  53.8 2.3 %project_out.3 = (f32[128,2048]{1,0:T(8,128)S(1)}, bf16[128,2048]{1,0:T(8,128)(2,1)S(1)}) custom-call(bf16[256,2048]{1,0:T(8,128)(2,1)S(1)} %attend.5.x_ref, bf16[2048,4096]{1,0:T(8,128)(2,1)S(1)} %bitcast.28), custom_call_target="tpu_custom_call" | custom-call | flops 2147483648 | bytes 19398656 | tf_op jit(solution)/shard_map/project_out/pallas_call | solution.py:37
  56.2 0.0 copy-start
  56.2 0.1 collective-permute-start.11
  56.2 2.3 %project_out.2 = (f32[128,2048]{1,0:T(8,128)S(1)}, bf16[128,2048]{1,0:T(8,128)(2,1)S(1)}) custom-call(bf16[256,2048]{1,0:T(8,128)(2,1)S(1)} %attend.5.x_ref, bf16[2048,4096]{1,0:T(8,128)(2,1)S(1)} %bitcast.28), custom_call_target="tpu_custom_call" | custom-call | flops 2147483648 | bytes 19398656 | tf_op jit(solution)/shard_map/project_out/pallas_call | solution.py:37
  58.6 0.6 collective-permute-start.10
  59.1 0.0 collective-permute-done.11.theirs
  59.1 1.1 %finish.2 = (bf16[128,4096]{1,0:T(8,128)(2,1)}, bf16[128,4096]{1,0:T(8,128)(2,1)}) custom-call(bf16[128,4096]{1,0:T(8,128)(2,1)S(1)} %copy-done, f32[128,2048]{1,0:T(8,128)S(1)} %get-tuple-element.41.mine, bf16[128,2048]{1,0:T(8,128)(2,1)S(1)} %collective-permute-done.11.theirs), custom_call_target="tpu_custom_call" | custom-call | flops 1048576 | bytes 4718592 | tf_op jit(solution)/shard_map/finish/pallas_call | solution.py:37
  60.2 0.4 collective-permute-done.10.theirs
  60.7 1.1 %finish.3 = (bf16[128,4096]{1,0:T(8,128)(2,1)}, bf16[128,4096]{1,0:T(8,128)(2,1)}) custom-call(bf16[128,4096]{1,0:T(8,128)(2,1)S(1)} %copy-done, f32[128,2048]{1,0:T(8,128)S(1)} %get-tuple-element.39.mine, bf16[128,2048]{1,0:T(8,128)(2,1)S(1)} %collective-permute-done.10.theirs, ...), custom_call_target="tpu_custom_call", output_to_operand_aliasing={{0}: (3, {}), {1}: (4, {})} | custom-call | flops 1048576 | bytes 6815744 | tf_op jit(solution)/shard_map/finish/pallas_call | solution.py:37
  (32 shorter events, 0.2 us)
Async XLA Ops:
  0.6 3.0 %collective-permute-start = (bf16[128,4096]{1,0:T(8,128)(2,1)}, bf16[128,4096]{1,0:T(8,128)(2,1)S(1)}, u32[]{:S(2)}, u32[]{:S(2)}) collective-permute-start(bf16[128,4096]{1,0:T(8,128)(2,1)} %tokens_ref.3), channel_id=1, source_target_pairs={{0,16},{16,0},{1,17},{17,1},{2,18},{18,2},{3,19},{19,3},{4,20},{20... | collective-permute-start | bytes 3145736 | tf_op jit(solution)/shard_map/ppermute | solution.py:310
  3.6 11.9 %copy-start.1 = (s32[2]{0:T(128)S(1)}, s32[2]{0:T(128)}, u32[]{:S(2)}) copy-start(s32[2]{0:T(128)} %param.15) | copy-start | bytes 28
  9.5 15.4 %collective-permute-start.1 = (bf16[4,2,256,128]{3,2,1,0:T(8,128)(2,1)}, bf16[4,2,256,128]{3,2,1,0:T(8,128)(2,1)S(1)}, u32[]{:S(2)}, u32[]{:S(2)}) collective-permute-start(bf16[4,2,256,128]{3,2,1,0:T(8,128)(2,1)} %get-tuple-element.26.refs_5_), channel_id=1, source_target_pairs={{0,1},{1,0},{2,3},{3,2},{4,5},{5,4},{6,7},{7,6},{8,9},{9,8},{10,11... | collective-permute-start | bytes 1572872 | tf_op jit(solution)/shard_map/ppermute | solution.py:324
  12.4 14.0 %collective-permute-start.2 = (bf16[4,2,256,128]{3,2,1,0:T(8,128)(2,1)}, bf16[4,2,256,128]{3,2,1,0:T(8,128)(2,1)}, u32[]{:S(2)}, u32[]{:S(2)}) collective-permute-start(bf16[4,2,256,128]{3,2,1,0:T(8,128)(2,1)} %get-tuple-element.26.refs_5_), channel_id=1, source_target_pairs={{0,2},{1,3},{2,0},{3,1},{4,6},{5,7},{6,4},{7,5},{8,10},{9,11},{10,... | collective-permute-start | bytes 1572872 | tf_op jit(solution)/shard_map/ppermute | solution.py:324
  14.0 13.7 %collective-permute-start.3 = (bf16[4,2,256,128]{3,2,1,0:T(8,128)(2,1)}, bf16[4,2,256,128]{3,2,1,0:T(8,128)(2,1)}, u32[]{:S(2)}, u32[]{:S(2)}) collective-permute-start(bf16[4,2,256,128]{3,2,1,0:T(8,128)(2,1)} %get-tuple-element.26.refs_5_), channel_id=1, source_target_pairs={{0,4},{1,5},{2,6},{3,7},{4,0},{5,1},{6,2},{7,3},{8,12},{9,13},{10,... | collective-permute-start | bytes 1572872 | tf_op jit(solution)/shard_map/ppermute | solution.py:324
  27.7 12.7 %collective-permute-start.4 = (bf16[4,2,256,128]{3,2,1,0:T(8,128)(2,1)}, bf16[4,2,256,128]{3,2,1,0:T(8,128)(2,1)S(1)}, u32[]{:S(2)}, u32[]{:S(2)}) collective-permute-start(bf16[4,2,256,128]{3,2,1,0:T(8,128)(2,1)} %collective-permute-done.2.refs_7_), channel_id=1, source_target_pairs={{0,1},{1,0},{2,3},{3,2},{4,5},{5,4},{6,7},{7,6},{8,9},{9,8},{10,11... | collective-permute-start | bytes 1572872 | tf_op jit(solution)/shard_map/ppermute | solution.py:324
  28.2 12.4 %collective-permute-start.5 = (bf16[4,2,256,128]{3,2,1,0:T(8,128)(2,1)}, bf16[4,2,256,128]{3,2,1,0:T(8,128)(2,1)S(1)}, u32[]{:S(2)}, u32[]{:S(2)}) collective-permute-start(bf16[4,2,256,128]{3,2,1,0:T(8,128)(2,1)} %collective-permute-done.3.refs_8_), channel_id=1, source_target_pairs={{0,2},{1,3},{2,0},{3,1},{4,6},{5,7},{6,4},{7,5},{8,10},{9,11},{10,... | collective-permute-start | bytes 1572872 | tf_op jit(solution)/shard_map/ppermute | solution.py:324
  28.6 12.3 %collective-permute-start.6 = (bf16[4,2,256,128]{3,2,1,0:T(8,128)(2,1)S(1)}, bf16[4,2,256,128]{3,2,1,0:T(8,128)(2,1)S(1)}, u32[]{:S(2)}, u32[]{:S(2)}) collective-permute-start(bf16[4,2,256,128]{3,2,1,0:T(8,128)(2,1)S(1)} %collective-permute-done.1.refs_6_), channel_id=1, source_target_pairs={{0,4},{1,5},{2,6},{3,7},{4,0},{5,1},{6,2},{7,3},{8,12},{9,13},{10,... | collective-permute-start | bytes 1572872 | tf_op jit(solution)/shard_map/ppermute | solution.py:324
  31.2 22.6 %slice-start = ((s8[16777216]{0:T(1024)(128)(4,1)}), s8[4194304]{0:T(1024)(128)(4,1)S(1)}, s32[]{:S(2)}) async-start(s8[16777216]{0:T(1024)(128)(4,1)} %bitcast.27), calls=%async_computation | async-start | bytes 8388608
  31.2 22.6 %slice-start.1 = ((s8[16777216]{0:T(1024)(128)(4,1)}), s8[4194304]{0:T(1024)(128)(4,1)S(1)}, s32[]{:S(2)}) async-start(s8[16777216]{0:T(1024)(128)(4,1)} %bitcast.27), calls=%async_computation.1 | async-start | bytes 8388608
  41.0 10.1 %collective-permute-start.7 = (bf16[1024,128]{1,0:T(8,128)(2,1)S(1)}, bf16[1024,128]{1,0:T(8,128)(2,1)S(1)}, u32[]{:S(2)}, u32[]{:S(2)}) collective-permute-start(bf16[1024,128]{1,0:T(8,128)(2,1)S(1)} %bitcast_select_fusion), channel_id=1, source_target_pairs={{0,4},{1,5},{2,6},{3,7},{4,8},{5,1},{6,2},{7,3},{8,12},{9,13},{10,... | collective-permute-start | bytes 786440 | tf_op jit(solution)/shard_map/ppermute | solution.py:343
  42.6 8.4 %collective-permute-start.8 = (bf16[1,2,256,128]{3,2,1,0:T(8,128)(2,1)S(1)}, bf16[1,2,256,128]{3,2,1,0:T(8,128)(2,1)S(1)}, u32[]{:S(2)}, u32[]{:S(2)}) collective-permute-start(bf16[1,2,256,128]{3,2,1,0:T(8,128)(2,1)S(1)} %slice.10), channel_id=1, source_target_pairs={{0,1},{1,0},{2,3},{3,2},{4,5},{5,4},{6,7},{7,6},{8,9},{9,8},{10,11... | collective-permute-start | bytes 393224 | tf_op jit(solution)/shard_map/ppermute | solution.py:324
  44.1 9.7 %slice-start.2 = ((s8[16777216]{0:T(1024)(128)(4,1)}), s8[4194304]{0:T(1024)(128)(4,1)S(1)}, s32[]{:S(2)}) async-start(s8[16777216]{0:T(1024)(128)(4,1)} %bitcast.27), calls=%async_computation.2 | async-start | bytes 8388608
  44.1 6.9 %collective-permute-start.9 = (bf16[1,2,256,128]{3,2,1,0:T(8,128)(2,1)S(1)}, bf16[1,2,256,128]{3,2,1,0:T(8,128)(2,1)S(1)}, u32[]{:S(2)}, u32[]{:S(2)}) collective-permute-start(bf16[1,2,256,128]{3,2,1,0:T(8,128)(2,1)S(1)} %slice.11), channel_id=1, source_target_pairs={{0,2},{1,3},{2,0},{3,1},{4,6},{5,7},{6,4},{7,5},{8,10},{9,11},{10,... | collective-permute-start | bytes 393224 | tf_op jit(solution)/shard_map/ppermute | solution.py:324
  51.2 2.6 %slice-start.3 = ((s8[16777216]{0:T(1024)(128)(4,1)}), s8[4194304]{0:T(1024)(128)(4,1)S(1)}, s32[]{:S(2)}) async-start(s8[16777216]{0:T(1024)(128)(4,1)} %bitcast.27), calls=%async_computation.3 | async-start | bytes 8388608
  56.2 3.0 %copy-start = (bf16[128,4096]{1,0:T(8,128)(2,1)S(1)}, bf16[128,4096]{1,0:T(8,128)(2,1)}, u32[]{:S(2)}) copy-start(bf16[128,4096]{1,0:T(8,128)(2,1)} %tokens_ref.3) | copy-start | bytes 3145732
  56.2 3.0 %collective-permute-start.11 = (bf16[128,2048]{1,0:T(8,128)(2,1)S(1)}, bf16[128,2048]{1,0:T(8,128)(2,1)S(1)}, u32[]{:S(2)}, u32[]{:S(2)}) collective-permute-start(bf16[128,2048]{1,0:T(8,128)(2,1)S(1)} %get-tuple-element.42), channel_id=1, source_target_pairs={{0,16},{16,0},{1,17},{17,1},{2,18},{18,2},{3,19},{19,3},{4,20},{20... | collective-permute-start | bytes 1572872 | tf_op jit(solution)/shard_map/ppermute | solution.py:310
  58.6 2.1 %collective-permute-start.10 = (bf16[128,2048]{1,0:T(8,128)(2,1)S(1)}, bf16[128,2048]{1,0:T(8,128)(2,1)S(1)}, u32[]{:S(2)}, u32[]{:S(2)}) collective-permute-start(bf16[128,2048]{1,0:T(8,128)(2,1)S(1)} %get-tuple-element.40), channel_id=1, source_target_pairs={{0,16},{16,0},{1,17},{17,1},{2,18},{18,2},{3,19},{19,3},{4,20},{20... | collective-permute-start | bytes 1572872 | tf_op jit(solution)/shard_map/ppermute | solution.py:310

commit v4 on v3

--- a/solution.py
+++ b/solution.py
@@ -52,13 +52,13 @@
     )
 
 
-def norm_rows(x_ref, gain_ref, out_ref, first):
+def norm_rows(x_ref, gain_ref, out_ref):
     step = 16
     for start in range(0, x_ref.shape[0], step):
         wide = x_ref[start : start + step, :].astype(jnp.float32)
         mean = jnp.mean(wide * wide, axis=1, keepdims=True)
         normed = wide * lax.rsqrt(mean + NORM_EPS) * gain_ref[...]
-        out_ref[first + start : first + start + step, :] = normed.astype(jnp.bfloat16)
+        out_ref[start : start + step, :] = normed.astype(jnp.bfloat16)
 
 
 def stream(copies, ahead, use):
@@ -74,52 +74,57 @@
         use(n)
 
 
-def project_kv_kernel(
-    tokens_hbm, gain_hbm, wk_hbm, wv_hbm, other_ref, normed_ref, kv_ref,
-    x_ref, gain_ref, wk_ref, wv_ref, sems,
+def stage_kernel(
+    tokens_hbm, gain_hbm, wk_hbm, wv_hbm, normed_ref, gain_ref, wk_ref, wv_ref, x_ref, sems
 ):
-    half = x_ref.shape[0]
     pairs = ((tokens_hbm, x_ref), (gain_hbm, gain_ref), (wk_hbm, wk_ref), (wv_hbm, wv_ref))
     copies = [pltpu.make_async_copy(*pair, sems.at[n]) for n, pair in enumerate(pairs)]
     for copy in copies:
         copy.start()
+    copies[0].wait()
     copies[1].wait()
-    norm_rows(other_ref, gain_ref, normed_ref, half)
-    copies[0].wait()
-    norm_rows(x_ref, gain_ref, normed_ref, 0)
-    for n, ref in enumerate((wk_ref, wv_ref)):
-        copies[2 + n].wait()
-        part = jnp.dot(normed_ref[...], ref[...], preferred_element_type=jnp.float32)
-        for head in range(kv_ref.shape[0]):
-            kv_ref[head, n] = part[:, head * HD : (head + 1) * HD].astype(kv_ref.dtype)
-
-
-def project_kv(tokens, other_tokens, gain, w_key, w_value):
-    half, width = tokens.shape
+    norm_rows(x_ref, gain_ref, normed_ref)
+    copies[2].wait()
+    copies[3].wait()
+
+
+def stage(tokens, gain, w_key, w_value):
+    gain = gain[None, :]
+    return call(
+        stage_kernel,
+        "stage",
+        (tokens, gain, w_key, w_value),
+        [jax.ShapeDtypeStruct(a.shape, a.dtype) for a in (tokens, gain, w_key, w_value)],
+        4 * tokens.size,
+        scratch=[pltpu.VMEM(tokens.shape, tokens.dtype), pltpu.SemaphoreType.DMA((4,))],
+        in_specs=[IN_PLACE] * 4,
+    )
+
+
+def project_kv_kernel(own_ref, other_ref, gain_ref, wk_ref, wv_ref, normed_ref, kv_ref):
+    norm_rows(other_ref, gain_ref, normed_ref)
+    rows = jnp.concatenate([own_ref[...], normed_ref[...]], axis=0)
+    for head in range(kv_ref.shape[0]):
+        cols = slice(head * HD, (head + 1) * HD)
+        weights = jnp.concatenate([wk_ref[:, cols], wv_ref[:, cols]], axis=1)
+        pair = jnp.dot(rows, weights, preferred_element_type=jnp.float32).astype(jnp.bfloat16)
+        kv_ref[head, 0] = pair[:, :HD]
+        kv_ref[head, 1] = pair[:, HD:]
+
+
+def project_kv(normed, other_tokens, gain, w_key, w_value):
+    half, width = normed.shape
     heads = w_key.shape[1] // HD
     outs = [
-        jax.ShapeDtypeStruct((2 * half, width), jnp.bfloat16),
+        jax.ShapeDtypeStruct((half, width), jnp.bfloat16),
         jax.ShapeDtypeStruct((heads, 2, 2 * half, HD), jnp.bfloat16),
     ]
-    return call(
-        project_kv_kernel,
-        "project_kv",
-        (tokens, gain[None, :], w_key, w_value, other_tokens),
-        outs,
-        8 * half * width * heads * HD,
-        limit=14,
-        scratch=[
-            pltpu.VMEM(tokens.shape, tokens.dtype),
-            pltpu.VMEM((1, width), jnp.float32),
-            pltpu.VMEM(w_key.shape, w_key.dtype),
-            pltpu.VMEM(w_value.shape, w_value.dtype),
-            pltpu.SemaphoreType.DMA((4,)),
-        ],
-        in_specs=[IN_PLACE] * 4 + [IN_VMEM],
-    )
-
-
-def project_query_kernel(depth, x_ref, w_hbm, out_ref, w_ref, acc_ref, sems):
+    flops = 8 * half * width * heads * HD
+    args = (normed, other_tokens, gain, w_key, w_value)
+    return call(project_kv_kernel, "project_kv", args, outs, flops)
+
+
+def project_query_kernel(depth, own_ref, other_ref, w_hbm, out_ref, w_ref, acc_ref, sems):
     chunks = w_ref.shape[0] // depth
     copies = []
     for n in range(chunks):
@@ -128,12 +133,11 @@
 
     def use(n):
         rows = slice(n * depth, (n + 1) * depth)
+        x = jnp.concatenate([own_ref[:, rows], other_ref[:, rows]], axis=0)
         tile = 512
         for start in range(0, out_ref.shape[1], tile):
             cols = slice(start, start + tile)
-            part = jnp.dot(
-                x_ref[:, rows], w_ref[rows, cols], preferred_element_type=jnp.float32
-            )
+            part = jnp.dot(x, w_ref[rows, cols], preferred_element_type=jnp.float32)
             if n:
                 part = part + acc_ref[:, cols]
             if n < chunks - 1:
@@ -144,21 +148,21 @@
     stream(copies, 3, use)
 
 
-def project_query(normed, w_query, depth=512):
-    out = (normed.shape[0], w_query.shape[1])
+def project_query(own, other, w_query, depth=512):
+    out = (2 * own.shape[0], w_query.shape[1])
     return call(
         functools.partial(project_query_kernel, depth),
         "project_query",
-        (normed, w_query),
+        (own, other, w_query),
         jax.ShapeDtypeStruct(out, jnp.bfloat16),
-        2 * normed.shape[0] * w_query.size,
+        4 * own.shape[0] * w_query.size,
         limit=22,
         scratch=[
             pltpu.VMEM(w_query.shape, w_query.dtype),
             pltpu.VMEM(out, jnp.float32),
             pltpu.SemaphoreType.DMA((w_query.shape[0] // depth,)),
         ],
-        in_specs=[IN_VMEM, IN_PLACE],
+        in_specs=[IN_VMEM, IN_VMEM, IN_PLACE],
     )
 
 
@@ -178,41 +182,63 @@
     rows = q_ref.shape[0]
     width = seg_k.shape[1]
     factor = math.log2(math.e) / math.sqrt(HD)
-    for head in range(q_ref.shape[1] // HD):
-        if head % group == 0:
-            keys = jnp.concatenate([block[head // group, 0] for block in blocks], axis=0)
-            values = jnp.concatenate([block[head // group, 1] for block in blocks], axis=0)
-            values = jnp.concatenate([values, jnp.ones_like(values)], axis=1)
-        cols = slice(head * HD, (head + 1) * HD)
+    heads = q_ref.shape[1] // HD
+    cols = [slice(head * HD, (head + 1) * HD) for head in range(heads)]
+    pairs = {}
+
+    def key_values(head):
+        which = head // group
+        if which not in pairs:
+            keys = jnp.concatenate([block[which, 0] for block in blocks], axis=0)
+            values = jnp.concatenate([block[which, 1] for block in blocks], axis=0)
+            pairs[which] = keys, jnp.concatenate([values, jnp.ones_like(values)], axis=1)
+        return pairs[which]
+
+    def score(head):
+        keys = key_values(head)[0]
         scores = lax.dot_general(
-            q_ref[:, cols], keys, (((1,), (1,)), ((), ())), preferred_element_type=jnp.float32
+            q_ref[:, cols[head]], keys, (((1,), (1,)), ((), ())), preferred_element_type=jnp.float32
         )
-        scores = scores + bias_ref[...]
+        return scores + bias_ref[...]
+
+    def weigh(head, scores):
         peak = jnp.broadcast_to(jnp.max(scores, axis=1, keepdims=True), (rows, HD))
         if not first:
-            old = peak_in[:, cols]
-            peak = jnp.maximum(peak, old)
+            peak = jnp.maximum(peak, peak_in[:, cols[head]])
         shift = peak * factor
-        weights = jnp.concatenate(
-            [
-                jnp.exp2(scores[:, at : at + HD] * factor - shift).astype(jnp.bfloat16)
-                for at in range(0, width, HD)
-            ],
-            axis=1,
-        )
-        total = jnp.dot(weights, values, preferred_element_type=jnp.float32)
+        weights = [
+            jnp.exp2(scores[:, at : at + HD] * factor - shift).astype(jnp.bfloat16)
+            for at in range(0, width, HD)
+        ]
+        return peak, jnp.concatenate(weights, axis=1)
+
+    def add_up(head, peak, weights):
+        total = jnp.dot(weights, key_values(head)[1], preferred_element_type=jnp.float32)
         acc = total[:, :HD]
         mass = total[:, HD:]
         if not first:
-            keep = jnp.exp2((old - peak) * factor)
-            acc = acc + acc_in[:, cols] * keep
-            mass = mass + mass_in[:, cols] * keep
+            keep = jnp.exp2((peak_in[:, cols[head]] - peak) * factor)
+            acc = acc + acc_in[:, cols[head]] * keep
+            mass = mass + mass_in[:, cols[head]] * keep
         if last:
-            out_ref[:, cols] = (acc / mass).astype(jnp.bfloat16)
+            out_ref[:, cols[head]] = (acc / mass).astype(jnp.bfloat16)
         else:
-            acc_out[:, cols] = acc
-            peak_out[:, cols] = peak
-            mass_out[:, cols] = mass
+            acc_out[:, cols[head]] = acc
+            peak_out[:, cols[head]] = peak
+            mass_out[:, cols[head]] = mass
+
+    if last:
+        for start in range(0, heads, 4):
+            many = range(start, start + 4)
+            scores = [score(head) for head in many]
+            weighed = [weigh(head, scores[head - start]) for head in many]
+            for head in many:
+                add_up(head, *weighed[head - start])
+    else:
+        ahead = score(0)
+        for head in range(heads):
+            scores, ahead = ahead, score(head + 1) if head + 1 < heads else None
+            add_up(head, *weigh(head, scores))
 
 
 def attend(query, query_labels, blocks, key_labels, group, state, last):
@@ -240,65 +266,62 @@
     )
 
 
-def project_out_kernel(pieces, x_ref, w_ref, own_ref, other_ref, *, piece):
-    half = own_ref.shape[0]
-    cols = own_ref.shape[1]
+def project_out_kernel(first, x_ref, w_ref, own_ref, other_ref):
+    half, cols = own_ref.shape
     tile = 512
     for start in range(0, cols, tile):
-        at = piece * cols + start
-        part = jnp.dot(
-            x_ref[...], w_ref[:, at : at + tile], preferred_element_type=jnp.float32
-        )
+        weights = w_ref[:, first + start : first + start + tile]
+        part = jnp.dot(x_ref[...], weights, preferred_element_type=jnp.float32)
         own_ref[:, start : start + tile] = part[:half]
         other_ref[:, start : start + tile] = part[half:].astype(other_ref.dtype)
 
 
-def project_out(attention, w_out, piece, pieces):
+def project_out(attention, w_out, first, cols):
     rows, depth = attention.shape
-    cols = w_out.shape[1] // pieces
     outs = [
         jax.ShapeDtypeStruct((rows // 2, cols), jnp.float32),
         jax.ShapeDtypeStruct((rows // 2, cols), jnp.bfloat16),
     ]
+    kernel = functools.partial(project_out_kernel, first)
+    return call(kernel, "project_out", (attention, w_out), outs, 2 * rows * depth * cols)
+
+
+def finish_kernel(parts, tokens_ref, *refs):
+    mixed_hbm, out_hbm, mixed, out, sems = refs[2 * parts :]
+    copies = []
+    first = 0
+    for part in range(parts):
+        mine, theirs = refs[2 * part : 2 * part + 2]
+        tile = 1024
+        for start in range(0, mine.shape[1], tile):
+            cols = slice(start, start + tile)
+            at = slice(first + start, first + start + tile)
+            branch = mine[:, cols] + theirs[:, cols].astype(jnp.float32)
+            out[:, at] = branch.astype(out.dtype)
+            mixed[:, at] = (tokens_ref[:, at].astype(jnp.float32) + branch).astype(mixed.dtype)
+            for here, there in ((out, out_hbm), (mixed, mixed_hbm)):
+                sem = sems.at[len(copies)]
+                copies.append(pltpu.make_async_copy(here.at[:, at], there.at[:, at], sem))
+                copies[-1].start()
+        first += mine.shape[1]
+    for copy in copies:
+        copy.wait()
+
+
+def finish(tokens, parts):
+    args = [tokens] + [array for part in parts for array in part]
     return call(
-        functools.partial(project_out_kernel, pieces, piece=piece),
-        "project_out",
-        (attention, w_out),
-        outs,
-        2 * rows * depth * cols,
-    )
-
-
-def finish_kernel(piece, tokens_ref, mine, theirs, *refs):
-    mixed_hbm, out_hbm, mixed, out, sems = refs[-5:]
-    at = slice(piece * mine.shape[1], (piece + 1) * mine.shape[1])
-    branch = mine[...] + theirs[...].astype(jnp.float32)
-    out[...] = branch.astype(out.dtype)
-    out_copy = pltpu.make_async_copy(out, out_hbm.at[:, at], sems.at[0])
-    out_copy.start()
-    mixed[...] = (tokens_ref[:, at].astype(jnp.float32) + branch).astype(mixed.dtype)
-    mixed_copy = pltpu.make_async_copy(mixed, mixed_hbm.at[:, at], sems.at[1])
-    mixed_copy.start()
-    out_copy.wait()
-    mixed_copy.wait()
-
-
-def finish(tokens, mine, theirs, piece, before):
-    outs = [jax.ShapeDtypeStruct(tokens.shape, jnp.bfloat16)] * 2
-    return call(
-        functools.partial(finish_kernel, piece),
+        functools.partial(finish_kernel, len(parts)),
         "finish",
-        (tokens, mine, theirs, *before),
-        outs,
+        args,
+        [jax.ShapeDtypeStruct(tokens.shape, jnp.bfloat16)] * 2,
         2 * tokens.size,
         scratch=[
-            pltpu.VMEM(mine.shape, jnp.bfloat16),
-            pltpu.VMEM(mine.shape, jnp.bfloat16),
-            pltpu.SemaphoreType.DMA((2,)),
+            pltpu.VMEM(tokens.shape, jnp.bfloat16),
+            pltpu.VMEM(tokens.shape, jnp.bfloat16),
+            pltpu.SemaphoreType.DMA((tokens.shape[1] // 512,)),
         ],
-        in_specs=[IN_VMEM] * 3 + [IN_PLACE] * len(before),
         out_specs=IN_PLACE,
-        aliases={3 + n: n for n in range(len(before))},
     )
 
 
@@ -325,10 +348,10 @@
 
     from_x, from_y, from_z = exchange(block, 1), exchange(block, 2), exchange(block, 4)
     work = yield [(from_x, index ^ 1), (from_y, index ^ 2), (from_z, index ^ 4)]
-    from_x, from_y, from_z = after((from_x, from_y, from_z), work)
-    from_xy, from_yz, from_xz = exchange(from_y, 1), exchange(from_z, 2), exchange(from_x, 4)
+    from_x, from_y, from_z = (after(value, work) for value in (from_x, from_y, from_z))
+    from_xz, from_xy, from_yz = exchange(from_x, 4), exchange(from_y, 1), exchange(from_z, 2)
     work = yield [(from_xy, index ^ 3), (from_yz, index ^ 6), (from_xz, index ^ 5)]
-    from_xy, from_yz, from_xz = after((from_xy, from_yz, from_xz), work)
+    from_xy, from_yz, from_xz = (after(value, work) for value in (from_xy, from_yz, from_xz))
     seam_page = lax.dynamic_slice_in_dim(from_xy, (1 - core) * page, page, 2)
     up = jnp.where(
         index % half == half // 2,
@@ -368,7 +391,11 @@
     reach = min(8, count // 2 - 1)
 
     other_tokens = swap_cores(tokens)
-    normed, own_block = project_kv(tokens, other_tokens, gain, w_key, w_value)
+    normed, staged_gain, staged_key, staged_value = stage(tokens, gain, w_key, w_value)
+    other_normed, own_block = project_kv(
+        normed, other_tokens, staged_gain, staged_key, staged_value
+    )
+    page_table, index, core = after((page_table, index, core), own_block)
 
     if count == 2 * (reach + 1) and count // 2 == 8:
         exchanges = cube_exchanges(own_block, index, core, count)
@@ -376,7 +403,7 @@
         exchanges = distance_exchanges(own_block, index, count, reach)
     group = [(own_block, index)] + next(exchanges)
 
-    query = project_query(normed, w_query)
+    query = project_query(normed, other_normed, w_query)
 
     offsets = jnp.arange(half_rows, dtype=jnp.int32)
     local = jnp.concatenate([core * half_rows + offsets, (1 - core) * half_rows + offsets])
@@ -423,12 +450,13 @@
         group, done = following, (state, page_pool)
     attention = state
 
-    pieces = 2
-    parts = [project_out(attention, w_out, piece, pieces) for piece in range(pieces)]
-    results = ()
-    for piece, (mine, theirs) in enumerate(parts):
-        results = finish(tokens, mine, swap_cores(theirs), piece, results)
-    mixed, attn_out = results
+    width = w_out.shape[1]
+    cuts = [0, width * 3 // 4, width]
+    parts = []
+    for first, end in zip(cuts, cuts[1:]):
+        mine, theirs = project_out(attention, w_out, first, end - first)
+        parts.append((mine, swap_cores(theirs)))
+    mixed, attn_out = finish(tokens, parts)
     return (mixed, attn_out, page_pool)
 
 

time: 62.2 us -> 58.7 us (0.944)
  waiting for transfers between devices: 5.82 us -> 4.59 us
  Pallas kernels: 35.3 us -> 34.2 us
  other arithmetic: 2.5 us -> 1.45 us
  starting transfers between devices: 14.4 us -> 13.5 us
  local copies, waits for them, and re-layouts: 2.04 us -> 2.85 us
    ppermute x8, waiting for transfers between devices: 4.72 us -> 3.05 us  [exchange(): return lax.ppermute(value, 'seq', [(i, i ^ bit) for i in range(count)])]
    dynamic_slice x1, other arithmetic: 1.22 us -> 0.14 us  [labels(): lax.dynamic_slice_in_dim(segment_ids, begin + s, half_rows)]
    pallas_call x9, Pallas kernels: 35.3 us -> 34.2 us  [call(): pl.pallas_call(kernel, in_specs=in_specs or [IN_VMEM] * len(args), out_sp...]
    ppermute x1, starting transfers between devices: 1.61 us -> 0.8 us  [cube_exchanges(): part_z = lax.ppermute(up, 'seq', pairs)]
    unnamed x12 -> x18, local copies, waits for them, and re-layouts: 0.03 us -> 0.84 us
  transfers between devices with their start and end apart: 12 -> 12, of which waited for: 8 -> 5; matrix products, arithmetic and copies ran while one was open for 7% -> 6% of each run, Pallas kernels for 38% -> 42%
where the time goes in v4:
time: 58.7 us; the launch traced here: 58.5 us
  Pallas kernels  34.2 us (58%)
  starting transfers between devices  13.5 us (23%)
  waiting for transfers between devices  4.59 us (8%)
  local copies, waits for them, and re-layouts  2.85 us (5%)
  between operations  1.85 us (3%)
  other arithmetic  1.45 us (2%)
    pallas_call x9, Pallas kernels, call(): pl.pallas_call(kernel, in_specs=in_specs or [IN_VMEM] * len(args), out_sp...  34.2 us
    ppermute x8, starting transfers between devices, exchange(): return lax.ppermute(value, 'seq', [(i, i ^ bit) for i in range(count)])  11.6 us
    ppermute x8, waiting for transfers between devices, exchange(): return lax.ppermute(value, 'seq', [(i, i ^ bit) for i in range(count)])  3.05 us
  transfers between devices with their start and end apart: 12, of which 5 were waited for; matrix products, arithmetic and copies ran while one was open for 6% of the time, Pallas kernels for 42%

profile of v4, /device:TPU:0, one launch (start us, length us, event | category | flops | bytes accessed | tf_op | source)
XLA Modules:
  0.0 58.5 jit_solution(6023433166092123353)
XLA Ops:
  0.6 0.5 collective-permute-start
  1.1 3.8 %stage.1 = (bf16[128,4096]{1,0:T(8,128)(2,1)S(1)}, f32[1,4096]{1,0:T(1,128)S(1)}, bf16[4096,512]{1,0:T(8,128)(2,1)S(1)}, bf16[4096,512]{1,0:T(8,128)(2,1)S(1)}) custom-call(bf16[128,4096]{1,0:T(8,128)(2,1)} %tokens_ref.1, f32[1,4096]{1,0:T(1,128)} %bitcast.36, bf16[4096,512]{1,0:T(8,128)(2,1)} %wk_hbm.1, bf16[4096,512]{1,0:T(8,128)(2,1)} %wv_hbm.1), custom_call_target="tpu_custom_call" | custom-call | flops 2097152 | bytes 18907136 | tf_op jit(solution)/shard_map/stage/pallas_call | solution.py:37
  5.0 0.0 collective-permute-done.other_ref
  5.0 0.0 copy-start.3
  5.0 2.6 %project_kv.1 = (bf16[128,4096]{1,0:T(8,128)(2,1)S(1)}, bf16[4,2,256,128]{3,2,1,0:T(8,128)(2,1)S(1)}) custom-call(bf16[128,4096]{1,0:T(8,128)(2,1)S(1)} %get-tuple-element.30.own_ref, bf16[128,4096]{1,0:T(8,128)(2,1)S(1)} %collective-permute-done.other_ref, f32[1,4096]{1,0:T(1,128)S(1)} %get-tuple-element.31.gain_ref, ...), custom_call_target="tpu_custom_call" | custom-call | flops 2147483648 | bytes 12075008 | tf_op jit(solution)/shard_map/project_kv/pallas_call | solution.py:37
  7.6 0.0 copy-start.1
  7.7 0.8 %copy-done.1 = bf16[4,2,256,128]{3,2,1,0:T(8,128)(2,1)} copy-done((bf16[4,2,256,128]{3,2,1,0:T(8,128)(2,1)}, bf16[4,2,256,128]{3,2,1,0:T(8,128)(2,1)S(1)}, u32[]{:S(2)}) %copy-start.1) | copy-done | bytes 524312
  8.4 2.5 %collective-permute-start.1 = (bf16[4,2,256,128]{3,2,1,0:T(8,128)(2,1)}, bf16[4,2,256,128]{3,2,1,0:T(8,128)(2,1)}, u32[]{:S(2)}, u32[]{:S(2)}) collective-permute-start(bf16[4,2,256,128]{3,2,1,0:T(8,128)(2,1)} %copy-done.1), channel_id=1, source_target_pairs={{0,2},{1,3},{2,0},{3,1},{4,6},{5,7},{6,4},{7,5},{8,10},{9,11},{10,... | collective-permute-start | bytes 1572872 | tf_op jit(solution)/shard_map/ppermute | solution.py:347
  11.0 1.5 %collective-permute-start.3 = (bf16[4,2,256,128]{3,2,1,0:T(8,128)(2,1)}, bf16[4,2,256,128]{3,2,1,0:T(8,128)(2,1)}, u32[]{:S(2)}, u32[]{:S(2)}) collective-permute-start(bf16[4,2,256,128]{3,2,1,0:T(8,128)(2,1)} %copy-done.1), channel_id=1, source_target_pairs={{0,1},{1,0},{2,3},{3,2},{4,5},{5,4},{6,7},{7,6},{8,9},{9,8},{10,11... | collective-permute-start | bytes 1572872 | tf_op jit(solution)/shard_map/ppermute | solution.py:347
  12.5 1.6 %collective-permute-start.4 = (bf16[4,2,256,128]{3,2,1,0:T(8,128)(2,1)}, bf16[4,2,256,128]{3,2,1,0:T(8,128)(2,1)}, u32[]{:S(2)}, u32[]{:S(2)}) collective-permute-start(bf16[4,2,256,128]{3,2,1,0:T(8,128)(2,1)} %copy-done.1), channel_id=1, source_target_pairs={{0,4},{1,5},{2,6},{3,7},{4,0},{5,1},{6,2},{7,3},{8,12},{9,13},{10,... | collective-permute-start | bytes 1572872 | tf_op jit(solution)/shard_map/ppermute | solution.py:347
  14.1 0.1 fusion.5
  14.2 0.1 copy.16
  14.4 0.0 copy-start.4
  14.4 6.9 %project_query.1.refs_4_ = bf16[256,2048]{1,0:T(8,128)(2,1)S(1)} custom-call(bf16[128,4096]{1,0:T(8,128)(2,1)S(1)} %get-tuple-element.30.own_ref, bf16[128,4096]{1,0:T(8,128)(2,1)S(1)} %get-tuple-element.37.other_ref, bf16[4096,2048]{1,0:T(8,128)(2,1)} %w_hbm.1), custom_call_target="tpu_custom_call" | custom-call | flops 4294967296 | bytes 19922944 | tf_op jit(solution)/shard_map/project_query/pallas_call | solution.py:37
  21.3 0.0 copy-start.2
  21.5 0.1 copy.17
  21.7 1.1 %copy.20 = bf16[4,2,2,128,128]{4,3,0,1,2:T(8,128)(2,1)S(1)} copy(bf16[4,2,2,128,128]{4,3,2,1,0:T(8,128)(2,1)} %bitcast.29) | data formatting | bytes 1048576 | tf_op jit(solution)/shard_map/reshape | solution.py:434
  22.8 0.6 %dynamic_slice.75 = s32[1]{0:T(128)} dynamic-slice(s32[2]{0:T(128)S(1)} %copy-done.4, s32[]{:T(128)S(6)} %select_n.222), dynamic_slice_sizes={1} | dynamic-slice | bytes 12 | tf_op jit(solution)/shard_map/jit(dynamic_index_in_dim)/dynamic_slice | solution.py:435
  24.0 0.9 %reverse_select_fusion = bf16[2,2,4,128,128]{4,3,2,1,0:T(8,128)(2,1)} fusion(bf16[2,2,4,128,128]{4,3,2,1,0:T(8,128)(2,1)S(1)} %bitcast.33, pred[]{:T(512)} %bitcast.11), kind=kLoop, calls=%fused_computation | loop fusion | flops 262144 | bytes 1048577 | tf_op jit(solution)/shard_map/jit(_where)/select_n | solution.py:436
  25.0 0.0 collective-permute-done.1.refs_7_
  25.0 0.6 %collective-permute-start.2 = (bf16[4,2,256,128]{3,2,1,0:T(8,128)(2,1)}, bf16[4,2,256,128]{3,2,1,0:T(8,128)(2,1)S(1)}, u32[]{:S(2)}, u32[]{:S(2)}) collective-permute-start(bf16[4,2,256,128]{3,2,1,0:T(8,128)(2,1)} %collective-permute-done.1.refs_7_), channel_id=1, source_target_pairs={{0,1},{1,0},{2,3},{3,2},{4,5},{5,4},{6,7},{7,6},{8,9},{9,8},{10,11... | collective-permute-start | bytes 1572872 | tf_op jit(solution)/shard_map/ppermute | solution.py:347
  25.6 0.9 %collective-permute-done.4.refs_8_ = bf16[4,2,256,128]{3,2,1,0:T(8,128)(2,1)} collective-permute-done((bf16[4,2,256,128]{3,2,1,0:T(8,128)(2,1)}, bf16[4,2,256,128]{3,2,1,0:T(8,128)(2,1)}, u32[]{:S(2)}, u32[]{:S(2)}) %collective-permute-start.4) | collective-permute-done | bytes 524320 | tf_op jit(solution)/shard_map/ppermute | solution.py:347
  26.6 0.6 %collective-permute-start.6 = (bf16[4,2,256,128]{3,2,1,0:T(8,128)(2,1)}, bf16[4,2,256,128]{3,2,1,0:T(8,128)(2,1)S(1)}, u32[]{:S(2)}, u32[]{:S(2)}) collective-permute-start(bf16[4,2,256,128]{3,2,1,0:T(8,128)(2,1)} %collective-permute-done.4.refs_8_), channel_id=1, source_target_pairs={{0,2},{1,3},{2,0},{3,1},{4,6},{5,7},{6,4},{7,5},{8,10},{9,11},{10,... | collective-permute-start | bytes 1572872 | tf_op jit(solution)/shard_map/ppermute | solution.py:347
  27.2 0.0 collective-permute-done.3.refs_6_
  27.2 1.6 %collective-permute-start.8 = (bf16[4,2,256,128]{3,2,1,0:T(8,128)(2,1)}, bf16[4,2,256,128]{3,2,1,0:T(8,128)(2,1)S(1)}, u32[]{:S(2)}, u32[]{:S(2)}) collective-permute-start(bf16[4,2,256,128]{3,2,1,0:T(8,128)(2,1)} %collective-permute-done.3.refs_6_), channel_id=1, source_target_pairs={{0,4},{1,5},{2,6},{3,7},{4,0},{5,1},{6,2},{7,3},{8,12},{9,13},{10,... | collective-permute-start | bytes 1572872 | tf_op jit(solution)/shard_map/ppermute | solution.py:347
  28.8 7.8 %attend.3 = (f32[256,2048]{1,0:T(8,128)S(1)}, f32[256,2048]{1,0:T(8,128)S(1)}, f32[256,2048]{1,0:T(8,128)S(1)}) custom-call(s32[256,1]{1,0:T(8,128)S(1)} %broadcast_select_fusion.refs_0_, s32[256,1]{1,0:T(8,128)S(1)} %broadcast_add_fusion.refs_1_, s32[1,1024]{1,0:T(1,128)S(1)} %bitcast.32, s32[1,1024]{1,0:T(1,128)S(1)} %bitcast.31, ...), custom_call_target="tpu_custom_call" | custom-call | flops 3221225472 | bytes 9447424 | tf_op jit(solution)/shard_map/attend/pallas_call | solution.py:37
  36.6 2.0 %collective-permute-done.2.refs_5_ = bf16[4,2,256,128]{3,2,1,0:T(8,128)(2,1)S(1)} collective-permute-done((bf16[4,2,256,128]{3,2,1,0:T(8,128)(2,1)}, bf16[4,2,256,128]{3,2,1,0:T(8,128)(2,1)S(1)}, u32[]{:S(2)}, u32[]{:S(2)}) %collective-permute-start.2) | collective-permute-done | bytes 524320 | tf_op jit(solution)/shard_map/ppermute | solution.py:347
  38.7 0.1 bitcast_select_fusion
  38.8 0.8 %collective-permute-start.5 = (bf16[1024,128]{1,0:T(8,128)(2,1)S(1)}, bf16[1024,128]{1,0:T(8,128)(2,1)S(1)}, u32[]{:S(2)}, u32[]{:S(2)}) collective-permute-start(bf16[1024,128]{1,0:T(8,128)(2,1)S(1)} %bitcast_select_fusion), channel_id=1, source_target_pairs={{0,4},{1,5},{2,6},{3,7},{4,8},{5,1},{6,2},{7,3},{8,12},{9,13},{10,... | collective-permute-start | bytes 786440 | tf_op jit(solution)/shard_map/ppermute | solution.py:366
  39.6 0.1 collective-permute-done.6.refs_6_
  39.7 1.5 %collective-permute-start.7 = (bf16[1,2,256,128]{3,2,1,0:T(8,128)(2,1)S(1)}, bf16[1,2,256,128]{3,2,1,0:T(8,128)(2,1)S(1)}, u32[]{:S(2)}, u32[]{:S(2)}) collective-permute-start(bf16[1,2,256,128]{3,2,1,0:T(8,128)(2,1)S(1)} %slice.10), channel_id=1, source_target_pairs={{0,1},{1,0},{2,3},{3,2},{4,5},{5,4},{6,7},{7,6},{8,9},{9,8},{10,11... | collective-permute-start | bytes 393224 | tf_op jit(solution)/shard_map/ppermute | solution.py:347
  41.2 0.0 collective-permute-done.8.refs_7_
  41.2 0.0 slice-start.2
  41.2 1.6 %collective-permute-start.9 = (bf16[1,2,256,128]{3,2,1,0:T(8,128)(2,1)S(1)}, bf16[1,2,256,128]{3,2,1,0:T(8,128)(2,1)S(1)}, u32[]{:S(2)}, u32[]{:S(2)}) collective-permute-start(bf16[1,2,256,128]{3,2,1,0:T(8,128)(2,1)S(1)} %slice.11), channel_id=1, source_target_pairs={{0,2},{1,3},{2,0},{3,1},{4,6},{5,7},{6,4},{7,5},{8,10},{9,11},{10,... | collective-permute-start | bytes 393224 | tf_op jit(solution)/shard_map/ppermute | solution.py:347
  42.8 4.8 %attend.4 = (f32[256,2048]{1,0:T(8,128)S(1)}, f32[256,2048]{1,0:T(8,128)S(1)}, f32[256,2048]{1,0:T(8,128)S(1)}) custom-call(s32[256,1]{1,0:T(8,128)S(1)} %broadcast_select_fusion.refs_0_, s32[256,1]{1,0:T(8,128)S(1)} %broadcast_add_fusion.refs_1_, s32[1,768]{1,0:T(1,128)S(1)} %broadcast_in_dim.53.refs_2_, s32[1,768]{1,0:T(1,128)S(1)} %broadcast_in_dim.54.refs_3_, ...), custom_call_target="tpu_custom_call" | custom-call | flops 2415919104 | bytes 15212544 | tf_op jit(solution)/shard_map/attend/pallas_call | solution.py:37
  47.6 0.0 collective-permute-done.7
  47.6 0.4 collective-permute-done.5
  48.0 0.1 maximum_select_fusion.refs_5_
  48.2 0.0 slice-start.3
  48.2 2.2 %attend.5.x_ref = bf16[256,2048]{1,0:T(8,128)(2,1)S(1)} custom-call(s32[256,1]{1,0:T(8,128)S(1)} %broadcast_select_fusion.refs_0_, s32[256,1]{1,0:T(8,128)S(1)} %broadcast_add_fusion.refs_1_, s32[1,256]{1,0:T(1,128)S(1)} %bitcast.30, s32[1,256]{1,0:T(1,128)S(1)} %broadcast_select_fusion.1.refs_3_, bf16[256,2048]{1,0:T(8,128)(2,1)S(1)} %project_query.1.refs_4_, ...), custom_call_target="tpu_custom_call" | custom-call | flops 805306368 | bytes 8916992 | tf_op jit(solution)/shard_map/attend/pallas_call | solution.py:37
  50.4 3.4 %project_out.2 = (f32[128,3072]{1,0:T(8,128)S(1)}, bf16[128,3072]{1,0:T(8,128)(2,1)S(1)}) custom-call(bf16[256,2048]{1,0:T(8,128)(2,1)S(1)} %attend.5.x_ref, bf16[2048,4096]{1,0:T(8,128)(2,1)S(1)} %bitcast.28), custom_call_target="tpu_custom_call" | custom-call | flops 3221225472 | bytes 20185088 | tf_op jit(solution)/shard_map/project_out/pallas_call | solution.py:37
  53.8 0.0 copy-start
  53.8 0.1 collective-permute-start.10
  53.9 1.2 %project_out.3 = (f32[128,1024]{1,0:T(8,128)S(1)}, bf16[128,1024]{1,0:T(8,128)(2,1)S(1)}) custom-call(bf16[256,2048]{1,0:T(8,128)(2,1)S(1)} %attend.5.x_ref, bf16[2048,4096]{1,0:T(8,128)(2,1)S(1)} %bitcast.28), custom_call_target="tpu_custom_call" | custom-call | flops 1073741824 | bytes 18612224 | tf_op jit(solution)/shard_map/project_out/pallas_call | solution.py:37
  55.2 0.6 collective-permute-start.11
  55.7 1.2 %collective-permute-done.11.refs_3_ = bf16[128,1024]{1,0:T(8,128)(2,1)S(1)} collective-permute-done((bf16[128,1024]{1,0:T(8,128)(2,1)S(1)}, bf16[128,1024]{1,0:T(8,128)(2,1)S(1)}, u32[]{:S(2)}, u32[]{:S(2)}) %collective-permute-start.11) | collective-permute-done | bytes 262176 | tf_op jit(solution)/shard_map/ppermute | solution.py:333
  56.9 0.0 collective-permute-done.10.refs_1_
  56.9 1.4 %finish.1 = (bf16[128,4096]{1,0:T(8,128)(2,1)}, bf16[128,4096]{1,0:T(8,128)(2,1)}) custom-call(bf16[128,4096]{1,0:T(8,128)(2,1)S(1)} %copy-done, f32[128,3072]{1,0:T(8,128)S(1)} %get-tuple-element.51.refs_0_, bf16[128,3072]{1,0:T(8,128)(2,1)S(1)} %collective-permute-done.10.refs_1_, f32[128,1024]{1,0:T(8,128)S(1)} %get-tuple-element.53.refs_2_, ...), custom_call_target="tpu_custom_call" | custom-call | flops 1048576 | bytes 6291456 | tf_op jit(solution)/shard_map/finish/pallas_call | solution.py:37
  (38 shorter events, 0.3 us)
Async XLA Ops:
  0.6 4.3 %collective-permute-start = (bf16[128,4096]{1,0:T(8,128)(2,1)}, bf16[128,4096]{1,0:T(8,128)(2,1)S(1)}, u32[]{:S(2)}, u32[]{:S(2)}) collective-permute-start(bf16[128,4096]{1,0:T(8,128)(2,1)} %tokens_ref.1), channel_id=1, source_target_pairs={{0,16},{16,0},{1,17},{17,1},{2,18},{18,2},{3,19},{19,3},{4,20},{20... | collective-permute-start | bytes 3145736 | tf_op jit(solution)/shard_map/ppermute | solution.py:333
  5.0 9.1 %copy-start.3 = (s32[4096]{0:T(1024)S(1)}, s32[4096]{0:T(1024)}, u32[]{:S(2)}) copy-start(s32[4096]{0:T(1024)} %param.14) | copy-start | bytes 49156
  7.6 0.8 %copy-start.1 = (bf16[4,2,256,128]{3,2,1,0:T(8,128)(2,1)}, bf16[4,2,256,128]{3,2,1,0:T(8,128)(2,1)S(1)}, u32[]{:S(2)}) copy-start(bf16[4,2,256,128]{3,2,1,0:T(8,128)(2,1)S(1)} %get-tuple-element.34.refs_5_) | copy-start | bytes 1572868
  8.4 16.5 %collective-permute-start.1 = (bf16[4,2,256,128]{3,2,1,0:T(8,128)(2,1)}, bf16[4,2,256,128]{3,2,1,0:T(8,128)(2,1)}, u32[]{:S(2)}, u32[]{:S(2)}) collective-permute-start(bf16[4,2,256,128]{3,2,1,0:T(8,128)(2,1)} %copy-done.1), channel_id=1, source_target_pairs={{0,2},{1,3},{2,0},{3,1},{4,6},{5,7},{6,4},{7,5},{8,10},{9,11},{10,... | collective-permute-start | bytes 1572872 | tf_op jit(solution)/shard_map/ppermute | solution.py:347
  11.0 16.2 %collective-permute-start.3 = (bf16[4,2,256,128]{3,2,1,0:T(8,128)(2,1)}, bf16[4,2,256,128]{3,2,1,0:T(8,128)(2,1)}, u32[]{:S(2)}, u32[]{:S(2)}) collective-permute-start(bf16[4,2,256,128]{3,2,1,0:T(8,128)(2,1)} %copy-done.1), channel_id=1, source_target_pairs={{0,1},{1,0},{2,3},{3,2},{4,5},{5,4},{6,7},{7,6},{8,9},{9,8},{10,11... | collective-permute-start | bytes 1572872 | tf_op jit(solution)/shard_map/ppermute | solution.py:347
  12.5 14.1 %collective-permute-start.4 = (bf16[4,2,256,128]{3,2,1,0:T(8,128)(2,1)}, bf16[4,2,256,128]{3,2,1,0:T(8,128)(2,1)}, u32[]{:S(2)}, u32[]{:S(2)}) collective-permute-start(bf16[4,2,256,128]{3,2,1,0:T(8,128)(2,1)} %copy-done.1), channel_id=1, source_target_pairs={{0,4},{1,5},{2,6},{3,7},{4,0},{5,1},{6,2},{7,3},{8,12},{9,13},{10,... | collective-permute-start | bytes 1572872 | tf_op jit(solution)/shard_map/ppermute | solution.py:347
  14.4 8.4 %copy-start.4 = (s32[2]{0:T(128)S(1)}, s32[2]{0:T(128)}, u32[]{:S(2)}) copy-start(s32[2]{0:T(128)} %param.15) | copy-start | bytes 28
  21.3 7.5 %copy-start.2 = (bf16[4,2,256,128]{3,2,1,0:T(8,128)(2,1)S(1)}, bf16[4,2,256,128]{3,2,1,0:T(8,128)(2,1)}, u32[]{:S(2)}) copy-start(bf16[4,2,256,128]{3,2,1,0:T(8,128)(2,1)} %copy-done.1) | copy-start | bytes 1572868
  25.0 13.7 %collective-permute-start.2 = (bf16[4,2,256,128]{3,2,1,0:T(8,128)(2,1)}, bf16[4,2,256,128]{3,2,1,0:T(8,128)(2,1)S(1)}, u32[]{:S(2)}, u32[]{:S(2)}) collective-permute-start(bf16[4,2,256,128]{3,2,1,0:T(8,128)(2,1)} %collective-permute-done.1.refs_7_), channel_id=1, source_target_pairs={{0,1},{1,0},{2,3},{3,2},{4,5},{5,4},{6,7},{7,6},{8,9},{9,8},{10,11... | collective-permute-start | bytes 1572872 | tf_op jit(solution)/shard_map/ppermute | solution.py:347
  26.6 13.1 %collective-permute-start.6 = (bf16[4,2,256,128]{3,2,1,0:T(8,128)(2,1)}, bf16[4,2,256,128]{3,2,1,0:T(8,128)(2,1)S(1)}, u32[]{:S(2)}, u32[]{:S(2)}) collective-permute-start(bf16[4,2,256,128]{3,2,1,0:T(8,128)(2,1)} %collective-permute-done.4.refs_8_), channel_id=1, source_target_pairs={{0,2},{1,3},{2,0},{3,1},{4,6},{5,7},{6,4},{7,5},{8,10},{9,11},{10,... | collective-permute-start | bytes 1572872 | tf_op jit(solution)/shard_map/ppermute | solution.py:347
  27.2 14.0 %collective-permute-start.8 = (bf16[4,2,256,128]{3,2,1,0:T(8,128)(2,1)}, bf16[4,2,256,128]{3,2,1,0:T(8,128)(2,1)S(1)}, u32[]{:S(2)}, u32[]{:S(2)}) collective-permute-start(bf16[4,2,256,128]{3,2,1,0:T(8,128)(2,1)} %collective-permute-done.3.refs_6_), channel_id=1, source_target_pairs={{0,4},{1,5},{2,6},{3,7},{4,0},{5,1},{6,2},{7,3},{8,12},{9,13},{10,... | collective-permute-start | bytes 1572872 | tf_op jit(solution)/shard_map/ppermute | solution.py:347
  28.8 21.6 %slice-start = ((s8[16777216]{0:T(1024)(128)(4,1)}), s8[4194304]{0:T(1024)(128)(4,1)S(1)}, s32[]{:S(2)}) async-start(s8[16777216]{0:T(1024)(128)(4,1)} %bitcast.27), calls=%async_computation | async-start | bytes 8388608
  28.8 21.6 %slice-start.1 = ((s8[16777216]{0:T(1024)(128)(4,1)}), s8[4194304]{0:T(1024)(128)(4,1)S(1)}, s32[]{:S(2)}) async-start(s8[16777216]{0:T(1024)(128)(4,1)} %bitcast.27), calls=%async_computation.1 | async-start | bytes 8388608
  38.8 9.2 %collective-permute-start.5 = (bf16[1024,128]{1,0:T(8,128)(2,1)S(1)}, bf16[1024,128]{1,0:T(8,128)(2,1)S(1)}, u32[]{:S(2)}, u32[]{:S(2)}) collective-permute-start(bf16[1024,128]{1,0:T(8,128)(2,1)S(1)} %bitcast_select_fusion), channel_id=1, source_target_pairs={{0,4},{1,5},{2,6},{3,7},{4,8},{5,1},{6,2},{7,3},{8,12},{9,13},{10,... | collective-permute-start | bytes 786440 | tf_op jit(solution)/shard_map/ppermute | solution.py:366
  39.7 7.9 %collective-permute-start.7 = (bf16[1,2,256,128]{3,2,1,0:T(8,128)(2,1)S(1)}, bf16[1,2,256,128]{3,2,1,0:T(8,128)(2,1)S(1)}, u32[]{:S(2)}, u32[]{:S(2)}) collective-permute-start(bf16[1,2,256,128]{3,2,1,0:T(8,128)(2,1)S(1)} %slice.10), channel_id=1, source_target_pairs={{0,1},{1,0},{2,3},{3,2},{4,5},{5,4},{6,7},{7,6},{8,9},{9,8},{10,11... | collective-permute-start | bytes 393224 | tf_op jit(solution)/shard_map/ppermute | solution.py:347
  41.2 9.2 %slice-start.2 = ((s8[16777216]{0:T(1024)(128)(4,1)}), s8[4194304]{0:T(1024)(128)(4,1)S(1)}, s32[]{:S(2)}) async-start(s8[16777216]{0:T(1024)(128)(4,1)} %bitcast.27), calls=%async_computation.2 | async-start | bytes 8388608
  41.2 6.4 %collective-permute-start.9 = (bf16[1,2,256,128]{3,2,1,0:T(8,128)(2,1)S(1)}, bf16[1,2,256,128]{3,2,1,0:T(8,128)(2,1)S(1)}, u32[]{:S(2)}, u32[]{:S(2)}) collective-permute-start(bf16[1,2,256,128]{3,2,1,0:T(8,128)(2,1)S(1)} %slice.11), channel_id=1, source_target_pairs={{0,2},{1,3},{2,0},{3,1},{4,6},{5,7},{6,4},{7,5},{8,10},{9,11},{10,... | collective-permute-start | bytes 393224 | tf_op jit(solution)/shard_map/ppermute | solution.py:347
  48.2 2.2 %slice-start.3 = ((s8[16777216]{0:T(1024)(128)(4,1)}), s8[4194304]{0:T(1024)(128)(4,1)S(1)}, s32[]{:S(2)}) async-start(s8[16777216]{0:T(1024)(128)(4,1)} %bitcast.27), calls=%async_computation.3 | async-start | bytes 8388608
  53.8 3.1 %copy-start = (bf16[128,4096]{1,0:T(8,128)(2,1)S(1)}, bf16[128,4096]{1,0:T(8,128)(2,1)}, u32[]{:S(2)}) copy-start(bf16[128,4096]{1,0:T(8,128)(2,1)} %tokens_ref.1) | copy-start | bytes 3145732
  53.8 3.1 %collective-permute-start.10 = (bf16[128,3072]{1,0:T(8,128)(2,1)S(1)}, bf16[128,3072]{1,0:T(8,128)(2,1)S(1)}, u32[]{:S(2)}, u32[]{:S(2)}) collective-permute-start(bf16[128,3072]{1,0:T(8,128)(2,1)S(1)} %get-tuple-element.52), channel_id=1, source_target_pairs={{0,16},{16,0},{1,17},{17,1},{2,18},{18,2},{3,19},{19,3},{4,20},{20... | collective-permute-start | bytes 2359304 | tf_op jit(solution)/shard_map/ppermute | solution.py:333
  55.2 1.7 %collective-permute-start.11 = (bf16[128,1024]{1,0:T(8,128)(2,1)S(1)}, bf16[128,1024]{1,0:T(8,128)(2,1)S(1)}, u32[]{:S(2)}, u32[]{:S(2)}) collective-permute-start(bf16[128,1024]{1,0:T(8,128)(2,1)S(1)} %get-tuple-element.54), channel_id=1, source_target_pairs={{0,16},{16,0},{1,17},{17,1},{2,18},{18,2},{3,19},{19,3},{4,20},{20... | collective-permute-start | bytes 786440 | tf_op jit(solution)/shard_map/ppermute | solution.py:333

commit v5 on v4

--- a/solution.py
+++ b/solution.py
@@ -174,7 +174,7 @@
         acc_in, peak_in, mass_in = refs[:3]
         refs = refs[3:]
     if last:
-        out_ref, bias_ref = refs
+        own_out, other_out, bias_ref = refs
     else:
         acc_out, peak_out, mass_out, bias_ref = refs
     seen = (seg_q[...] == seg_k[...]) & (pos_k[...] <= pos_q[...])
@@ -221,7 +221,9 @@
             acc = acc + acc_in[:, cols[head]] * keep
             mass = mass + mass_in[:, cols[head]] * keep
         if last:
-            out_ref[:, cols[head]] = (acc / mass).astype(jnp.bfloat16)
+            result = (acc / mass).astype(jnp.bfloat16)
+            own_out[:, cols[head]] = result[: rows // 2]
+            other_out[:, cols[head]] = result[rows // 2 :]
         else:
             acc_out[:, cols[head]] = acc
             peak_out[:, cols[head]] = peak
@@ -251,7 +253,7 @@
     first = state is None
     args += [] if first else state
     if last:
-        outs = jax.ShapeDtypeStruct((rows, q_cols), jnp.bfloat16)
+        outs = [jax.ShapeDtypeStruct((rows // 2, q_cols), jnp.bfloat16)] * 2
     else:
         outs = [jax.ShapeDtypeStruct((rows, q_cols), jnp.float32)] * 3
     return call(
@@ -266,24 +268,18 @@
     )
 
 
-def project_out_kernel(first, x_ref, w_ref, own_ref, other_ref):
-    half, cols = own_ref.shape
+def project_out_kernel(x_ref, w_ref, out_ref):
     tile = 512
-    for start in range(0, cols, tile):
-        weights = w_ref[:, first + start : first + start + tile]
-        part = jnp.dot(x_ref[...], weights, preferred_element_type=jnp.float32)
-        own_ref[:, start : start + tile] = part[:half]
-        other_ref[:, start : start + tile] = part[half:].astype(other_ref.dtype)
-
-
-def project_out(attention, w_out, first, cols):
-    rows, depth = attention.shape
-    outs = [
-        jax.ShapeDtypeStruct((rows // 2, cols), jnp.float32),
-        jax.ShapeDtypeStruct((rows // 2, cols), jnp.bfloat16),
-    ]
-    kernel = functools.partial(project_out_kernel, first)
-    return call(kernel, "project_out", (attention, w_out), outs, 2 * rows * depth * cols)
+    for start in range(0, out_ref.shape[1], tile):
+        cols = slice(start, start + tile)
+        part = jnp.dot(x_ref[...], w_ref[:, cols], preferred_element_type=jnp.float32)
+        out_ref[:, cols] = part.astype(out_ref.dtype)
+
+
+def project_out(rows, w_out, kind):
+    out = jax.ShapeDtypeStruct((rows.shape[0], w_out.shape[1]), kind)
+    flops = 2 * rows.shape[0] * w_out.size
+    return call(project_out_kernel, "project_out", (rows, w_out), out, flops)
 
 
 def finish_kernel(parts, tokens_ref, *refs):
@@ -348,8 +344,12 @@
 
     from_x, from_y, from_z = exchange(block, 1), exchange(block, 2), exchange(block, 4)
     work = yield [(from_x, index ^ 1), (from_y, index ^ 2), (from_z, index ^ 4)]
-    from_x, from_y, from_z = (after(value, work) for value in (from_x, from_y, from_z))
-    from_xz, from_xy, from_yz = exchange(from_x, 4), exchange(from_y, 1), exchange(from_z, 2)
+    from_y = after(from_y, work)
+    from_xy = exchange(from_y, 1)
+    from_x = after(from_x, from_y)
+    from_xz = exchange(from_x, 4)
+    from_z = after(from_z, from_x)
+    from_yz = exchange(from_z, 2)
     work = yield [(from_xy, index ^ 3), (from_yz, index ^ 6), (from_xz, index ^ 5)]
     from_xy, from_yz, from_xz = (after(value, work) for value in (from_xy, from_yz, from_xz))
     seam_page = lax.dynamic_slice_in_dim(from_xy, (1 - core) * page, page, 2)
@@ -450,13 +450,10 @@
         group, done = following, (state, page_pool)
     attention = state
 
-    width = w_out.shape[1]
-    cuts = [0, width * 3 // 4, width]
-    parts = []
-    for first, end in zip(cuts, cuts[1:]):
-        mine, theirs = project_out(attention, w_out, first, end - first)
-        parts.append((mine, swap_cores(theirs)))
-    mixed, attn_out = finish(tokens, parts)
+    own_rows, other_rows = attention
+    theirs = project_out(other_rows, w_out, jnp.bfloat16)
+    mine = project_out(after(own_rows, theirs), w_out, jnp.float32)
+    mixed, attn_out = finish(tokens, [(mine, swap_cores(theirs))])
     return (mixed, attn_out, page_pool)
 
 

time: 58.7 us -> 57.1 us (0.973)
  waiting for transfers between devices: 4.59 us -> 3.16 us
    ppermute x3 -> x2, waiting for transfers between devices: 1.17 us -> 0.29 us  [swap_cores(): return lax.ppermute(value, 'kv', [(0, 1), (1, 0)])]
  transfers between devices with their start and end apart: 12 -> 11, of which waited for: 5 -> 3; matrix products, arithmetic and copies ran while one was open for 6% -> 6% of each run, Pallas kernels for 42% -> 45%
where the time goes in v5:
time: 57.1 us; the launch traced here: 56.9 us
  Pallas kernels  34.1 us (60%)
  starting transfers between devices  13.5 us (24%)
  waiting for transfers between devices  3.16 us (6%)
  local copies, waits for them, and re-layouts  2.85 us (5%)
  between operations  1.86 us (3%)
  other arithmetic  1.45 us (3%)
    pallas_call x9, Pallas kernels, call(): pl.pallas_call(kernel, in_specs=in_specs or [IN_VMEM] * len(args), out_sp...  34.1 us
    ppermute x8, starting transfers between devices, exchange(): return lax.ppermute(value, 'seq', [(i, i ^ bit) for i in range(count)])  11.9 us
    ppermute x8, waiting for transfers between devices, exchange(): return lax.ppermute(value, 'seq', [(i, i ^ bit) for i in range(count)])  2.87 us
  transfers between devices with their start and end apart: 11, of which 3 were waited for; matrix products, arithmetic and copies ran while one was open for 6% of the time, Pallas kernels for 45%

profile of v5, /device:TPU:0, one launch (start us, length us, event | category | flops | bytes accessed | tf_op | source)
XLA Modules:
  0.0 56.9 jit_solution(11206142697798725349)
XLA Ops:
  0.6 0.5 collective-permute-start
  1.1 3.8 %stage.1 = (bf16[128,4096]{1,0:T(8,128)(2,1)S(1)}, f32[1,4096]{1,0:T(1,128)S(1)}, bf16[4096,512]{1,0:T(8,128)(2,1)S(1)}, bf16[4096,512]{1,0:T(8,128)(2,1)S(1)}) custom-call(bf16[128,4096]{1,0:T(8,128)(2,1)} %tokens_ref.1, f32[1,4096]{1,0:T(1,128)} %bitcast.36, bf16[4096,512]{1,0:T(8,128)(2,1)} %wk_hbm.1, bf16[4096,512]{1,0:T(8,128)(2,1)} %wv_hbm.1), custom_call_target="tpu_custom_call" | custom-call | flops 2097152 | bytes 18907136 | tf_op jit(solution)/shard_map/stage/pallas_call | solution.py:37
  5.0 0.0 collective-permute-done.other_ref
  5.0 0.0 copy-start.3
  5.0 2.6 %project_kv.1 = (bf16[128,4096]{1,0:T(8,128)(2,1)S(1)}, bf16[4,2,256,128]{3,2,1,0:T(8,128)(2,1)S(1)}) custom-call(bf16[128,4096]{1,0:T(8,128)(2,1)S(1)} %get-tuple-element.29.own_ref, bf16[128,4096]{1,0:T(8,128)(2,1)S(1)} %collective-permute-done.other_ref, f32[1,4096]{1,0:T(1,128)S(1)} %get-tuple-element.30.gain_ref, ...), custom_call_target="tpu_custom_call" | custom-call | flops 2147483648 | bytes 12075008 | tf_op jit(solution)/shard_map/project_kv/pallas_call | solution.py:37
  7.6 0.0 copy-start.1
  7.7 0.8 %copy-done.1 = bf16[4,2,256,128]{3,2,1,0:T(8,128)(2,1)} copy-done((bf16[4,2,256,128]{3,2,1,0:T(8,128)(2,1)}, bf16[4,2,256,128]{3,2,1,0:T(8,128)(2,1)S(1)}, u32[]{:S(2)}) %copy-start.1) | copy-done | bytes 524312
  8.4 2.5 %collective-permute-start.1 = (bf16[4,2,256,128]{3,2,1,0:T(8,128)(2,1)}, bf16[4,2,256,128]{3,2,1,0:T(8,128)(2,1)}, u32[]{:S(2)}, u32[]{:S(2)}) collective-permute-start(bf16[4,2,256,128]{3,2,1,0:T(8,128)(2,1)} %copy-done.1), channel_id=1, source_target_pairs={{0,2},{1,3},{2,0},{3,1},{4,6},{5,7},{6,4},{7,5},{8,10},{9,11},{10,... | collective-permute-start | bytes 1572872 | tf_op jit(solution)/shard_map/ppermute | solution.py:343
  11.0 1.5 %collective-permute-start.3 = (bf16[4,2,256,128]{3,2,1,0:T(8,128)(2,1)}, bf16[4,2,256,128]{3,2,1,0:T(8,128)(2,1)}, u32[]{:S(2)}, u32[]{:S(2)}) collective-permute-start(bf16[4,2,256,128]{3,2,1,0:T(8,128)(2,1)} %copy-done.1), channel_id=1, source_target_pairs={{0,1},{1,0},{2,3},{3,2},{4,5},{5,4},{6,7},{7,6},{8,9},{9,8},{10,11... | collective-permute-start | bytes 1572872 | tf_op jit(solution)/shard_map/ppermute | solution.py:343
  12.5 1.6 %collective-permute-start.4 = (bf16[4,2,256,128]{3,2,1,0:T(8,128)(2,1)}, bf16[4,2,256,128]{3,2,1,0:T(8,128)(2,1)}, u32[]{:S(2)}, u32[]{:S(2)}) collective-permute-start(bf16[4,2,256,128]{3,2,1,0:T(8,128)(2,1)} %copy-done.1), channel_id=1, source_target_pairs={{0,4},{1,5},{2,6},{3,7},{4,0},{5,1},{6,2},{7,3},{8,12},{9,13},{10,... | collective-permute-start | bytes 1572872 | tf_op jit(solution)/shard_map/ppermute | solution.py:343
  14.1 0.0 copy-done.3
  14.1 0.1 fusion.5
  14.2 0.1 copy.16
  14.4 0.0 copy-start.4
  14.4 6.9 %project_query.1.refs_4_ = bf16[256,2048]{1,0:T(8,128)(2,1)S(1)} custom-call(bf16[128,4096]{1,0:T(8,128)(2,1)S(1)} %get-tuple-element.29.own_ref, bf16[128,4096]{1,0:T(8,128)(2,1)S(1)} %get-tuple-element.36.other_ref, bf16[4096,2048]{1,0:T(8,128)(2,1)} %w_hbm.1), custom_call_target="tpu_custom_call" | custom-call | flops 4294967296 | bytes 19922944 | tf_op jit(solution)/shard_map/project_query/pallas_call | solution.py:37
  21.3 0.0 copy-start.2
  21.5 0.1 copy.17
  21.7 1.1 %copy.20 = bf16[4,2,2,128,128]{4,3,0,1,2:T(8,128)(2,1)S(1)} copy(bf16[4,2,2,128,128]{4,3,2,1,0:T(8,128)(2,1)} %bitcast.29) | data formatting | bytes 1048576 | tf_op jit(solution)/shard_map/reshape | solution.py:434
  22.8 0.6 %dynamic_slice.75 = s32[1]{0:T(128)} dynamic-slice(s32[2]{0:T(128)S(1)} %copy-done.4, s32[]{:T(128)S(6)} %select_n.222), dynamic_slice_sizes={1} | dynamic-slice | bytes 12 | tf_op jit(solution)/shard_map/jit(dynamic_index_in_dim)/dynamic_slice | solution.py:435
  24.0 0.9 %reverse_select_fusion = bf16[2,2,4,128,128]{4,3,2,1,0:T(8,128)(2,1)} fusion(bf16[2,2,4,128,128]{4,3,2,1,0:T(8,128)(2,1)S(1)} %bitcast.33, pred[]{:T(512)} %bitcast.11), kind=kLoop, calls=%fused_computation | loop fusion | flops 262144 | bytes 1048577 | tf_op jit(solution)/shard_map/jit(_where)/select_n | solution.py:436
  25.0 0.0 collective-permute-done.1.refs_7_
  25.0 0.6 %collective-permute-start.2 = (bf16[4,2,256,128]{3,2,1,0:T(8,128)(2,1)}, bf16[4,2,256,128]{3,2,1,0:T(8,128)(2,1)S(1)}, u32[]{:S(2)}, u32[]{:S(2)}) collective-permute-start(bf16[4,2,256,128]{3,2,1,0:T(8,128)(2,1)} %collective-permute-done.1.refs_7_), channel_id=1, source_target_pairs={{0,1},{1,0},{2,3},{3,2},{4,5},{5,4},{6,7},{7,6},{8,9},{9,8},{10,11... | collective-permute-start | bytes 1572872 | tf_op jit(solution)/shard_map/ppermute | solution.py:343
  25.6 0.0 collective-permute-done.3.refs_6_
  25.6 1.6 %collective-permute-start.8 = (bf16[4,2,256,128]{3,2,1,0:T(8,128)(2,1)}, bf16[4,2,256,128]{3,2,1,0:T(8,128)(2,1)S(1)}, u32[]{:S(2)}, u32[]{:S(2)}) collective-permute-start(bf16[4,2,256,128]{3,2,1,0:T(8,128)(2,1)} %collective-permute-done.3.refs_6_), channel_id=1, source_target_pairs={{0,4},{1,5},{2,6},{3,7},{4,0},{5,1},{6,2},{7,3},{8,12},{9,13},{10,... | collective-permute-start | bytes 1572872 | tf_op jit(solution)/shard_map/ppermute | solution.py:343
  27.2 0.0 collective-permute-done.4.refs_8_
  27.3 1.5 %collective-permute-start.6 = (bf16[4,2,256,128]{3,2,1,0:T(8,128)(2,1)}, bf16[4,2,256,128]{3,2,1,0:T(8,128)(2,1)S(1)}, u32[]{:S(2)}, u32[]{:S(2)}) collective-permute-start(bf16[4,2,256,128]{3,2,1,0:T(8,128)(2,1)} %collective-permute-done.4.refs_8_), channel_id=1, source_target_pairs={{0,2},{1,3},{2,0},{3,1},{4,6},{5,7},{6,4},{7,5},{8,10},{9,11},{10,... | collective-permute-start | bytes 1572872 | tf_op jit(solution)/shard_map/ppermute | solution.py:343
  28.8 7.6 %attend.3 = (f32[256,2048]{1,0:T(8,128)S(1)}, f32[256,2048]{1,0:T(8,128)S(1)}, f32[256,2048]{1,0:T(8,128)S(1)}) custom-call(s32[256,1]{1,0:T(8,128)S(1)} %broadcast_select_fusion.refs_0_, s32[256,1]{1,0:T(8,128)S(1)} %broadcast_add_fusion.refs_1_, s32[1,1024]{1,0:T(1,128)S(1)} %bitcast.32, s32[1,1024]{1,0:T(1,128)S(1)} %bitcast.31, ...), custom_call_target="tpu_custom_call" | custom-call | flops 3221225472 | bytes 9447424 | tf_op jit(solution)/shard_map/attend/pallas_call | solution.py:37
  36.4 2.2 %collective-permute-done.2.refs_5_ = bf16[4,2,256,128]{3,2,1,0:T(8,128)(2,1)S(1)} collective-permute-done((bf16[4,2,256,128]{3,2,1,0:T(8,128)(2,1)}, bf16[4,2,256,128]{3,2,1,0:T(8,128)(2,1)S(1)}, u32[]{:S(2)}, u32[]{:S(2)}) %collective-permute-start.2) | collective-permute-done | bytes 524320 | tf_op jit(solution)/shard_map/ppermute | solution.py:343
  38.7 0.1 bitcast_select_fusion
  38.8 1.0 %collective-permute-start.5 = (bf16[1024,128]{1,0:T(8,128)(2,1)S(1)}, bf16[1024,128]{1,0:T(8,128)(2,1)S(1)}, u32[]{:S(2)}, u32[]{:S(2)}) collective-permute-start(bf16[1024,128]{1,0:T(8,128)(2,1)S(1)} %bitcast_select_fusion), channel_id=1, source_target_pairs={{0,4},{1,5},{2,6},{3,7},{4,8},{5,1},{6,2},{7,3},{8,12},{9,13},{10,... | collective-permute-start | bytes 786440 | tf_op jit(solution)/shard_map/ppermute | solution.py:366
  39.8 0.6 %collective-permute-done.6.refs_6_ = bf16[4,2,256,128]{3,2,1,0:T(8,128)(2,1)S(1)} collective-permute-done((bf16[4,2,256,128]{3,2,1,0:T(8,128)(2,1)}, bf16[4,2,256,128]{3,2,1,0:T(8,128)(2,1)S(1)}, u32[]{:S(2)}, u32[]{:S(2)}) %collective-permute-start.6) | collective-permute-done | bytes 524320 | tf_op jit(solution)/shard_map/ppermute | solution.py:343
  40.4 1.2 %collective-permute-start.7 = (bf16[1,2,256,128]{3,2,1,0:T(8,128)(2,1)S(1)}, bf16[1,2,256,128]{3,2,1,0:T(8,128)(2,1)S(1)}, u32[]{:S(2)}, u32[]{:S(2)}) collective-permute-start(bf16[1,2,256,128]{3,2,1,0:T(8,128)(2,1)S(1)} %slice.10), channel_id=1, source_target_pairs={{0,1},{1,0},{2,3},{3,2},{4,5},{5,4},{6,7},{7,6},{8,9},{9,8},{10,11... | collective-permute-start | bytes 393224 | tf_op jit(solution)/shard_map/ppermute | solution.py:343
  41.6 0.0 collective-permute-done.8.refs_7_
  41.7 0.0 slice-start.2
  41.7 1.3 %collective-permute-start.9 = (bf16[1,2,256,128]{3,2,1,0:T(8,128)(2,1)S(1)}, bf16[1,2,256,128]{3,2,1,0:T(8,128)(2,1)S(1)}, u32[]{:S(2)}, u32[]{:S(2)}) collective-permute-start(bf16[1,2,256,128]{3,2,1,0:T(8,128)(2,1)S(1)} %slice.11), channel_id=1, source_target_pairs={{0,2},{1,3},{2,0},{3,1},{4,6},{5,7},{6,4},{7,5},{8,10},{9,11},{10,... | collective-permute-start | bytes 393224 | tf_op jit(solution)/shard_map/ppermute | solution.py:343
  43.0 4.8 %attend.4 = (f32[256,2048]{1,0:T(8,128)S(1)}, f32[256,2048]{1,0:T(8,128)S(1)}, f32[256,2048]{1,0:T(8,128)S(1)}) custom-call(s32[256,1]{1,0:T(8,128)S(1)} %broadcast_select_fusion.refs_0_, s32[256,1]{1,0:T(8,128)S(1)} %broadcast_add_fusion.refs_1_, s32[1,768]{1,0:T(1,128)S(1)} %broadcast_in_dim.53.refs_2_, s32[1,768]{1,0:T(1,128)S(1)} %broadcast_in_dim.54.refs_3_, ...), custom_call_target="tpu_custom_call" | custom-call | flops 2415919104 | bytes 15212544 | tf_op jit(solution)/shard_map/attend/pallas_call | solution.py:37
  47.8 0.0 collective-permute-done.7
  47.8 0.0 collective-permute-done.9
  47.8 0.0 collective-permute-done.5
  47.8 0.0 slice-start.3
  47.8 0.1 maximum_select_fusion.refs_5_
  48.0 2.2 %attend.5 = (bf16[128,2048]{1,0:T(8,128)(2,1)S(1)}, bf16[128,2048]{1,0:T(8,128)(2,1)S(1)}) custom-call(s32[256,1]{1,0:T(8,128)S(1)} %broadcast_select_fusion.refs_0_, s32[256,1]{1,0:T(8,128)S(1)} %broadcast_add_fusion.refs_1_, s32[1,256]{1,0:T(1,128)S(1)} %bitcast.30, s32[1,256]{1,0:T(1,128)S(1)} %broadcast_select_fusion.1.refs_3_, ...), custom_call_target="tpu_custom_call" | custom-call | flops 805306368 | bytes 8916992 | tf_op jit(solution)/shard_map/attend/pallas_call | solution.py:37
  50.2 2.3 %project_out.2 = bf16[128,4096]{1,0:T(8,128)(2,1)S(1)} custom-call(bf16[128,2048]{1,0:T(8,128)(2,1)S(1)} %get-tuple-element.51.x_ref, bf16[2048,4096]{1,0:T(8,128)(2,1)S(1)} %bitcast.28), custom_call_target="tpu_custom_call" | custom-call | flops 2147483648 | bytes 18350080 | tf_op jit(solution)/shard_map/project_out/pallas_call | solution.py:37
  52.6 0.1 collective-permute-start.10
  52.7 0.0 copy-start
  52.7 2.3 %project_out.3.refs_0_ = f32[128,4096]{1,0:T(8,128)S(1)} custom-call(bf16[128,2048]{1,0:T(8,128)(2,1)S(1)} %get-tuple-element.52.x_ref, bf16[2048,4096]{1,0:T(8,128)(2,1)S(1)} %bitcast.28), custom_call_target="tpu_custom_call" | custom-call | flops 2147483648 | bytes 19398656 | tf_op jit(solution)/shard_map/project_out/pallas_call | solution.py:37
  55.0 0.3 collective-permute-done.10.refs_1_
  55.3 1.4 %finish.1 = (bf16[128,4096]{1,0:T(8,128)(2,1)}, bf16[128,4096]{1,0:T(8,128)(2,1)}) custom-call(bf16[128,4096]{1,0:T(8,128)(2,1)S(1)} %copy-done, f32[128,4096]{1,0:T(8,128)S(1)} %project_out.3.refs_0_, bf16[128,4096]{1,0:T(8,128)(2,1)S(1)} %collective-permute-done.10.refs_1_), custom_call_target="tpu_custom_call" | custom-call | flops 1048576 | bytes 6291456 | tf_op jit(solution)/shard_map/finish/pallas_call | solution.py:37
  (36 shorter events, 0.3 us)
Async XLA Ops:
  0.6 4.3 %collective-permute-start = (bf16[128,4096]{1,0:T(8,128)(2,1)}, bf16[128,4096]{1,0:T(8,128)(2,1)S(1)}, u32[]{:S(2)}, u32[]{:S(2)}) collective-permute-start(bf16[128,4096]{1,0:T(8,128)(2,1)} %tokens_ref.1), channel_id=1, source_target_pairs={{0,16},{16,0},{1,17},{17,1},{2,18},{18,2},{3,19},{19,3},{4,20},{20... | collective-permute-start | bytes 3145736 | tf_op jit(solution)/shard_map/ppermute | solution.py:329
  5.0 9.1 %copy-start.3 = (s32[4096]{0:T(1024)S(1)}, s32[4096]{0:T(1024)}, u32[]{:S(2)}) copy-start(s32[4096]{0:T(1024)} %param.14) | copy-start | bytes 49156
  7.6 0.8 %copy-start.1 = (bf16[4,2,256,128]{3,2,1,0:T(8,128)(2,1)}, bf16[4,2,256,128]{3,2,1,0:T(8,128)(2,1)S(1)}, u32[]{:S(2)}) copy-start(bf16[4,2,256,128]{3,2,1,0:T(8,128)(2,1)S(1)} %get-tuple-element.33.refs_5_) | copy-start | bytes 1572868
  8.4 16.5 %collective-permute-start.1 = (bf16[4,2,256,128]{3,2,1,0:T(8,128)(2,1)}, bf16[4,2,256,128]{3,2,1,0:T(8,128)(2,1)}, u32[]{:S(2)}, u32[]{:S(2)}) collective-permute-start(bf16[4,2,256,128]{3,2,1,0:T(8,128)(2,1)} %copy-done.1), channel_id=1, source_target_pairs={{0,2},{1,3},{2,0},{3,1},{4,6},{5,7},{6,4},{7,5},{8,10},{9,11},{10,... | collective-permute-start | bytes 1572872 | tf_op jit(solution)/shard_map/ppermute | solution.py:343
  11.0 14.6 %collective-permute-start.3 = (bf16[4,2,256,128]{3,2,1,0:T(8,128)(2,1)}, bf16[4,2,256,128]{3,2,1,0:T(8,128)(2,1)}, u32[]{:S(2)}, u32[]{:S(2)}) collective-permute-start(bf16[4,2,256,128]{3,2,1,0:T(8,128)(2,1)} %copy-done.1), channel_id=1, source_target_pairs={{0,1},{1,0},{2,3},{3,2},{4,5},{5,4},{6,7},{7,6},{8,9},{9,8},{10,11... | collective-permute-start | bytes 1572872 | tf_op jit(solution)/shard_map/ppermute | solution.py:343
  12.5 14.8 %collective-permute-start.4 = (bf16[4,2,256,128]{3,2,1,0:T(8,128)(2,1)}, bf16[4,2,256,128]{3,2,1,0:T(8,128)(2,1)}, u32[]{:S(2)}, u32[]{:S(2)}) collective-permute-start(bf16[4,2,256,128]{3,2,1,0:T(8,128)(2,1)} %copy-done.1), channel_id=1, source_target_pairs={{0,4},{1,5},{2,6},{3,7},{4,0},{5,1},{6,2},{7,3},{8,12},{9,13},{10,... | collective-permute-start | bytes 1572872 | tf_op jit(solution)/shard_map/ppermute | solution.py:343
  14.4 8.4 %copy-start.4 = (s32[2]{0:T(128)S(1)}, s32[2]{0:T(128)}, u32[]{:S(2)}) copy-start(s32[2]{0:T(128)} %param.15) | copy-start | bytes 28
  21.3 7.5 %copy-start.2 = (bf16[4,2,256,128]{3,2,1,0:T(8,128)(2,1)S(1)}, bf16[4,2,256,128]{3,2,1,0:T(8,128)(2,1)}, u32[]{:S(2)}) copy-start(bf16[4,2,256,128]{3,2,1,0:T(8,128)(2,1)} %copy-done.1) | copy-start | bytes 1572868
  25.0 13.7 %collective-permute-start.2 = (bf16[4,2,256,128]{3,2,1,0:T(8,128)(2,1)}, bf16[4,2,256,128]{3,2,1,0:T(8,128)(2,1)S(1)}, u32[]{:S(2)}, u32[]{:S(2)}) collective-permute-start(bf16[4,2,256,128]{3,2,1,0:T(8,128)(2,1)} %collective-permute-done.1.refs_7_), channel_id=1, source_target_pairs={{0,1},{1,0},{2,3},{3,2},{4,5},{5,4},{6,7},{7,6},{8,9},{9,8},{10,11... | collective-permute-start | bytes 1572872 | tf_op jit(solution)/shard_map/ppermute | solution.py:343
  25.6 16.0 %collective-permute-start.8 = (bf16[4,2,256,128]{3,2,1,0:T(8,128)(2,1)}, bf16[4,2,256,128]{3,2,1,0:T(8,128)(2,1)S(1)}, u32[]{:S(2)}, u32[]{:S(2)}) collective-permute-start(bf16[4,2,256,128]{3,2,1,0:T(8,128)(2,1)} %collective-permute-done.3.refs_6_), channel_id=1, source_target_pairs={{0,4},{1,5},{2,6},{3,7},{4,0},{5,1},{6,2},{7,3},{8,12},{9,13},{10,... | collective-permute-start | bytes 1572872 | tf_op jit(solution)/shard_map/ppermute | solution.py:343
  27.3 13.2 %collective-permute-start.6 = (bf16[4,2,256,128]{3,2,1,0:T(8,128)(2,1)}, bf16[4,2,256,128]{3,2,1,0:T(8,128)(2,1)S(1)}, u32[]{:S(2)}, u32[]{:S(2)}) collective-permute-start(bf16[4,2,256,128]{3,2,1,0:T(8,128)(2,1)} %collective-permute-done.4.refs_8_), channel_id=1, source_target_pairs={{0,2},{1,3},{2,0},{3,1},{4,6},{5,7},{6,4},{7,5},{8,10},{9,11},{10,... | collective-permute-start | bytes 1572872 | tf_op jit(solution)/shard_map/ppermute | solution.py:343
  28.8 21.4 %slice-start = ((s8[16777216]{0:T(1024)(128)(4,1)}), s8[4194304]{0:T(1024)(128)(4,1)S(1)}, s32[]{:S(2)}) async-start(s8[16777216]{0:T(1024)(128)(4,1)} %bitcast.27), calls=%async_computation | async-start | bytes 8388608
  28.8 21.4 %slice-start.1 = ((s8[16777216]{0:T(1024)(128)(4,1)}), s8[4194304]{0:T(1024)(128)(4,1)S(1)}, s32[]{:S(2)}) async-start(s8[16777216]{0:T(1024)(128)(4,1)} %bitcast.27), calls=%async_computation.1 | async-start | bytes 8388608
  38.8 9.0 %collective-permute-start.5 = (bf16[1024,128]{1,0:T(8,128)(2,1)S(1)}, bf16[1024,128]{1,0:T(8,128)(2,1)S(1)}, u32[]{:S(2)}, u32[]{:S(2)}) collective-permute-start(bf16[1024,128]{1,0:T(8,128)(2,1)S(1)} %bitcast_select_fusion), channel_id=1, source_target_pairs={{0,4},{1,5},{2,6},{3,7},{4,8},{5,1},{6,2},{7,3},{8,12},{9,13},{10,... | collective-permute-start | bytes 786440 | tf_op jit(solution)/shard_map/ppermute | solution.py:366
  40.4 7.4 %collective-permute-start.7 = (bf16[1,2,256,128]{3,2,1,0:T(8,128)(2,1)S(1)}, bf16[1,2,256,128]{3,2,1,0:T(8,128)(2,1)S(1)}, u32[]{:S(2)}, u32[]{:S(2)}) collective-permute-start(bf16[1,2,256,128]{3,2,1,0:T(8,128)(2,1)S(1)} %slice.10), channel_id=1, source_target_pairs={{0,1},{1,0},{2,3},{3,2},{4,5},{5,4},{6,7},{7,6},{8,9},{9,8},{10,11... | collective-permute-start | bytes 393224 | tf_op jit(solution)/shard_map/ppermute | solution.py:343
  41.7 8.6 %slice-start.2 = ((s8[16777216]{0:T(1024)(128)(4,1)}), s8[4194304]{0:T(1024)(128)(4,1)S(1)}, s32[]{:S(2)}) async-start(s8[16777216]{0:T(1024)(128)(4,1)} %bitcast.27), calls=%async_computation.2 | async-start | bytes 8388608
  41.7 6.1 %collective-permute-start.9 = (bf16[1,2,256,128]{3,2,1,0:T(8,128)(2,1)S(1)}, bf16[1,2,256,128]{3,2,1,0:T(8,128)(2,1)S(1)}, u32[]{:S(2)}, u32[]{:S(2)}) collective-permute-start(bf16[1,2,256,128]{3,2,1,0:T(8,128)(2,1)S(1)} %slice.11), channel_id=1, source_target_pairs={{0,2},{1,3},{2,0},{3,1},{4,6},{5,7},{6,4},{7,5},{8,10},{9,11},{10,... | collective-permute-start | bytes 393224 | tf_op jit(solution)/shard_map/ppermute | solution.py:343
  47.8 2.4 %slice-start.3 = ((s8[16777216]{0:T(1024)(128)(4,1)}), s8[4194304]{0:T(1024)(128)(4,1)S(1)}, s32[]{:S(2)}) async-start(s8[16777216]{0:T(1024)(128)(4,1)} %bitcast.27), calls=%async_computation.3 | async-start | bytes 8388608
  52.6 2.7 %collective-permute-start.10 = (bf16[128,4096]{1,0:T(8,128)(2,1)S(1)}, bf16[128,4096]{1,0:T(8,128)(2,1)S(1)}, u32[]{:S(2)}, u32[]{:S(2)}) collective-permute-start(bf16[128,4096]{1,0:T(8,128)(2,1)S(1)} %project_out.2), channel_id=1, source_target_pairs={{0,16},{16,0},{1,17},{17,1},{2,18},{18,2},{3,19},{19,3},{4,20},{20... | collective-permute-start | bytes 3145736 | tf_op jit(solution)/shard_map/ppermute | solution.py:329
  52.7 2.6 %copy-start = (bf16[128,4096]{1,0:T(8,128)(2,1)S(1)}, bf16[128,4096]{1,0:T(8,128)(2,1)}, u32[]{:S(2)}) copy-start(bf16[128,4096]{1,0:T(8,128)(2,1)} %tokens_ref.1) | copy-start | bytes 3145732

commit v6 on v5

--- a/solution.py
+++ b/solution.py
@@ -230,8 +230,8 @@
             mass_out[:, cols[head]] = mass
 
     if last:
-        for start in range(0, heads, 4):
-            many = range(start, start + 4)
+        for start in range(0, heads, 8):
+            many = range(start, start + 8)
             scores = [score(head) for head in many]
             weighed = [weigh(head, scores[head - start]) for head in many]
             for head in many:

time: 57.1 us -> 57 us (level)
  no operation moved by 1% of the time
where the time goes in v6:
time: 57 us; the launch traced here: 56.8 us
  Pallas kernels  34 us (60%)
  starting transfers between devices  13.5 us (24%)
  waiting for transfers between devices  3.16 us (6%)
  local copies, waits for them, and re-layouts  2.85 us (5%)
  between operations  1.86 us (3%)
  other arithmetic  1.45 us (3%)
    pallas_call x9, Pallas kernels, call(): pl.pallas_call(kernel, in_specs=in_specs or [IN_VMEM] * len(args), out_sp...  34 us
    ppermute x8, starting transfers between devices, exchange(): return lax.ppermute(value, 'seq', [(i, i ^ bit) for i in range(count)])  11.9 us
    ppermute x8, waiting for transfers between devices, exchange(): return lax.ppermute(value, 'seq', [(i, i ^ bit) for i in range(count)])  2.87 us
  transfers between devices with their start and end apart: 11, of which 3 were waited for; matrix products, arithmetic and copies ran while one was open for 6% of the time, Pallas kernels for 45%

profile of v6, /device:TPU:0, one launch (start us, length us, event | category | flops | bytes accessed | tf_op | source)
XLA Modules:
  0.0 56.8 jit_solution(15956322204347808751)
XLA Ops:
  0.6 0.5 collective-permute-start
  1.1 3.8 %stage.1 = (bf16[128,4096]{1,0:T(8,128)(2,1)S(1)}, f32[1,4096]{1,0:T(1,128)S(1)}, bf16[4096,512]{1,0:T(8,128)(2,1)S(1)}, bf16[4096,512]{1,0:T(8,128)(2,1)S(1)}) custom-call(bf16[128,4096]{1,0:T(8,128)(2,1)} %tokens_ref.1, f32[1,4096]{1,0:T(1,128)} %bitcast.36, bf16[4096,512]{1,0:T(8,128)(2,1)} %wk_hbm.1, bf16[4096,512]{1,0:T(8,128)(2,1)} %wv_hbm.1), custom_call_target="tpu_custom_call" | custom-call | flops 2097152 | bytes 18907136 | tf_op jit(solution)/shard_map/stage/pallas_call | solution.py:37
  5.0 0.0 collective-permute-done.other_ref
  5.0 0.0 copy-start.3
  5.0 2.6 %project_kv.1 = (bf16[128,4096]{1,0:T(8,128)(2,1)S(1)}, bf16[4,2,256,128]{3,2,1,0:T(8,128)(2,1)S(1)}) custom-call(bf16[128,4096]{1,0:T(8,128)(2,1)S(1)} %get-tuple-element.29.own_ref, bf16[128,4096]{1,0:T(8,128)(2,1)S(1)} %collective-permute-done.other_ref, f32[1,4096]{1,0:T(1,128)S(1)} %get-tuple-element.30.gain_ref, ...), custom_call_target="tpu_custom_call" | custom-call | flops 2147483648 | bytes 12075008 | tf_op jit(solution)/shard_map/project_kv/pallas_call | solution.py:37
  7.6 0.0 copy-start.1
  7.7 0.8 %copy-done.1 = bf16[4,2,256,128]{3,2,1,0:T(8,128)(2,1)} copy-done((bf16[4,2,256,128]{3,2,1,0:T(8,128)(2,1)}, bf16[4,2,256,128]{3,2,1,0:T(8,128)(2,1)S(1)}, u32[]{:S(2)}) %copy-start.1) | copy-done | bytes 524312
  8.4 2.5 %collective-permute-start.1 = (bf16[4,2,256,128]{3,2,1,0:T(8,128)(2,1)}, bf16[4,2,256,128]{3,2,1,0:T(8,128)(2,1)}, u32[]{:S(2)}, u32[]{:S(2)}) collective-permute-start(bf16[4,2,256,128]{3,2,1,0:T(8,128)(2,1)} %copy-done.1), channel_id=1, source_target_pairs={{0,2},{1,3},{2,0},{3,1},{4,6},{5,7},{6,4},{7,5},{8,10},{9,11},{10,... | collective-permute-start | bytes 1572872 | tf_op jit(solution)/shard_map/ppermute | solution.py:343
  11.0 1.5 %collective-permute-start.3 = (bf16[4,2,256,128]{3,2,1,0:T(8,128)(2,1)}, bf16[4,2,256,128]{3,2,1,0:T(8,128)(2,1)}, u32[]{:S(2)}, u32[]{:S(2)}) collective-permute-start(bf16[4,2,256,128]{3,2,1,0:T(8,128)(2,1)} %copy-done.1), channel_id=1, source_target_pairs={{0,1},{1,0},{2,3},{3,2},{4,5},{5,4},{6,7},{7,6},{8,9},{9,8},{10,11... | collective-permute-start | bytes 1572872 | tf_op jit(solution)/shard_map/ppermute | solution.py:343
  12.5 1.6 %collective-permute-start.4 = (bf16[4,2,256,128]{3,2,1,0:T(8,128)(2,1)}, bf16[4,2,256,128]{3,2,1,0:T(8,128)(2,1)}, u32[]{:S(2)}, u32[]{:S(2)}) collective-permute-start(bf16[4,2,256,128]{3,2,1,0:T(8,128)(2,1)} %copy-done.1), channel_id=1, source_target_pairs={{0,4},{1,5},{2,6},{3,7},{4,0},{5,1},{6,2},{7,3},{8,12},{9,13},{10,... | collective-permute-start | bytes 1572872 | tf_op jit(solution)/shard_map/ppermute | solution.py:343
  14.1 0.0 copy-done.3
  14.1 0.1 fusion.5
  14.2 0.1 copy.16
  14.4 0.0 copy-start.4
  14.4 6.9 %project_query.1.refs_4_ = bf16[256,2048]{1,0:T(8,128)(2,1)S(1)} custom-call(bf16[128,4096]{1,0:T(8,128)(2,1)S(1)} %get-tuple-element.29.own_ref, bf16[128,4096]{1,0:T(8,128)(2,1)S(1)} %get-tuple-element.36.other_ref, bf16[4096,2048]{1,0:T(8,128)(2,1)} %w_hbm.1), custom_call_target="tpu_custom_call" | custom-call | flops 4294967296 | bytes 19922944 | tf_op jit(solution)/shard_map/project_query/pallas_call | solution.py:37
  21.3 0.0 copy-start.2
  21.5 0.1 copy.17
  21.7 1.1 %copy.20 = bf16[4,2,2,128,128]{4,3,0,1,2:T(8,128)(2,1)S(1)} copy(bf16[4,2,2,128,128]{4,3,2,1,0:T(8,128)(2,1)} %bitcast.29) | data formatting | bytes 1048576 | tf_op jit(solution)/shard_map/reshape | solution.py:434
  22.8 0.6 %dynamic_slice.75 = s32[1]{0:T(128)} dynamic-slice(s32[2]{0:T(128)S(1)} %copy-done.4, s32[]{:T(128)S(6)} %select_n.222), dynamic_slice_sizes={1} | dynamic-slice | bytes 12 | tf_op jit(solution)/shard_map/jit(dynamic_index_in_dim)/dynamic_slice | solution.py:435
  24.0 0.9 %reverse_select_fusion = bf16[2,2,4,128,128]{4,3,2,1,0:T(8,128)(2,1)} fusion(bf16[2,2,4,128,128]{4,3,2,1,0:T(8,128)(2,1)S(1)} %bitcast.33, pred[]{:T(512)} %bitcast.11), kind=kLoop, calls=%fused_computation | loop fusion | flops 262144 | bytes 1048577 | tf_op jit(solution)/shard_map/jit(_where)/select_n | solution.py:436
  25.0 0.0 collective-permute-done.1.refs_7_
  25.0 0.6 %collective-permute-start.2 = (bf16[4,2,256,128]{3,2,1,0:T(8,128)(2,1)}, bf16[4,2,256,128]{3,2,1,0:T(8,128)(2,1)S(1)}, u32[]{:S(2)}, u32[]{:S(2)}) collective-permute-start(bf16[4,2,256,128]{3,2,1,0:T(8,128)(2,1)} %collective-permute-done.1.refs_7_), channel_id=1, source_target_pairs={{0,1},{1,0},{2,3},{3,2},{4,5},{5,4},{6,7},{7,6},{8,9},{9,8},{10,11... | collective-permute-start | bytes 1572872 | tf_op jit(solution)/shard_map/ppermute | solution.py:343
  25.6 0.0 collective-permute-done.3.refs_6_
  25.6 1.6 %collective-permute-start.8 = (bf16[4,2,256,128]{3,2,1,0:T(8,128)(2,1)}, bf16[4,2,256,128]{3,2,1,0:T(8,128)(2,1)S(1)}, u32[]{:S(2)}, u32[]{:S(2)}) collective-permute-start(bf16[4,2,256,128]{3,2,1,0:T(8,128)(2,1)} %collective-permute-done.3.refs_6_), channel_id=1, source_target_pairs={{0,4},{1,5},{2,6},{3,7},{4,0},{5,1},{6,2},{7,3},{8,12},{9,13},{10,... | collective-permute-start | bytes 1572872 | tf_op jit(solution)/shard_map/ppermute | solution.py:343
  27.2 0.0 collective-permute-done.4.refs_8_
  27.3 1.5 %collective-permute-start.6 = (bf16[4,2,256,128]{3,2,1,0:T(8,128)(2,1)}, bf16[4,2,256,128]{3,2,1,0:T(8,128)(2,1)S(1)}, u32[]{:S(2)}, u32[]{:S(2)}) collective-permute-start(bf16[4,2,256,128]{3,2,1,0:T(8,128)(2,1)} %collective-permute-done.4.refs_8_), channel_id=1, source_target_pairs={{0,2},{1,3},{2,0},{3,1},{4,6},{5,7},{6,4},{7,5},{8,10},{9,11},{10,... | collective-permute-start | bytes 1572872 | tf_op jit(solution)/shard_map/ppermute | solution.py:343
  28.8 7.6 %attend.3 = (f32[256,2048]{1,0:T(8,128)S(1)}, f32[256,2048]{1,0:T(8,128)S(1)}, f32[256,2048]{1,0:T(8,128)S(1)}) custom-call(s32[256,1]{1,0:T(8,128)S(1)} %broadcast_select_fusion.refs_0_, s32[256,1]{1,0:T(8,128)S(1)} %broadcast_add_fusion.refs_1_, s32[1,1024]{1,0:T(1,128)S(1)} %bitcast.32, s32[1,1024]{1,0:T(1,128)S(1)} %bitcast.31, ...), custom_call_target="tpu_custom_call" | custom-call | flops 3221225472 | bytes 9447424 | tf_op jit(solution)/shard_map/attend/pallas_call | solution.py:37
  36.4 2.2 %collective-permute-done.2.refs_5_ = bf16[4,2,256,128]{3,2,1,0:T(8,128)(2,1)S(1)} collective-permute-done((bf16[4,2,256,128]{3,2,1,0:T(8,128)(2,1)}, bf16[4,2,256,128]{3,2,1,0:T(8,128)(2,1)S(1)}, u32[]{:S(2)}, u32[]{:S(2)}) %collective-permute-start.2) | collective-permute-done | bytes 524320 | tf_op jit(solution)/shard_map/ppermute | solution.py:343
  38.7 0.1 bitcast_select_fusion
  38.8 1.0 %collective-permute-start.5 = (bf16[1024,128]{1,0:T(8,128)(2,1)S(1)}, bf16[1024,128]{1,0:T(8,128)(2,1)S(1)}, u32[]{:S(2)}, u32[]{:S(2)}) collective-permute-start(bf16[1024,128]{1,0:T(8,128)(2,1)S(1)} %bitcast_select_fusion), channel_id=1, source_target_pairs={{0,4},{1,5},{2,6},{3,7},{4,8},{5,1},{6,2},{7,3},{8,12},{9,13},{10,... | collective-permute-start | bytes 786440 | tf_op jit(solution)/shard_map/ppermute | solution.py:366
  39.8 0.6 %collective-permute-done.6.refs_6_ = bf16[4,2,256,128]{3,2,1,0:T(8,128)(2,1)S(1)} collective-permute-done((bf16[4,2,256,128]{3,2,1,0:T(8,128)(2,1)}, bf16[4,2,256,128]{3,2,1,0:T(8,128)(2,1)S(1)}, u32[]{:S(2)}, u32[]{:S(2)}) %collective-permute-start.6) | collective-permute-done | bytes 524320 | tf_op jit(solution)/shard_map/ppermute | solution.py:343
  40.4 1.2 %collective-permute-start.7 = (bf16[1,2,256,128]{3,2,1,0:T(8,128)(2,1)S(1)}, bf16[1,2,256,128]{3,2,1,0:T(8,128)(2,1)S(1)}, u32[]{:S(2)}, u32[]{:S(2)}) collective-permute-start(bf16[1,2,256,128]{3,2,1,0:T(8,128)(2,1)S(1)} %slice.10), channel_id=1, source_target_pairs={{0,1},{1,0},{2,3},{3,2},{4,5},{5,4},{6,7},{7,6},{8,9},{9,8},{10,11... | collective-permute-start | bytes 393224 | tf_op jit(solution)/shard_map/ppermute | solution.py:343
  41.6 0.0 collective-permute-done.8.refs_7_
  41.7 0.0 slice-start.2
  41.7 1.3 %collective-permute-start.9 = (bf16[1,2,256,128]{3,2,1,0:T(8,128)(2,1)S(1)}, bf16[1,2,256,128]{3,2,1,0:T(8,128)(2,1)S(1)}, u32[]{:S(2)}, u32[]{:S(2)}) collective-permute-start(bf16[1,2,256,128]{3,2,1,0:T(8,128)(2,1)S(1)} %slice.11), channel_id=1, source_target_pairs={{0,2},{1,3},{2,0},{3,1},{4,6},{5,7},{6,4},{7,5},{8,10},{9,11},{10,... | collective-permute-start | bytes 393224 | tf_op jit(solution)/shard_map/ppermute | solution.py:343
  43.0 4.8 %attend.4 = (f32[256,2048]{1,0:T(8,128)S(1)}, f32[256,2048]{1,0:T(8,128)S(1)}, f32[256,2048]{1,0:T(8,128)S(1)}) custom-call(s32[256,1]{1,0:T(8,128)S(1)} %broadcast_select_fusion.refs_0_, s32[256,1]{1,0:T(8,128)S(1)} %broadcast_add_fusion.refs_1_, s32[1,768]{1,0:T(1,128)S(1)} %broadcast_in_dim.53.refs_2_, s32[1,768]{1,0:T(1,128)S(1)} %broadcast_in_dim.54.refs_3_, ...), custom_call_target="tpu_custom_call" | custom-call | flops 2415919104 | bytes 15212544 | tf_op jit(solution)/shard_map/attend/pallas_call | solution.py:37
  47.8 0.0 collective-permute-done.7
  47.8 0.0 collective-permute-done.9
  47.8 0.0 collective-permute-done.5
  47.8 0.0 slice-start.3
  47.8 0.1 maximum_select_fusion.refs_5_
  48.0 2.1 %attend.5 = (bf16[128,2048]{1,0:T(8,128)(2,1)S(1)}, bf16[128,2048]{1,0:T(8,128)(2,1)S(1)}) custom-call(s32[256,1]{1,0:T(8,128)S(1)} %broadcast_select_fusion.refs_0_, s32[256,1]{1,0:T(8,128)S(1)} %broadcast_add_fusion.refs_1_, s32[1,256]{1,0:T(1,128)S(1)} %bitcast.30, s32[1,256]{1,0:T(1,128)S(1)} %broadcast_select_fusion.1.refs_3_, ...), custom_call_target="tpu_custom_call" | custom-call | flops 805306368 | bytes 8916992 | tf_op jit(solution)/shard_map/attend/pallas_call | solution.py:37
  50.1 2.3 %project_out.2 = bf16[128,4096]{1,0:T(8,128)(2,1)S(1)} custom-call(bf16[128,2048]{1,0:T(8,128)(2,1)S(1)} %get-tuple-element.51.x_ref, bf16[2048,4096]{1,0:T(8,128)(2,1)S(1)} %bitcast.28), custom_call_target="tpu_custom_call" | custom-call | flops 2147483648 | bytes 18350080 | tf_op jit(solution)/shard_map/project_out/pallas_call | solution.py:37
  52.5 0.1 collective-permute-start.10
  52.6 0.0 copy-start
  52.6 2.3 %project_out.3.refs_0_ = f32[128,4096]{1,0:T(8,128)S(1)} custom-call(bf16[128,2048]{1,0:T(8,128)(2,1)S(1)} %get-tuple-element.52.x_ref, bf16[2048,4096]{1,0:T(8,128)(2,1)S(1)} %bitcast.28), custom_call_target="tpu_custom_call" | custom-call | flops 2147483648 | bytes 19398656 | tf_op jit(solution)/shard_map/project_out/pallas_call | solution.py:37
  54.9 0.3 collective-permute-done.10.refs_1_
  55.2 1.4 %finish.1 = (bf16[128,4096]{1,0:T(8,128)(2,1)}, bf16[128,4096]{1,0:T(8,128)(2,1)}) custom-call(bf16[128,4096]{1,0:T(8,128)(2,1)S(1)} %copy-done, f32[128,4096]{1,0:T(8,128)S(1)} %project_out.3.refs_0_, bf16[128,4096]{1,0:T(8,128)(2,1)S(1)} %collective-permute-done.10.refs_1_), custom_call_target="tpu_custom_call" | custom-call | flops 1048576 | bytes 6291456 | tf_op jit(solution)/shard_map/finish/pallas_call | solution.py:37
  (36 shorter events, 0.3 us)
Async XLA Ops:
  0.6 4.3 %collective-permute-start = (bf16[128,4096]{1,0:T(8,128)(2,1)}, bf16[128,4096]{1,0:T(8,128)(2,1)S(1)}, u32[]{:S(2)}, u32[]{:S(2)}) collective-permute-start(bf16[128,4096]{1,0:T(8,128)(2,1)} %tokens_ref.1), channel_id=1, source_target_pairs={{0,16},{16,0},{1,17},{17,1},{2,18},{18,2},{3,19},{19,3},{4,20},{20... | collective-permute-start | bytes 3145736 | tf_op jit(solution)/shard_map/ppermute | solution.py:329
  5.0 9.1 %copy-start.3 = (s32[4096]{0:T(1024)S(1)}, s32[4096]{0:T(1024)}, u32[]{:S(2)}) copy-start(s32[4096]{0:T(1024)} %param.14) | copy-start | bytes 49156
  7.6 0.8 %copy-start.1 = (bf16[4,2,256,128]{3,2,1,0:T(8,128)(2,1)}, bf16[4,2,256,128]{3,2,1,0:T(8,128)(2,1)S(1)}, u32[]{:S(2)}) copy-start(bf16[4,2,256,128]{3,2,1,0:T(8,128)(2,1)S(1)} %get-tuple-element.33.refs_5_) | copy-start | bytes 1572868
  8.4 16.5 %collective-permute-start.1 = (bf16[4,2,256,128]{3,2,1,0:T(8,128)(2,1)}, bf16[4,2,256,128]{3,2,1,0:T(8,128)(2,1)}, u32[]{:S(2)}, u32[]{:S(2)}) collective-permute-start(bf16[4,2,256,128]{3,2,1,0:T(8,128)(2,1)} %copy-done.1), channel_id=1, source_target_pairs={{0,2},{1,3},{2,0},{3,1},{4,6},{5,7},{6,4},{7,5},{8,10},{9,11},{10,... | collective-permute-start | bytes 1572872 | tf_op jit(solution)/shard_map/ppermute | solution.py:343
  11.0 14.6 %collective-permute-start.3 = (bf16[4,2,256,128]{3,2,1,0:T(8,128)(2,1)}, bf16[4,2,256,128]{3,2,1,0:T(8,128)(2,1)}, u32[]{:S(2)}, u32[]{:S(2)}) collective-permute-start(bf16[4,2,256,128]{3,2,1,0:T(8,128)(2,1)} %copy-done.1), channel_id=1, source_target_pairs={{0,1},{1,0},{2,3},{3,2},{4,5},{5,4},{6,7},{7,6},{8,9},{9,8},{10,11... | collective-permute-start | bytes 1572872 | tf_op jit(solution)/shard_map/ppermute | solution.py:343
  12.5 14.8 %collective-permute-start.4 = (bf16[4,2,256,128]{3,2,1,0:T(8,128)(2,1)}, bf16[4,2,256,128]{3,2,1,0:T(8,128)(2,1)}, u32[]{:S(2)}, u32[]{:S(2)}) collective-permute-start(bf16[4,2,256,128]{3,2,1,0:T(8,128)(2,1)} %copy-done.1), channel_id=1, source_target_pairs={{0,4},{1,5},{2,6},{3,7},{4,0},{5,1},{6,2},{7,3},{8,12},{9,13},{10,... | collective-permute-start | bytes 1572872 | tf_op jit(solution)/shard_map/ppermute | solution.py:343
  14.4 8.4 %copy-start.4 = (s32[2]{0:T(128)S(1)}, s32[2]{0:T(128)}, u32[]{:S(2)}) copy-start(s32[2]{0:T(128)} %param.15) | copy-start | bytes 28
  21.3 7.5 %copy-start.2 = (bf16[4,2,256,128]{3,2,1,0:T(8,128)(2,1)S(1)}, bf16[4,2,256,128]{3,2,1,0:T(8,128)(2,1)}, u32[]{:S(2)}) copy-start(bf16[4,2,256,128]{3,2,1,0:T(8,128)(2,1)} %copy-done.1) | copy-start | bytes 1572868
  25.0 13.7 %collective-permute-start.2 = (bf16[4,2,256,128]{3,2,1,0:T(8,128)(2,1)}, bf16[4,2,256,128]{3,2,1,0:T(8,128)(2,1)S(1)}, u32[]{:S(2)}, u32[]{:S(2)}) collective-permute-start(bf16[4,2,256,128]{3,2,1,0:T(8,128)(2,1)} %collective-permute-done.1.refs_7_), channel_id=1, source_target_pairs={{0,1},{1,0},{2,3},{3,2},{4,5},{5,4},{6,7},{7,6},{8,9},{9,8},{10,11... | collective-permute-start | bytes 1572872 | tf_op jit(solution)/shard_map/ppermute | solution.py:343
  25.6 16.0 %collective-permute-start.8 = (bf16[4,2,256,128]{3,2,1,0:T(8,128)(2,1)}, bf16[4,2,256,128]{3,2,1,0:T(8,128)(2,1)S(1)}, u32[]{:S(2)}, u32[]{:S(2)}) collective-permute-start(bf16[4,2,256,128]{3,2,1,0:T(8,128)(2,1)} %collective-permute-done.3.refs_6_), channel_id=1, source_target_pairs={{0,4},{1,5},{2,6},{3,7},{4,0},{5,1},{6,2},{7,3},{8,12},{9,13},{10,... | collective-permute-start | bytes 1572872 | tf_op jit(solution)/shard_map/ppermute | solution.py:343
  27.3 13.2 %collective-permute-start.6 = (bf16[4,2,256,128]{3,2,1,0:T(8,128)(2,1)}, bf16[4,2,256,128]{3,2,1,0:T(8,128)(2,1)S(1)}, u32[]{:S(2)}, u32[]{:S(2)}) collective-permute-start(bf16[4,2,256,128]{3,2,1,0:T(8,128)(2,1)} %collective-permute-done.4.refs_8_), channel_id=1, source_target_pairs={{0,2},{1,3},{2,0},{3,1},{4,6},{5,7},{6,4},{7,5},{8,10},{9,11},{10,... | collective-permute-start | bytes 1572872 | tf_op jit(solution)/shard_map/ppermute | solution.py:343
  28.8 21.3 %slice-start = ((s8[16777216]{0:T(1024)(128)(4,1)}), s8[4194304]{0:T(1024)(128)(4,1)S(1)}, s32[]{:S(2)}) async-start(s8[16777216]{0:T(1024)(128)(4,1)} %bitcast.27), calls=%async_computation | async-start | bytes 8388608
  28.8 21.3 %slice-start.1 = ((s8[16777216]{0:T(1024)(128)(4,1)}), s8[4194304]{0:T(1024)(128)(4,1)S(1)}, s32[]{:S(2)}) async-start(s8[16777216]{0:T(1024)(128)(4,1)} %bitcast.27), calls=%async_computation.1 | async-start | bytes 8388608
  38.8 9.0 %collective-permute-start.5 = (bf16[1024,128]{1,0:T(8,128)(2,1)S(1)}, bf16[1024,128]{1,0:T(8,128)(2,1)S(1)}, u32[]{:S(2)}, u32[]{:S(2)}) collective-permute-start(bf16[1024,128]{1,0:T(8,128)(2,1)S(1)} %bitcast_select_fusion), channel_id=1, source_target_pairs={{0,4},{1,5},{2,6},{3,7},{4,8},{5,1},{6,2},{7,3},{8,12},{9,13},{10,... | collective-permute-start | bytes 786440 | tf_op jit(solution)/shard_map/ppermute | solution.py:366
  40.4 7.4 %collective-permute-start.7 = (bf16[1,2,256,128]{3,2,1,0:T(8,128)(2,1)S(1)}, bf16[1,2,256,128]{3,2,1,0:T(8,128)(2,1)S(1)}, u32[]{:S(2)}, u32[]{:S(2)}) collective-permute-start(bf16[1,2,256,128]{3,2,1,0:T(8,128)(2,1)S(1)} %slice.10), channel_id=1, source_target_pairs={{0,1},{1,0},{2,3},{3,2},{4,5},{5,4},{6,7},{7,6},{8,9},{9,8},{10,11... | collective-permute-start | bytes 393224 | tf_op jit(solution)/shard_map/ppermute | solution.py:343
  41.7 8.4 %slice-start.2 = ((s8[16777216]{0:T(1024)(128)(4,1)}), s8[4194304]{0:T(1024)(128)(4,1)S(1)}, s32[]{:S(2)}) async-start(s8[16777216]{0:T(1024)(128)(4,1)} %bitcast.27), calls=%async_computation.2 | async-start | bytes 8388608
  41.7 6.1 %collective-permute-start.9 = (bf16[1,2,256,128]{3,2,1,0:T(8,128)(2,1)S(1)}, bf16[1,2,256,128]{3,2,1,0:T(8,128)(2,1)S(1)}, u32[]{:S(2)}, u32[]{:S(2)}) collective-permute-start(bf16[1,2,256,128]{3,2,1,0:T(8,128)(2,1)S(1)} %slice.11), channel_id=1, source_target_pairs={{0,2},{1,3},{2,0},{3,1},{4,6},{5,7},{6,4},{7,5},{8,10},{9,11},{10,... | collective-permute-start | bytes 393224 | tf_op jit(solution)/shard_map/ppermute | solution.py:343
  47.8 2.3 %slice-start.3 = ((s8[16777216]{0:T(1024)(128)(4,1)}), s8[4194304]{0:T(1024)(128)(4,1)S(1)}, s32[]{:S(2)}) async-start(s8[16777216]{0:T(1024)(128)(4,1)} %bitcast.27), calls=%async_computation.3 | async-start | bytes 8388608
  52.5 2.7 %collective-permute-start.10 = (bf16[128,4096]{1,0:T(8,128)(2,1)S(1)}, bf16[128,4096]{1,0:T(8,128)(2,1)S(1)}, u32[]{:S(2)}, u32[]{:S(2)}) collective-permute-start(bf16[128,4096]{1,0:T(8,128)(2,1)S(1)} %project_out.2), channel_id=1, source_target_pairs={{0,16},{16,0},{1,17},{17,1},{2,18},{18,2},{3,19},{19,3},{4,20},{20... | collective-permute-start | bytes 3145736 | tf_op jit(solution)/shard_map/ppermute | solution.py:329
  52.6 2.6 %copy-start = (bf16[128,4096]{1,0:T(8,128)(2,1)S(1)}, bf16[128,4096]{1,0:T(8,128)(2,1)}, u32[]{:S(2)}) copy-start(bf16[128,4096]{1,0:T(8,128)(2,1)} %tokens_ref.1) | copy-start | bytes 3145732

commit v7 on v6

--- a/solution.py
+++ b/solution.py
@@ -75,7 +75,7 @@
 
 
 def stage_kernel(
-    tokens_hbm, gain_hbm, wk_hbm, wv_hbm, normed_ref, gain_ref, wk_ref, wv_ref, x_ref, sems
+    tokens_hbm, gain_hbm, wk_hbm, wv_hbm, normed_ref, gain_ref, wk_ref, wv_ref, own_ref, x_ref, sems
 ):
     pairs = ((tokens_hbm, x_ref), (gain_hbm, gain_ref), (wk_hbm, wk_ref), (wv_hbm, wv_ref))
     copies = [pltpu.make_async_copy(*pair, sems.at[n]) for n, pair in enumerate(pairs)]
@@ -84,8 +84,11 @@
     copies[0].wait()
     copies[1].wait()
     norm_rows(x_ref, gain_ref, normed_ref)
-    copies[2].wait()
-    copies[3].wait()
+    for which, ref in enumerate((wk_ref, wv_ref)):
+        copies[2 + which].wait()
+        part = jnp.dot(normed_ref[...], ref[...], preferred_element_type=jnp.float32)
+        for head in range(own_ref.shape[0]):
+            own_ref[head, which] = part[:, head * HD : (head + 1) * HD].astype(own_ref.dtype)
 
 
 def stage(tokens, gain, w_key, w_value):
@@ -94,7 +97,8 @@
         stage_kernel,
         "stage",
         (tokens, gain, w_key, w_value),
-        [jax.ShapeDtypeStruct(a.shape, a.dtype) for a in (tokens, gain, w_key, w_value)],
+        [jax.ShapeDtypeStruct(a.shape, a.dtype) for a in (tokens, gain, w_key, w_value)]
+        + [jax.ShapeDtypeStruct((w_key.shape[1] // HD, 2, tokens.shape[0], HD), jnp.bfloat16)],
         4 * tokens.size,
         scratch=[pltpu.VMEM(tokens.shape, tokens.dtype), pltpu.SemaphoreType.DMA((4,))],
         in_specs=[IN_PLACE] * 4,
@@ -103,24 +107,26 @@
 
 def project_kv_kernel(own_ref, other_ref, gain_ref, wk_ref, wv_ref, normed_ref, kv_ref):
     norm_rows(other_ref, gain_ref, normed_ref)
-    rows = jnp.concatenate([own_ref[...], normed_ref[...]], axis=0)
+    half = other_ref.shape[0]
+    kv_ref[:, :, :half] = own_ref[...]
     for head in range(kv_ref.shape[0]):
         cols = slice(head * HD, (head + 1) * HD)
         weights = jnp.concatenate([wk_ref[:, cols], wv_ref[:, cols]], axis=1)
-        pair = jnp.dot(rows, weights, preferred_element_type=jnp.float32).astype(jnp.bfloat16)
-        kv_ref[head, 0] = pair[:, :HD]
-        kv_ref[head, 1] = pair[:, HD:]
-
-
-def project_kv(normed, other_tokens, gain, w_key, w_value):
-    half, width = normed.shape
+        pair = jnp.dot(normed_ref[...], weights, preferred_element_type=jnp.float32)
+        pair = pair.astype(jnp.bfloat16)
+        kv_ref[head, 0, half:] = pair[:, :HD]
+        kv_ref[head, 1, half:] = pair[:, HD:]
+
+
+def project_kv(own_part, other_tokens, gain, w_key, w_value):
+    half, width = other_tokens.shape
     heads = w_key.shape[1] // HD
     outs = [
         jax.ShapeDtypeStruct((half, width), jnp.bfloat16),
         jax.ShapeDtypeStruct((heads, 2, 2 * half, HD), jnp.bfloat16),
     ]
     flops = 8 * half * width * heads * HD
-    args = (normed, other_tokens, gain, w_key, w_value)
+    args = (own_part, other_tokens, gain, w_key, w_value)
     return call(project_kv_kernel, "project_kv", args, outs, flops)
 
 
@@ -391,9 +397,9 @@
     reach = min(8, count // 2 - 1)
 
     other_tokens = swap_cores(tokens)
-    normed, staged_gain, staged_key, staged_value = stage(tokens, gain, w_key, w_value)
+    normed, staged_gain, staged_key, staged_value, own_part = stage(tokens, gain, w_key, w_value)
     other_normed, own_block = project_kv(
-        normed, other_tokens, staged_gain, staged_key, staged_value
+        own_part, other_tokens, staged_gain, staged_key, staged_value
     )
     page_table, index, core = after((page_table, index, core), own_block)
 

time: 57 us -> 56.7 us (level)
  waiting for transfers between devices: 3.16 us -> 2.1 us
  local copies, waits for them, and re-layouts: 2.85 us -> 3.89 us
    ppermute x8, waiting for transfers between devices: 2.87 us -> 1.81 us  [exchange(): return lax.ppermute(value, 'seq', [(i, i ^ bit) for i in range(count)])]
    unnamed x18, local copies, waits for them, and re-layouts: 0.84 us -> 1.87 us
  transfers between devices with their start and end apart: 11 -> 11, of which waited for: 3 -> 3; matrix products, arithmetic and copies ran while one was open for 6% -> 6% of each run, Pallas kernels for 45% -> 46%
where the time goes in v7:
time: 56.7 us; the launch traced here: 56.4 us
  Pallas kernels  33.6 us (59%)
  starting transfers between devices  13.5 us (24%)
  local copies, waits for them, and re-layouts  3.89 us (7%)
  waiting for transfers between devices  2.1 us (4%)
  between operations  1.86 us (3%)
  other arithmetic  1.42 us (3%)
    pallas_call x9, Pallas kernels, call(): pl.pallas_call(kernel, in_specs=in_specs or [IN_VMEM] * len(args), out_sp...  33.6 us
    ppermute x8, starting transfers between devices, exchange(): return lax.ppermute(value, 'seq', [(i, i ^ bit) for i in range(count)])  11.9 us
    unnamed x18, local copies, waits for them, and re-layouts  1.87 us
    ppermute x8, waiting for transfers between devices, exchange(): return lax.ppermute(value, 'seq', [(i, i ^ bit) for i in range(count)])  1.81 us
  transfers between devices with their start and end apart: 11, of which 3 were waited for; matrix products, arithmetic and copies ran while one was open for 6% of the time, Pallas kernels for 46%

profile of v7, /device:TPU:0, one launch (start us, length us, event | category | flops | bytes accessed | tf_op | source)
XLA Modules:
  0.0 56.4 jit_solution(6802705611486118983)
XLA Ops:
  0.6 0.5 collective-permute-start
  1.1 4.5 %stage.1 = (bf16[128,4096]{1,0:T(8,128)(2,1)S(1)}, f32[1,4096]{1,0:T(1,128)S(1)}, bf16[4096,512]{1,0:T(8,128)(2,1)S(1)}, bf16[4096,512]{1,0:T(8,128)(2,1)S(1)}, bf16[4,2,128,128]{3,2,1,0:T(8,128)(2,1)S(1)}) custom-call(bf16[128,4096]{1,0:T(8,128)(2,1)} %tokens_ref.1, f32[1,4096]{1,0:T(1,128)} %bitcast.36, bf16[4096,512]{1,0:T(8,128)(2,1)} %wk_hbm.1, ...), custom_call_target="tpu_custom_call" | custom-call | flops 2097152 | bytes 19169280 | tf_op jit(solution)/shard_map/stage/pallas_call | solution.py:37
  5.7 0.0 collective-permute-done.other_ref
  5.7 0.0 copy-start.3
  5.7 1.6 %project_kv.1 = (bf16[128,4096]{1,0:T(8,128)(2,1)S(1)}, bf16[4,2,256,128]{3,2,1,0:T(8,128)(2,1)S(1)}) custom-call(bf16[4,2,128,128]{3,2,1,0:T(8,128)(2,1)S(1)} %get-tuple-element.30.own_ref, bf16[128,4096]{1,0:T(8,128)(2,1)S(1)} %collective-permute-done.other_ref, f32[1,4096]{1,0:T(1,128)S(1)} %get-tuple-element.31.gain_ref, ...), custom_call_target="tpu_custom_call" | custom-call | flops 2147483648 | bytes 11288576 | tf_op jit(solution)/shard_map/project_kv/pallas_call | solution.py:37
  7.3 0.0 copy-start.1
  7.3 0.8 %copy-done.1 = bf16[4,2,256,128]{3,2,1,0:T(8,128)(2,1)} copy-done((bf16[4,2,256,128]{3,2,1,0:T(8,128)(2,1)}, bf16[4,2,256,128]{3,2,1,0:T(8,128)(2,1)S(1)}, u32[]{:S(2)}) %copy-start.1) | copy-done | bytes 524312
  8.1 2.5 %collective-permute-start.1 = (bf16[4,2,256,128]{3,2,1,0:T(8,128)(2,1)}, bf16[4,2,256,128]{3,2,1,0:T(8,128)(2,1)}, u32[]{:S(2)}, u32[]{:S(2)}) collective-permute-start(bf16[4,2,256,128]{3,2,1,0:T(8,128)(2,1)} %copy-done.1), channel_id=1, source_target_pairs={{0,2},{1,3},{2,0},{3,1},{4,6},{5,7},{6,4},{7,5},{8,10},{9,11},{10,... | collective-permute-start | bytes 1572872 | tf_op jit(solution)/shard_map/ppermute | solution.py:349
  10.6 1.5 %collective-permute-start.3 = (bf16[4,2,256,128]{3,2,1,0:T(8,128)(2,1)}, bf16[4,2,256,128]{3,2,1,0:T(8,128)(2,1)}, u32[]{:S(2)}, u32[]{:S(2)}) collective-permute-start(bf16[4,2,256,128]{3,2,1,0:T(8,128)(2,1)} %copy-done.1), channel_id=1, source_target_pairs={{0,1},{1,0},{2,3},{3,2},{4,5},{5,4},{6,7},{7,6},{8,9},{9,8},{10,11... | collective-permute-start | bytes 1572872 | tf_op jit(solution)/shard_map/ppermute | solution.py:349
  12.1 1.6 %collective-permute-start.4 = (bf16[4,2,256,128]{3,2,1,0:T(8,128)(2,1)}, bf16[4,2,256,128]{3,2,1,0:T(8,128)(2,1)}, u32[]{:S(2)}, u32[]{:S(2)}) collective-permute-start(bf16[4,2,256,128]{3,2,1,0:T(8,128)(2,1)} %copy-done.1), channel_id=1, source_target_pairs={{0,4},{1,5},{2,6},{3,7},{4,0},{5,1},{6,2},{7,3},{8,12},{9,13},{10,... | collective-permute-start | bytes 1572872 | tf_op jit(solution)/shard_map/ppermute | solution.py:349
  13.7 0.0 copy-done.3
  13.7 0.1 fusion.5
  13.9 0.1 copy.16
  14.1 0.0 copy-start.4
  14.2 6.9 %project_query.1.refs_4_ = bf16[256,2048]{1,0:T(8,128)(2,1)S(1)} custom-call(bf16[128,4096]{1,0:T(8,128)(2,1)S(1)} %get-tuple-element.37.own_ref, bf16[128,4096]{1,0:T(8,128)(2,1)S(1)} %get-tuple-element.38.other_ref, bf16[4096,2048]{1,0:T(8,128)(2,1)} %w_hbm.1), custom_call_target="tpu_custom_call" | custom-call | flops 4294967296 | bytes 19922944 | tf_op jit(solution)/shard_map/project_query/pallas_call | solution.py:37
  21.2 0.1 copy.17
  21.3 1.1 %copy.20 = bf16[4,2,2,128,128]{4,3,0,1,2:T(8,128)(2,1)S(1)} copy(bf16[4,2,2,128,128]{4,3,2,1,0:T(8,128)(2,1)} %bitcast.29) | data formatting | bytes 1048576 | tf_op jit(solution)/shard_map/reshape | solution.py:440
  22.4 0.6 %dynamic_slice.75 = s32[1]{0:T(128)} dynamic-slice(s32[2]{0:T(128)S(1)} %copy-done.4, s32[]{:T(128)S(6)} %select_n.222), dynamic_slice_sizes={1} | dynamic-slice | bytes 12 | tf_op jit(solution)/shard_map/jit(dynamic_index_in_dim)/dynamic_slice | solution.py:441
  23.7 0.9 %reverse_select_fusion = bf16[2,2,4,128,128]{4,3,2,1,0:T(8,128)(2,1)} fusion(bf16[2,2,4,128,128]{4,3,2,1,0:T(8,128)(2,1)S(1)} %bitcast.33, pred[]{:T(512)} %bitcast.11), kind=kLoop, calls=%fused_computation | loop fusion | flops 262144 | bytes 1048577 | tf_op jit(solution)/shard_map/jit(_where)/select_n | solution.py:442
  24.6 0.0 collective-permute-done.1.refs_7_
  24.6 0.6 %collective-permute-start.2 = (bf16[4,2,256,128]{3,2,1,0:T(8,128)(2,1)}, bf16[4,2,256,128]{3,2,1,0:T(8,128)(2,1)S(1)}, u32[]{:S(2)}, u32[]{:S(2)}) collective-permute-start(bf16[4,2,256,128]{3,2,1,0:T(8,128)(2,1)} %collective-permute-done.1.refs_7_), channel_id=1, source_target_pairs={{0,1},{1,0},{2,3},{3,2},{4,5},{5,4},{6,7},{7,6},{8,9},{9,8},{10,11... | collective-permute-start | bytes 1572872 | tf_op jit(solution)/shard_map/ppermute | solution.py:349
  25.2 0.0 collective-permute-done.3.refs_6_
  25.3 1.6 %collective-permute-start.8 = (bf16[4,2,256,128]{3,2,1,0:T(8,128)(2,1)}, bf16[4,2,256,128]{3,2,1,0:T(8,128)(2,1)S(1)}, u32[]{:S(2)}, u32[]{:S(2)}) collective-permute-start(bf16[4,2,256,128]{3,2,1,0:T(8,128)(2,1)} %collective-permute-done.3.refs_6_), channel_id=1, source_target_pairs={{0,4},{1,5},{2,6},{3,7},{4,0},{5,1},{6,2},{7,3},{8,12},{9,13},{10,... | collective-permute-start | bytes 1572872 | tf_op jit(solution)/shard_map/ppermute | solution.py:349
  26.9 0.0 collective-permute-done.4.refs_8_
  26.9 1.5 %collective-permute-start.6 = (bf16[4,2,256,128]{3,2,1,0:T(8,128)(2,1)}, bf16[4,2,256,128]{3,2,1,0:T(8,128)(2,1)S(1)}, u32[]{:S(2)}, u32[]{:S(2)}) collective-permute-start(bf16[4,2,256,128]{3,2,1,0:T(8,128)(2,1)} %collective-permute-done.4.refs_8_), channel_id=1, source_target_pairs={{0,2},{1,3},{2,0},{3,1},{4,6},{5,7},{6,4},{7,5},{8,10},{9,11},{10,... | collective-permute-start | bytes 1572872 | tf_op jit(solution)/shard_map/ppermute | solution.py:349
  28.4 1.0 %copy-done.2 = bf16[4,2,256,128]{3,2,1,0:T(8,128)(2,1)S(1)} copy-done((bf16[4,2,256,128]{3,2,1,0:T(8,128)(2,1)S(1)}, bf16[4,2,256,128]{3,2,1,0:T(8,128)(2,1)}, u32[]{:S(2)}) %copy-start.2) | copy-done | bytes 524312
  29.5 7.6 %attend.3 = (f32[256,2048]{1,0:T(8,128)S(1)}, f32[256,2048]{1,0:T(8,128)S(1)}, f32[256,2048]{1,0:T(8,128)S(1)}) custom-call(s32[256,1]{1,0:T(8,128)S(1)} %broadcast_select_fusion.refs_0_, s32[256,1]{1,0:T(8,128)S(1)} %broadcast_add_fusion.refs_1_, s32[1,1024]{1,0:T(1,128)S(1)} %bitcast.32, s32[1,1024]{1,0:T(1,128)S(1)} %bitcast.31, ...), custom_call_target="tpu_custom_call" | custom-call | flops 3221225472 | bytes 9447424 | tf_op jit(solution)/shard_map/attend/pallas_call | solution.py:37
  37.1 1.1 %collective-permute-done.2.refs_5_ = bf16[4,2,256,128]{3,2,1,0:T(8,128)(2,1)S(1)} collective-permute-done((bf16[4,2,256,128]{3,2,1,0:T(8,128)(2,1)}, bf16[4,2,256,128]{3,2,1,0:T(8,128)(2,1)S(1)}, u32[]{:S(2)}, u32[]{:S(2)}) %collective-permute-start.2) | collective-permute-done | bytes 524320 | tf_op jit(solution)/shard_map/ppermute | solution.py:349
  38.3 0.1 bitcast_select_fusion
  38.4 1.0 %collective-permute-start.5 = (bf16[1024,128]{1,0:T(8,128)(2,1)S(1)}, bf16[1024,128]{1,0:T(8,128)(2,1)S(1)}, u32[]{:S(2)}, u32[]{:S(2)}) collective-permute-start(bf16[1024,128]{1,0:T(8,128)(2,1)S(1)} %bitcast_select_fusion), channel_id=1, source_target_pairs={{0,4},{1,5},{2,6},{3,7},{4,8},{5,1},{6,2},{7,3},{8,12},{9,13},{10,... | collective-permute-start | bytes 786440 | tf_op jit(solution)/shard_map/ppermute | solution.py:372
  39.4 0.6 %collective-permute-done.6.refs_6_ = bf16[4,2,256,128]{3,2,1,0:T(8,128)(2,1)S(1)} collective-permute-done((bf16[4,2,256,128]{3,2,1,0:T(8,128)(2,1)}, bf16[4,2,256,128]{3,2,1,0:T(8,128)(2,1)S(1)}, u32[]{:S(2)}, u32[]{:S(2)}) %collective-permute-start.6) | collective-permute-done | bytes 524320 | tf_op jit(solution)/shard_map/ppermute | solution.py:349
  40.1 1.2 %collective-permute-start.7 = (bf16[1,2,256,128]{3,2,1,0:T(8,128)(2,1)S(1)}, bf16[1,2,256,128]{3,2,1,0:T(8,128)(2,1)S(1)}, u32[]{:S(2)}, u32[]{:S(2)}) collective-permute-start(bf16[1,2,256,128]{3,2,1,0:T(8,128)(2,1)S(1)} %slice.10), channel_id=1, source_target_pairs={{0,1},{1,0},{2,3},{3,2},{4,5},{5,4},{6,7},{7,6},{8,9},{9,8},{10,11... | collective-permute-start | bytes 393224 | tf_op jit(solution)/shard_map/ppermute | solution.py:349
  41.3 0.0 collective-permute-done.8.refs_7_
  41.3 0.0 slice-start.2
  41.3 1.3 %collective-permute-start.9 = (bf16[1,2,256,128]{3,2,1,0:T(8,128)(2,1)S(1)}, bf16[1,2,256,128]{3,2,1,0:T(8,128)(2,1)S(1)}, u32[]{:S(2)}, u32[]{:S(2)}) collective-permute-start(bf16[1,2,256,128]{3,2,1,0:T(8,128)(2,1)S(1)} %slice.11), channel_id=1, source_target_pairs={{0,2},{1,3},{2,0},{3,1},{4,6},{5,7},{6,4},{7,5},{8,10},{9,11},{10,... | collective-permute-start | bytes 393224 | tf_op jit(solution)/shard_map/ppermute | solution.py:349
  42.6 4.8 %attend.4 = (f32[256,2048]{1,0:T(8,128)S(1)}, f32[256,2048]{1,0:T(8,128)S(1)}, f32[256,2048]{1,0:T(8,128)S(1)}) custom-call(s32[256,1]{1,0:T(8,128)S(1)} %broadcast_select_fusion.refs_0_, s32[256,1]{1,0:T(8,128)S(1)} %broadcast_add_fusion.refs_1_, s32[1,768]{1,0:T(1,128)S(1)} %broadcast_in_dim.53.refs_2_, s32[1,768]{1,0:T(1,128)S(1)} %broadcast_in_dim.54.refs_3_, ...), custom_call_target="tpu_custom_call" | custom-call | flops 2415919104 | bytes 15212544 | tf_op jit(solution)/shard_map/attend/pallas_call | solution.py:37
  47.4 0.0 collective-permute-done.7
  47.4 0.0 collective-permute-done.9
  47.5 0.0 collective-permute-done.5
  47.5 0.0 slice-start.3
  47.5 0.1 maximum_select_fusion.refs_5_
  47.6 2.1 %attend.5 = (bf16[128,2048]{1,0:T(8,128)(2,1)S(1)}, bf16[128,2048]{1,0:T(8,128)(2,1)S(1)}) custom-call(s32[256,1]{1,0:T(8,128)S(1)} %broadcast_select_fusion.refs_0_, s32[256,1]{1,0:T(8,128)S(1)} %broadcast_add_fusion.refs_1_, s32[1,256]{1,0:T(1,128)S(1)} %bitcast.30, s32[1,256]{1,0:T(1,128)S(1)} %broadcast_select_fusion.1.refs_3_, ...), custom_call_target="tpu_custom_call" | custom-call | flops 805306368 | bytes 8916992 | tf_op jit(solution)/shard_map/attend/pallas_call | solution.py:37
  49.8 2.3 %project_out.2 = bf16[128,4096]{1,0:T(8,128)(2,1)S(1)} custom-call(bf16[128,2048]{1,0:T(8,128)(2,1)S(1)} %get-tuple-element.53.x_ref, bf16[2048,4096]{1,0:T(8,128)(2,1)S(1)} %bitcast.28), custom_call_target="tpu_custom_call" | custom-call | flops 2147483648 | bytes 18350080 | tf_op jit(solution)/shard_map/project_out/pallas_call | solution.py:37
  52.1 0.1 collective-permute-start.10
  52.2 0.0 copy-start
  52.2 2.3 %project_out.3.refs_0_ = f32[128,4096]{1,0:T(8,128)S(1)} custom-call(bf16[128,2048]{1,0:T(8,128)(2,1)S(1)} %get-tuple-element.54.x_ref, bf16[2048,4096]{1,0:T(8,128)(2,1)S(1)} %bitcast.28), custom_call_target="tpu_custom_call" | custom-call | flops 2147483648 | bytes 19398656 | tf_op jit(solution)/shard_map/project_out/pallas_call | solution.py:37
  54.6 0.3 collective-permute-done.10.refs_1_
  54.8 1.4 %finish.1 = (bf16[128,4096]{1,0:T(8,128)(2,1)}, bf16[128,4096]{1,0:T(8,128)(2,1)}) custom-call(bf16[128,4096]{1,0:T(8,128)(2,1)S(1)} %copy-done, f32[128,4096]{1,0:T(8,128)S(1)} %project_out.3.refs_0_, bf16[128,4096]{1,0:T(8,128)(2,1)S(1)} %collective-permute-done.10.refs_1_), custom_call_target="tpu_custom_call" | custom-call | flops 1048576 | bytes 6291456 | tf_op jit(solution)/shard_map/finish/pallas_call | solution.py:37
  (36 shorter events, 0.2 us)
Async XLA Ops:
  0.6 5.1 %collective-permute-start = (bf16[128,4096]{1,0:T(8,128)(2,1)}, bf16[128,4096]{1,0:T(8,128)(2,1)S(1)}, u32[]{:S(2)}, u32[]{:S(2)}) collective-permute-start(bf16[128,4096]{1,0:T(8,128)(2,1)} %tokens_ref.1), channel_id=1, source_target_pairs={{0,16},{16,0},{1,17},{17,1},{2,18},{18,2},{3,19},{19,3},{4,20},{20... | collective-permute-start | bytes 3145736 | tf_op jit(solution)/shard_map/ppermute | solution.py:335
  5.7 8.0 %copy-start.3 = (s32[4096]{0:T(1024)S(1)}, s32[4096]{0:T(1024)}, u32[]{:S(2)}) copy-start(s32[4096]{0:T(1024)} %param.14) | copy-start | bytes 49156
  7.3 0.8 %copy-start.1 = (bf16[4,2,256,128]{3,2,1,0:T(8,128)(2,1)}, bf16[4,2,256,128]{3,2,1,0:T(8,128)(2,1)S(1)}, u32[]{:S(2)}) copy-start(bf16[4,2,256,128]{3,2,1,0:T(8,128)(2,1)S(1)} %get-tuple-element.34.refs_5_) | copy-start | bytes 1572868
  8.1 16.5 %collective-permute-start.1 = (bf16[4,2,256,128]{3,2,1,0:T(8,128)(2,1)}, bf16[4,2,256,128]{3,2,1,0:T(8,128)(2,1)}, u32[]{:S(2)}, u32[]{:S(2)}) collective-permute-start(bf16[4,2,256,128]{3,2,1,0:T(8,128)(2,1)} %copy-done.1), channel_id=1, source_target_pairs={{0,2},{1,3},{2,0},{3,1},{4,6},{5,7},{6,4},{7,5},{8,10},{9,11},{10,... | collective-permute-start | bytes 1572872 | tf_op jit(solution)/shard_map/ppermute | solution.py:349
  10.6 14.6 %collective-permute-start.3 = (bf16[4,2,256,128]{3,2,1,0:T(8,128)(2,1)}, bf16[4,2,256,128]{3,2,1,0:T(8,128)(2,1)}, u32[]{:S(2)}, u32[]{:S(2)}) collective-permute-start(bf16[4,2,256,128]{3,2,1,0:T(8,128)(2,1)} %copy-done.1), channel_id=1, source_target_pairs={{0,1},{1,0},{2,3},{3,2},{4,5},{5,4},{6,7},{7,6},{8,9},{9,8},{10,11... | collective-permute-start | bytes 1572872 | tf_op jit(solution)/shard_map/ppermute | solution.py:349
  12.1 14.8 %collective-permute-start.4 = (bf16[4,2,256,128]{3,2,1,0:T(8,128)(2,1)}, bf16[4,2,256,128]{3,2,1,0:T(8,128)(2,1)}, u32[]{:S(2)}, u32[]{:S(2)}) collective-permute-start(bf16[4,2,256,128]{3,2,1,0:T(8,128)(2,1)} %copy-done.1), channel_id=1, source_target_pairs={{0,4},{1,5},{2,6},{3,7},{4,0},{5,1},{6,2},{7,3},{8,12},{9,13},{10,... | collective-permute-start | bytes 1572872 | tf_op jit(solution)/shard_map/ppermute | solution.py:349
  14.1 8.3 %copy-start.4 = (s32[2]{0:T(128)S(1)}, s32[2]{0:T(128)}, u32[]{:S(2)}) copy-start(s32[2]{0:T(128)} %param.15) | copy-start | bytes 28
  24.6 13.7 %collective-permute-start.2 = (bf16[4,2,256,128]{3,2,1,0:T(8,128)(2,1)}, bf16[4,2,256,128]{3,2,1,0:T(8,128)(2,1)S(1)}, u32[]{:S(2)}, u32[]{:S(2)}) collective-permute-start(bf16[4,2,256,128]{3,2,1,0:T(8,128)(2,1)} %collective-permute-done.1.refs_7_), channel_id=1, source_target_pairs={{0,1},{1,0},{2,3},{3,2},{4,5},{5,4},{6,7},{7,6},{8,9},{9,8},{10,11... | collective-permute-start | bytes 1572872 | tf_op jit(solution)/shard_map/ppermute | solution.py:349
  25.3 16.0 %collective-permute-start.8 = (bf16[4,2,256,128]{3,2,1,0:T(8,128)(2,1)}, bf16[4,2,256,128]{3,2,1,0:T(8,128)(2,1)S(1)}, u32[]{:S(2)}, u32[]{:S(2)}) collective-permute-start(bf16[4,2,256,128]{3,2,1,0:T(8,128)(2,1)} %collective-permute-done.3.refs_6_), channel_id=1, source_target_pairs={{0,4},{1,5},{2,6},{3,7},{4,0},{5,1},{6,2},{7,3},{8,12},{9,13},{10,... | collective-permute-start | bytes 1572872 | tf_op jit(solution)/shard_map/ppermute | solution.py:349
  26.9 13.2 %collective-permute-start.6 = (bf16[4,2,256,128]{3,2,1,0:T(8,128)(2,1)}, bf16[4,2,256,128]{3,2,1,0:T(8,128)(2,1)S(1)}, u32[]{:S(2)}, u32[]{:S(2)}) collective-permute-start(bf16[4,2,256,128]{3,2,1,0:T(8,128)(2,1)} %collective-permute-done.4.refs_8_), channel_id=1, source_target_pairs={{0,2},{1,3},{2,0},{3,1},{4,6},{5,7},{6,4},{7,5},{8,10},{9,11},{10,... | collective-permute-start | bytes 1572872 | tf_op jit(solution)/shard_map/ppermute | solution.py:349
  28.4 1.0 %copy-start.2 = (bf16[4,2,256,128]{3,2,1,0:T(8,128)(2,1)S(1)}, bf16[4,2,256,128]{3,2,1,0:T(8,128)(2,1)}, u32[]{:S(2)}) copy-start(bf16[4,2,256,128]{3,2,1,0:T(8,128)(2,1)} %copy-done.1) | copy-start | bytes 1572868
  29.5 20.2 %slice-start = ((s8[16777216]{0:T(1024)(128)(4,1)}), s8[4194304]{0:T(1024)(128)(4,1)S(1)}, s32[]{:S(2)}) async-start(s8[16777216]{0:T(1024)(128)(4,1)} %bitcast.27), calls=%async_computation | async-start | bytes 8388608
  29.5 20.3 %slice-start.1 = ((s8[16777216]{0:T(1024)(128)(4,1)}), s8[4194304]{0:T(1024)(128)(4,1)S(1)}, s32[]{:S(2)}) async-start(s8[16777216]{0:T(1024)(128)(4,1)} %bitcast.27), calls=%async_computation.1 | async-start | bytes 8388608
  38.4 9.1 %collective-permute-start.5 = (bf16[1024,128]{1,0:T(8,128)(2,1)S(1)}, bf16[1024,128]{1,0:T(8,128)(2,1)S(1)}, u32[]{:S(2)}, u32[]{:S(2)}) collective-permute-start(bf16[1024,128]{1,0:T(8,128)(2,1)S(1)} %bitcast_select_fusion), channel_id=1, source_target_pairs={{0,4},{1,5},{2,6},{3,7},{4,8},{5,1},{6,2},{7,3},{8,12},{9,13},{10,... | collective-permute-start | bytes 786440 | tf_op jit(solution)/shard_map/ppermute | solution.py:372
  40.1 7.3 %collective-permute-start.7 = (bf16[1,2,256,128]{3,2,1,0:T(8,128)(2,1)S(1)}, bf16[1,2,256,128]{3,2,1,0:T(8,128)(2,1)S(1)}, u32[]{:S(2)}, u32[]{:S(2)}) collective-permute-start(bf16[1,2,256,128]{3,2,1,0:T(8,128)(2,1)S(1)} %slice.10), channel_id=1, source_target_pairs={{0,1},{1,0},{2,3},{3,2},{4,5},{5,4},{6,7},{7,6},{8,9},{9,8},{10,11... | collective-permute-start | bytes 393224 | tf_op jit(solution)/shard_map/ppermute | solution.py:349
  41.3 8.4 %slice-start.2 = ((s8[16777216]{0:T(1024)(128)(4,1)}), s8[4194304]{0:T(1024)(128)(4,1)S(1)}, s32[]{:S(2)}) async-start(s8[16777216]{0:T(1024)(128)(4,1)} %bitcast.27), calls=%async_computation.2 | async-start | bytes 8388608
  41.3 6.1 %collective-permute-start.9 = (bf16[1,2,256,128]{3,2,1,0:T(8,128)(2,1)S(1)}, bf16[1,2,256,128]{3,2,1,0:T(8,128)(2,1)S(1)}, u32[]{:S(2)}, u32[]{:S(2)}) collective-permute-start(bf16[1,2,256,128]{3,2,1,0:T(8,128)(2,1)S(1)} %slice.11), channel_id=1, source_target_pairs={{0,2},{1,3},{2,0},{3,1},{4,6},{5,7},{6,4},{7,5},{8,10},{9,11},{10,... | collective-permute-start | bytes 393224 | tf_op jit(solution)/shard_map/ppermute | solution.py:349
  47.5 2.3 %slice-start.3 = ((s8[16777216]{0:T(1024)(128)(4,1)}), s8[4194304]{0:T(1024)(128)(4,1)S(1)}, s32[]{:S(2)}) async-start(s8[16777216]{0:T(1024)(128)(4,1)} %bitcast.27), calls=%async_computation.3 | async-start | bytes 8388608
  52.1 2.7 %collective-permute-start.10 = (bf16[128,4096]{1,0:T(8,128)(2,1)S(1)}, bf16[128,4096]{1,0:T(8,128)(2,1)S(1)}, u32[]{:S(2)}, u32[]{:S(2)}) collective-permute-start(bf16[128,4096]{1,0:T(8,128)(2,1)S(1)} %project_out.2), channel_id=1, source_target_pairs={{0,16},{16,0},{1,17},{17,1},{2,18},{18,2},{3,19},{19,3},{4,20},{20... | collective-permute-start | bytes 3145736 | tf_op jit(solution)/shard_map/ppermute | solution.py:335
  52.2 2.6 %copy-start = (bf16[128,4096]{1,0:T(8,128)(2,1)S(1)}, bf16[128,4096]{1,0:T(8,128)(2,1)}, u32[]{:S(2)}) copy-start(bf16[128,4096]{1,0:T(8,128)(2,1)} %tokens_ref.1) | copy-start | bytes 3145732

commit v8 on v7

--- a/solution.py
+++ b/solution.py
@@ -236,8 +236,8 @@
             mass_out[:, cols[head]] = mass
 
     if last:
-        for start in range(0, heads, 8):
-            many = range(start, start + 8)
+        for start in range(0, heads, heads):
+            many = range(start, start + heads)
             scores = [score(head) for head in many]
             weighed = [weigh(head, scores[head - start]) for head in many]
             for head in many:

time: 56.7 us -> 56.7 us (level)
  no operation moved by 1% of the time
where the time goes in v8:
time: 56.7 us; the launch traced here: 56.5 us
  Pallas kernels  33.7 us (59%)
  starting transfers between devices  13.5 us (24%)
  local copies, waits for them, and re-layouts  3.89 us (7%)
  waiting for transfers between devices  2.1 us (4%)
  between operations  1.86 us (3%)
  other arithmetic  1.42 us (3%)
    pallas_call x9, Pallas kernels, call(): pl.pallas_call(kernel, in_specs=in_specs or [IN_VMEM] * len(args), out_sp...  33.7 us
    ppermute x8, starting transfers between devices, exchange(): return lax.ppermute(value, 'seq', [(i, i ^ bit) for i in range(count)])  11.9 us
    unnamed x18, local copies, waits for them, and re-layouts  1.87 us
    ppermute x8, waiting for transfers between devices, exchange(): return lax.ppermute(value, 'seq', [(i, i ^ bit) for i in range(count)])  1.81 us
  transfers between devices with their start and end apart: 11, of which 3 were waited for; matrix products, arithmetic and copies ran while one was open for 6% of the time, Pallas kernels for 46%

profile of v8, /device:TPU:0, one launch (start us, length us, event | category | flops | bytes accessed | tf_op | source)
XLA Modules:
  0.0 56.5 jit_solution(5147202267544509313)
XLA Ops:
  0.6 0.5 collective-permute-start
  1.1 4.5 %stage.1 = (bf16[128,4096]{1,0:T(8,128)(2,1)S(1)}, f32[1,4096]{1,0:T(1,128)S(1)}, bf16[4096,512]{1,0:T(8,128)(2,1)S(1)}, bf16[4096,512]{1,0:T(8,128)(2,1)S(1)}, bf16[4,2,128,128]{3,2,1,0:T(8,128)(2,1)S(1)}) custom-call(bf16[128,4096]{1,0:T(8,128)(2,1)} %tokens_ref.1, f32[1,4096]{1,0:T(1,128)} %bitcast.36, bf16[4096,512]{1,0:T(8,128)(2,1)} %wk_hbm.1, ...), custom_call_target="tpu_custom_call" | custom-call | flops 2097152 | bytes 19169280 | tf_op jit(solution)/shard_map/stage/pallas_call | solution.py:37
  5.7 0.0 collective-permute-done.other_ref
  5.7 0.0 copy-start.3
  5.7 1.6 %project_kv.1 = (bf16[128,4096]{1,0:T(8,128)(2,1)S(1)}, bf16[4,2,256,128]{3,2,1,0:T(8,128)(2,1)S(1)}) custom-call(bf16[4,2,128,128]{3,2,1,0:T(8,128)(2,1)S(1)} %get-tuple-element.30.own_ref, bf16[128,4096]{1,0:T(8,128)(2,1)S(1)} %collective-permute-done.other_ref, f32[1,4096]{1,0:T(1,128)S(1)} %get-tuple-element.31.gain_ref, ...), custom_call_target="tpu_custom_call" | custom-call | flops 2147483648 | bytes 11288576 | tf_op jit(solution)/shard_map/project_kv/pallas_call | solution.py:37
  7.3 0.0 copy-start.1
  7.3 0.8 %copy-done.1 = bf16[4,2,256,128]{3,2,1,0:T(8,128)(2,1)} copy-done((bf16[4,2,256,128]{3,2,1,0:T(8,128)(2,1)}, bf16[4,2,256,128]{3,2,1,0:T(8,128)(2,1)S(1)}, u32[]{:S(2)}) %copy-start.1) | copy-done | bytes 524312
  8.1 2.5 %collective-permute-start.1 = (bf16[4,2,256,128]{3,2,1,0:T(8,128)(2,1)}, bf16[4,2,256,128]{3,2,1,0:T(8,128)(2,1)}, u32[]{:S(2)}, u32[]{:S(2)}) collective-permute-start(bf16[4,2,256,128]{3,2,1,0:T(8,128)(2,1)} %copy-done.1), channel_id=1, source_target_pairs={{0,2},{1,3},{2,0},{3,1},{4,6},{5,7},{6,4},{7,5},{8,10},{9,11},{10,... | collective-permute-start | bytes 1572872 | tf_op jit(solution)/shard_map/ppermute | solution.py:349
  10.6 1.5 %collective-permute-start.3 = (bf16[4,2,256,128]{3,2,1,0:T(8,128)(2,1)}, bf16[4,2,256,128]{3,2,1,0:T(8,128)(2,1)}, u32[]{:S(2)}, u32[]{:S(2)}) collective-permute-start(bf16[4,2,256,128]{3,2,1,0:T(8,128)(2,1)} %copy-done.1), channel_id=1, source_target_pairs={{0,1},{1,0},{2,3},{3,2},{4,5},{5,4},{6,7},{7,6},{8,9},{9,8},{10,11... | collective-permute-start | bytes 1572872 | tf_op jit(solution)/shard_map/ppermute | solution.py:349
  12.1 1.6 %collective-permute-start.4 = (bf16[4,2,256,128]{3,2,1,0:T(8,128)(2,1)}, bf16[4,2,256,128]{3,2,1,0:T(8,128)(2,1)}, u32[]{:S(2)}, u32[]{:S(2)}) collective-permute-start(bf16[4,2,256,128]{3,2,1,0:T(8,128)(2,1)} %copy-done.1), channel_id=1, source_target_pairs={{0,4},{1,5},{2,6},{3,7},{4,0},{5,1},{6,2},{7,3},{8,12},{9,13},{10,... | collective-permute-start | bytes 1572872 | tf_op jit(solution)/shard_map/ppermute | solution.py:349
  13.7 0.1 fusion.5
  13.9 0.1 copy.16
  14.1 0.0 copy-start.4
  14.2 6.9 %project_query.1.refs_4_ = bf16[256,2048]{1,0:T(8,128)(2,1)S(1)} custom-call(bf16[128,4096]{1,0:T(8,128)(2,1)S(1)} %get-tuple-element.37.own_ref, bf16[128,4096]{1,0:T(8,128)(2,1)S(1)} %get-tuple-element.38.other_ref, bf16[4096,2048]{1,0:T(8,128)(2,1)} %w_hbm.1), custom_call_target="tpu_custom_call" | custom-call | flops 4294967296 | bytes 19922944 | tf_op jit(solution)/shard_map/project_query/pallas_call | solution.py:37
  21.2 0.1 copy.17
  21.3 1.1 %copy.20 = bf16[4,2,2,128,128]{4,3,0,1,2:T(8,128)(2,1)S(1)} copy(bf16[4,2,2,128,128]{4,3,2,1,0:T(8,128)(2,1)} %bitcast.29) | data formatting | bytes 1048576 | tf_op jit(solution)/shard_map/reshape | solution.py:440
  22.4 0.6 %dynamic_slice.75 = s32[1]{0:T(128)} dynamic-slice(s32[2]{0:T(128)S(1)} %copy-done.4, s32[]{:T(128)S(6)} %select_n.222), dynamic_slice_sizes={1} | dynamic-slice | bytes 12 | tf_op jit(solution)/shard_map/jit(dynamic_index_in_dim)/dynamic_slice | solution.py:441
  23.7 0.9 %reverse_select_fusion = bf16[2,2,4,128,128]{4,3,2,1,0:T(8,128)(2,1)} fusion(bf16[2,2,4,128,128]{4,3,2,1,0:T(8,128)(2,1)S(1)} %bitcast.33, pred[]{:T(512)} %bitcast.11), kind=kLoop, calls=%fused_computation | loop fusion | flops 262144 | bytes 1048577 | tf_op jit(solution)/shard_map/jit(_where)/select_n | solution.py:442
  24.6 0.0 collective-permute-done.1.refs_7_
  24.6 0.6 %collective-permute-start.2 = (bf16[4,2,256,128]{3,2,1,0:T(8,128)(2,1)}, bf16[4,2,256,128]{3,2,1,0:T(8,128)(2,1)S(1)}, u32[]{:S(2)}, u32[]{:S(2)}) collective-permute-start(bf16[4,2,256,128]{3,2,1,0:T(8,128)(2,1)} %collective-permute-done.1.refs_7_), channel_id=1, source_target_pairs={{0,1},{1,0},{2,3},{3,2},{4,5},{5,4},{6,7},{7,6},{8,9},{9,8},{10,11... | collective-permute-start | bytes 1572872 | tf_op jit(solution)/shard_map/ppermute | solution.py:349
  25.2 0.0 collective-permute-done.3.refs_6_
  25.3 1.6 %collective-permute-start.8 = (bf16[4,2,256,128]{3,2,1,0:T(8,128)(2,1)}, bf16[4,2,256,128]{3,2,1,0:T(8,128)(2,1)S(1)}, u32[]{:S(2)}, u32[]{:S(2)}) collective-permute-start(bf16[4,2,256,128]{3,2,1,0:T(8,128)(2,1)} %collective-permute-done.3.refs_6_), channel_id=1, source_target_pairs={{0,4},{1,5},{2,6},{3,7},{4,0},{5,1},{6,2},{7,3},{8,12},{9,13},{10,... | collective-permute-start | bytes 1572872 | tf_op jit(solution)/shard_map/ppermute | solution.py:349
  26.9 0.0 collective-permute-done.4.refs_8_
  26.9 1.5 %collective-permute-start.6 = (bf16[4,2,256,128]{3,2,1,0:T(8,128)(2,1)}, bf16[4,2,256,128]{3,2,1,0:T(8,128)(2,1)S(1)}, u32[]{:S(2)}, u32[]{:S(2)}) collective-permute-start(bf16[4,2,256,128]{3,2,1,0:T(8,128)(2,1)} %collective-permute-done.4.refs_8_), channel_id=1, source_target_pairs={{0,2},{1,3},{2,0},{3,1},{4,6},{5,7},{6,4},{7,5},{8,10},{9,11},{10,... | collective-permute-start | bytes 1572872 | tf_op jit(solution)/shard_map/ppermute | solution.py:349
  28.4 1.0 %copy-done.2 = bf16[4,2,256,128]{3,2,1,0:T(8,128)(2,1)S(1)} copy-done((bf16[4,2,256,128]{3,2,1,0:T(8,128)(2,1)S(1)}, bf16[4,2,256,128]{3,2,1,0:T(8,128)(2,1)}, u32[]{:S(2)}) %copy-start.2) | copy-done | bytes 524312
  29.5 7.6 %attend.3 = (f32[256,2048]{1,0:T(8,128)S(1)}, f32[256,2048]{1,0:T(8,128)S(1)}, f32[256,2048]{1,0:T(8,128)S(1)}) custom-call(s32[256,1]{1,0:T(8,128)S(1)} %broadcast_select_fusion.refs_0_, s32[256,1]{1,0:T(8,128)S(1)} %broadcast_add_fusion.refs_1_, s32[1,1024]{1,0:T(1,128)S(1)} %bitcast.32, s32[1,1024]{1,0:T(1,128)S(1)} %bitcast.31, ...), custom_call_target="tpu_custom_call" | custom-call | flops 3221225472 | bytes 9447424 | tf_op jit(solution)/shard_map/attend/pallas_call | solution.py:37
  37.1 1.1 %collective-permute-done.2.refs_5_ = bf16[4,2,256,128]{3,2,1,0:T(8,128)(2,1)S(1)} collective-permute-done((bf16[4,2,256,128]{3,2,1,0:T(8,128)(2,1)}, bf16[4,2,256,128]{3,2,1,0:T(8,128)(2,1)S(1)}, u32[]{:S(2)}, u32[]{:S(2)}) %collective-permute-start.2) | collective-permute-done | bytes 524320 | tf_op jit(solution)/shard_map/ppermute | solution.py:349
  38.3 0.1 bitcast_select_fusion
  38.4 1.0 %collective-permute-start.5 = (bf16[1024,128]{1,0:T(8,128)(2,1)S(1)}, bf16[1024,128]{1,0:T(8,128)(2,1)S(1)}, u32[]{:S(2)}, u32[]{:S(2)}) collective-permute-start(bf16[1024,128]{1,0:T(8,128)(2,1)S(1)} %bitcast_select_fusion), channel_id=1, source_target_pairs={{0,4},{1,5},{2,6},{3,7},{4,8},{5,1},{6,2},{7,3},{8,12},{9,13},{10,... | collective-permute-start | bytes 786440 | tf_op jit(solution)/shard_map/ppermute | solution.py:372
  39.4 0.6 %collective-permute-done.6.refs_6_ = bf16[4,2,256,128]{3,2,1,0:T(8,128)(2,1)S(1)} collective-permute-done((bf16[4,2,256,128]{3,2,1,0:T(8,128)(2,1)}, bf16[4,2,256,128]{3,2,1,0:T(8,128)(2,1)S(1)}, u32[]{:S(2)}, u32[]{:S(2)}) %collective-permute-start.6) | collective-permute-done | bytes 524320 | tf_op jit(solution)/shard_map/ppermute | solution.py:349
  40.1 1.2 %collective-permute-start.7 = (bf16[1,2,256,128]{3,2,1,0:T(8,128)(2,1)S(1)}, bf16[1,2,256,128]{3,2,1,0:T(8,128)(2,1)S(1)}, u32[]{:S(2)}, u32[]{:S(2)}) collective-permute-start(bf16[1,2,256,128]{3,2,1,0:T(8,128)(2,1)S(1)} %slice.10), channel_id=1, source_target_pairs={{0,1},{1,0},{2,3},{3,2},{4,5},{5,4},{6,7},{7,6},{8,9},{9,8},{10,11... | collective-permute-start | bytes 393224 | tf_op jit(solution)/shard_map/ppermute | solution.py:349
  41.3 0.0 collective-permute-done.8.refs_7_
  41.3 0.0 slice-start.2
  41.3 1.3 %collective-permute-start.9 = (bf16[1,2,256,128]{3,2,1,0:T(8,128)(2,1)S(1)}, bf16[1,2,256,128]{3,2,1,0:T(8,128)(2,1)S(1)}, u32[]{:S(2)}, u32[]{:S(2)}) collective-permute-start(bf16[1,2,256,128]{3,2,1,0:T(8,128)(2,1)S(1)} %slice.11), channel_id=1, source_target_pairs={{0,2},{1,3},{2,0},{3,1},{4,6},{5,7},{6,4},{7,5},{8,10},{9,11},{10,... | collective-permute-start | bytes 393224 | tf_op jit(solution)/shard_map/ppermute | solution.py:349
  42.6 4.8 %attend.4 = (f32[256,2048]{1,0:T(8,128)S(1)}, f32[256,2048]{1,0:T(8,128)S(1)}, f32[256,2048]{1,0:T(8,128)S(1)}) custom-call(s32[256,1]{1,0:T(8,128)S(1)} %broadcast_select_fusion.refs_0_, s32[256,1]{1,0:T(8,128)S(1)} %broadcast_add_fusion.refs_1_, s32[1,768]{1,0:T(1,128)S(1)} %broadcast_in_dim.53.refs_2_, s32[1,768]{1,0:T(1,128)S(1)} %broadcast_in_dim.54.refs_3_, ...), custom_call_target="tpu_custom_call" | custom-call | flops 2415919104 | bytes 15212544 | tf_op jit(solution)/shard_map/attend/pallas_call | solution.py:37
  47.4 0.0 collective-permute-done.7
  47.4 0.0 collective-permute-done.9
  47.5 0.0 collective-permute-done.5
  47.5 0.0 slice-start.3
  47.5 0.1 maximum_select_fusion.refs_5_
  47.6 2.1 %attend.5 = (bf16[128,2048]{1,0:T(8,128)(2,1)S(1)}, bf16[128,2048]{1,0:T(8,128)(2,1)S(1)}) custom-call(s32[256,1]{1,0:T(8,128)S(1)} %broadcast_select_fusion.refs_0_, s32[256,1]{1,0:T(8,128)S(1)} %broadcast_add_fusion.refs_1_, s32[1,256]{1,0:T(1,128)S(1)} %bitcast.30, s32[1,256]{1,0:T(1,128)S(1)} %broadcast_select_fusion.1.refs_3_, ...), custom_call_target="tpu_custom_call" | custom-call | flops 805306368 | bytes 8916992 | tf_op jit(solution)/shard_map/attend/pallas_call | solution.py:37
  49.8 0.0 slice-done
  49.8 2.3 %project_out.2 = bf16[128,4096]{1,0:T(8,128)(2,1)S(1)} custom-call(bf16[128,2048]{1,0:T(8,128)(2,1)S(1)} %get-tuple-element.53.x_ref, bf16[2048,4096]{1,0:T(8,128)(2,1)S(1)} %bitcast.28), custom_call_target="tpu_custom_call" | custom-call | flops 2147483648 | bytes 18350080 | tf_op jit(solution)/shard_map/project_out/pallas_call | solution.py:37
  52.2 0.1 collective-permute-start.10
  52.2 0.0 copy-start
  52.3 2.3 %project_out.3.refs_0_ = f32[128,4096]{1,0:T(8,128)S(1)} custom-call(bf16[128,2048]{1,0:T(8,128)(2,1)S(1)} %get-tuple-element.54.x_ref, bf16[2048,4096]{1,0:T(8,128)(2,1)S(1)} %bitcast.28), custom_call_target="tpu_custom_call" | custom-call | flops 2147483648 | bytes 19398656 | tf_op jit(solution)/shard_map/project_out/pallas_call | solution.py:37
  54.6 0.3 collective-permute-done.10.refs_1_
  54.9 1.4 %finish.1 = (bf16[128,4096]{1,0:T(8,128)(2,1)}, bf16[128,4096]{1,0:T(8,128)(2,1)}) custom-call(bf16[128,4096]{1,0:T(8,128)(2,1)S(1)} %copy-done, f32[128,4096]{1,0:T(8,128)S(1)} %project_out.3.refs_0_, bf16[128,4096]{1,0:T(8,128)(2,1)S(1)} %collective-permute-done.10.refs_1_), custom_call_target="tpu_custom_call" | custom-call | flops 1048576 | bytes 6291456 | tf_op jit(solution)/shard_map/finish/pallas_call | solution.py:37
  (36 shorter events, 0.2 us)
Async XLA Ops:
  0.6 5.1 %collective-permute-start = (bf16[128,4096]{1,0:T(8,128)(2,1)}, bf16[128,4096]{1,0:T(8,128)(2,1)S(1)}, u32[]{:S(2)}, u32[]{:S(2)}) collective-permute-start(bf16[128,4096]{1,0:T(8,128)(2,1)} %tokens_ref.1), channel_id=1, source_target_pairs={{0,16},{16,0},{1,17},{17,1},{2,18},{18,2},{3,19},{19,3},{4,20},{20... | collective-permute-start | bytes 3145736 | tf_op jit(solution)/shard_map/ppermute | solution.py:335
  5.7 8.0 %copy-start.3 = (s32[4096]{0:T(1024)S(1)}, s32[4096]{0:T(1024)}, u32[]{:S(2)}) copy-start(s32[4096]{0:T(1024)} %param.14) | copy-start | bytes 49156
  7.3 0.8 %copy-start.1 = (bf16[4,2,256,128]{3,2,1,0:T(8,128)(2,1)}, bf16[4,2,256,128]{3,2,1,0:T(8,128)(2,1)S(1)}, u32[]{:S(2)}) copy-start(bf16[4,2,256,128]{3,2,1,0:T(8,128)(2,1)S(1)} %get-tuple-element.34.refs_5_) | copy-start | bytes 1572868
  8.1 16.5 %collective-permute-start.1 = (bf16[4,2,256,128]{3,2,1,0:T(8,128)(2,1)}, bf16[4,2,256,128]{3,2,1,0:T(8,128)(2,1)}, u32[]{:S(2)}, u32[]{:S(2)}) collective-permute-start(bf16[4,2,256,128]{3,2,1,0:T(8,128)(2,1)} %copy-done.1), channel_id=1, source_target_pairs={{0,2},{1,3},{2,0},{3,1},{4,6},{5,7},{6,4},{7,5},{8,10},{9,11},{10,... | collective-permute-start | bytes 1572872 | tf_op jit(solution)/shard_map/ppermute | solution.py:349
  10.6 14.6 %collective-permute-start.3 = (bf16[4,2,256,128]{3,2,1,0:T(8,128)(2,1)}, bf16[4,2,256,128]{3,2,1,0:T(8,128)(2,1)}, u32[]{:S(2)}, u32[]{:S(2)}) collective-permute-start(bf16[4,2,256,128]{3,2,1,0:T(8,128)(2,1)} %copy-done.1), channel_id=1, source_target_pairs={{0,1},{1,0},{2,3},{3,2},{4,5},{5,4},{6,7},{7,6},{8,9},{9,8},{10,11... | collective-permute-start | bytes 1572872 | tf_op jit(solution)/shard_map/ppermute | solution.py:349
  12.1 14.8 %collective-permute-start.4 = (bf16[4,2,256,128]{3,2,1,0:T(8,128)(2,1)}, bf16[4,2,256,128]{3,2,1,0:T(8,128)(2,1)}, u32[]{:S(2)}, u32[]{:S(2)}) collective-permute-start(bf16[4,2,256,128]{3,2,1,0:T(8,128)(2,1)} %copy-done.1), channel_id=1, source_target_pairs={{0,4},{1,5},{2,6},{3,7},{4,0},{5,1},{6,2},{7,3},{8,12},{9,13},{10,... | collective-permute-start | bytes 1572872 | tf_op jit(solution)/shard_map/ppermute | solution.py:349
  14.1 8.3 %copy-start.4 = (s32[2]{0:T(128)S(1)}, s32[2]{0:T(128)}, u32[]{:S(2)}) copy-start(s32[2]{0:T(128)} %param.15) | copy-start | bytes 28
  24.6 13.7 %collective-permute-start.2 = (bf16[4,2,256,128]{3,2,1,0:T(8,128)(2,1)}, bf16[4,2,256,128]{3,2,1,0:T(8,128)(2,1)S(1)}, u32[]{:S(2)}, u32[]{:S(2)}) collective-permute-start(bf16[4,2,256,128]{3,2,1,0:T(8,128)(2,1)} %collective-permute-done.1.refs_7_), channel_id=1, source_target_pairs={{0,1},{1,0},{2,3},{3,2},{4,5},{5,4},{6,7},{7,6},{8,9},{9,8},{10,11... | collective-permute-start | bytes 1572872 | tf_op jit(solution)/shard_map/ppermute | solution.py:349
  25.3 16.0 %collective-permute-start.8 = (bf16[4,2,256,128]{3,2,1,0:T(8,128)(2,1)}, bf16[4,2,256,128]{3,2,1,0:T(8,128)(2,1)S(1)}, u32[]{:S(2)}, u32[]{:S(2)}) collective-permute-start(bf16[4,2,256,128]{3,2,1,0:T(8,128)(2,1)} %collective-permute-done.3.refs_6_), channel_id=1, source_target_pairs={{0,4},{1,5},{2,6},{3,7},{4,0},{5,1},{6,2},{7,3},{8,12},{9,13},{10,... | collective-permute-start | bytes 1572872 | tf_op jit(solution)/shard_map/ppermute | solution.py:349
  26.9 13.2 %collective-permute-start.6 = (bf16[4,2,256,128]{3,2,1,0:T(8,128)(2,1)}, bf16[4,2,256,128]{3,2,1,0:T(8,128)(2,1)S(1)}, u32[]{:S(2)}, u32[]{:S(2)}) collective-permute-start(bf16[4,2,256,128]{3,2,1,0:T(8,128)(2,1)} %collective-permute-done.4.refs_8_), channel_id=1, source_target_pairs={{0,2},{1,3},{2,0},{3,1},{4,6},{5,7},{6,4},{7,5},{8,10},{9,11},{10,... | collective-permute-start | bytes 1572872 | tf_op jit(solution)/shard_map/ppermute | solution.py:349
  28.4 1.0 %copy-start.2 = (bf16[4,2,256,128]{3,2,1,0:T(8,128)(2,1)S(1)}, bf16[4,2,256,128]{3,2,1,0:T(8,128)(2,1)}, u32[]{:S(2)}) copy-start(bf16[4,2,256,128]{3,2,1,0:T(8,128)(2,1)} %copy-done.1) | copy-start | bytes 1572868
  29.5 20.3 %slice-start = ((s8[16777216]{0:T(1024)(128)(4,1)}), s8[4194304]{0:T(1024)(128)(4,1)S(1)}, s32[]{:S(2)}) async-start(s8[16777216]{0:T(1024)(128)(4,1)} %bitcast.27), calls=%async_computation | async-start | bytes 8388608
  29.5 20.3 %slice-start.1 = ((s8[16777216]{0:T(1024)(128)(4,1)}), s8[4194304]{0:T(1024)(128)(4,1)S(1)}, s32[]{:S(2)}) async-start(s8[16777216]{0:T(1024)(128)(4,1)} %bitcast.27), calls=%async_computation.1 | async-start | bytes 8388608
  38.4 9.1 %collective-permute-start.5 = (bf16[1024,128]{1,0:T(8,128)(2,1)S(1)}, bf16[1024,128]{1,0:T(8,128)(2,1)S(1)}, u32[]{:S(2)}, u32[]{:S(2)}) collective-permute-start(bf16[1024,128]{1,0:T(8,128)(2,1)S(1)} %bitcast_select_fusion), channel_id=1, source_target_pairs={{0,4},{1,5},{2,6},{3,7},{4,8},{5,1},{6,2},{7,3},{8,12},{9,13},{10,... | collective-permute-start | bytes 786440 | tf_op jit(solution)/shard_map/ppermute | solution.py:372
  40.1 7.3 %collective-permute-start.7 = (bf16[1,2,256,128]{3,2,1,0:T(8,128)(2,1)S(1)}, bf16[1,2,256,128]{3,2,1,0:T(8,128)(2,1)S(1)}, u32[]{:S(2)}, u32[]{:S(2)}) collective-permute-start(bf16[1,2,256,128]{3,2,1,0:T(8,128)(2,1)S(1)} %slice.10), channel_id=1, source_target_pairs={{0,1},{1,0},{2,3},{3,2},{4,5},{5,4},{6,7},{7,6},{8,9},{9,8},{10,11... | collective-permute-start | bytes 393224 | tf_op jit(solution)/shard_map/ppermute | solution.py:349
  41.3 8.5 %slice-start.2 = ((s8[16777216]{0:T(1024)(128)(4,1)}), s8[4194304]{0:T(1024)(128)(4,1)S(1)}, s32[]{:S(2)}) async-start(s8[16777216]{0:T(1024)(128)(4,1)} %bitcast.27), calls=%async_computation.2 | async-start | bytes 8388608
  41.3 6.1 %collective-permute-start.9 = (bf16[1,2,256,128]{3,2,1,0:T(8,128)(2,1)S(1)}, bf16[1,2,256,128]{3,2,1,0:T(8,128)(2,1)S(1)}, u32[]{:S(2)}, u32[]{:S(2)}) collective-permute-start(bf16[1,2,256,128]{3,2,1,0:T(8,128)(2,1)S(1)} %slice.11), channel_id=1, source_target_pairs={{0,2},{1,3},{2,0},{3,1},{4,6},{5,7},{6,4},{7,5},{8,10},{9,11},{10,... | collective-permute-start | bytes 393224 | tf_op jit(solution)/shard_map/ppermute | solution.py:349
  47.5 2.3 %slice-start.3 = ((s8[16777216]{0:T(1024)(128)(4,1)}), s8[4194304]{0:T(1024)(128)(4,1)S(1)}, s32[]{:S(2)}) async-start(s8[16777216]{0:T(1024)(128)(4,1)} %bitcast.27), calls=%async_computation.3 | async-start | bytes 8388608
  52.2 2.7 %collective-permute-start.10 = (bf16[128,4096]{1,0:T(8,128)(2,1)S(1)}, bf16[128,4096]{1,0:T(8,128)(2,1)S(1)}, u32[]{:S(2)}, u32[]{:S(2)}) collective-permute-start(bf16[128,4096]{1,0:T(8,128)(2,1)S(1)} %project_out.2), channel_id=1, source_target_pairs={{0,16},{16,0},{1,17},{17,1},{2,18},{18,2},{3,19},{19,3},{4,20},{20... | collective-permute-start | bytes 3145736 | tf_op jit(solution)/shard_map/ppermute | solution.py:335
  52.2 2.6 %copy-start = (bf16[128,4096]{1,0:T(8,128)(2,1)S(1)}, bf16[128,4096]{1,0:T(8,128)(2,1)}, u32[]{:S(2)}) copy-start(bf16[128,4096]{1,0:T(8,128)(2,1)} %tokens_ref.1) | copy-start | bytes 3145732
